TPU v7x, 128 devices: a whole 4x4x4 slice. The times are simulated.
128 devices in a mesh: gx: 16 (over y_lo, x, core), gz: 8 (over z, y_hi).
Axes of the slice: x: 4, y: 4 (y_hi: 2, y_lo: 2; y = y_hi * 2 + y_lo), z: 4, core: 2. Of those that a mesh axis runs over, the one named last changes fastest.
Arguments:
- face_residual: float32 [2, 6, 121, 16, 2048], P(None, None, None, 'gx', 'gz'), may hold values from -6 to 6
- edge_residual: float32 [2, 12, 11, 16, 2048], P(None, None, None, 'gx', 'gz'), may hold values from -6 to 6
- vertex_residual: float32 [2, 8, 16, 2048], P(None, None, 'gx', 'gz'), may hold values from -6 to 6
- face_orient: int32 [6, 16, 2048], P(None, 'gx', 'gz'), may hold values from 0 to 7
- edge_orient: int32 [12, 16, 2048], P(None, 'gx', 'gz'), may hold values from 0 to 1
- stiffness: float32 [16, 2048], P('gx', 'gz'), may hold values from 0.3 to 3
- face_basis: float32 [11, 11], replicated, may hold values from -0.3 to 1.3
- face_eigs: float32 [11], replicated, may hold values from 0.3 to 60
- extension: float32 [121, 48], replicated, may hold values from -0.875 to 0.875
- edge_diag: float32 [11], replicated, may hold values from 1 to 4
- element_heights: float32 [32], replicated, may hold values from 0.2 to 2
Outputs:
- face_solution: float32 [2, 6, 121, 16, 2048], P(None, None, None, 'gx', 'gz')
- edge_solution: float32 [2, 12, 11, 16, 2048], P(None, None, None, 'gx', 'gz')
- vertex_solution: float32 [2, 8, 16, 2048], P(None, None, 'gx', 'gz')
All inputs are finite; a program needn't handle non-finite values.
Results may differ from a plain program's by a relative error of at most 0.0003.
Values sent between devices are 32-bit elements; how exact they have to be, the bound alone decides.
No kernel may reach another device: no remote copies, remote signals or barrier semaphores. Data moves between devices by JAX's collectives and lax.ppermute only.
A program may use at most 192 MiB of HBM per device.

v0:
```python
import math

import jax
import jax.numpy as jnp
from jax import lax
from jax.sharding import PartitionSpec as P

FACE_SLOTS = ((-1, 0, 0), (1, 0, 0), (0, -1, 0), (0, 1, 0), (0, 0, -1), (0, 0, 1))
EDGE_SLOTS = (
    (0, -1, -1),
    (0, -1, 1),
    (0, 1, -1),
    (0, 1, 1),
    (-1, 0, -1),
    (-1, 0, 1),
    (1, 0, -1),
    (1, 0, 1),
    (-1, -1, 0),
    (-1, 1, 0),
    (1, -1, 0),
    (1, 1, 0),
)
VERTEX_SLOTS = (
    (-1, -1, -1),
    (-1, -1, 1),
    (-1, 1, -1),
    (-1, 1, 1),
    (1, -1, -1),
    (1, -1, 1),
    (1, 1, -1),
    (1, 1, 1),
)
shift_mass = 0.004
HIGHEST = lax.Precision.HIGHEST


def extended_2(cells, sides, width):
    for axis, dim in sides:
        count = lax.axis_size(axis)
        head = lax.slice_in_dim(cells, 0, width, axis=dim)
        tail = lax.slice_in_dim(cells, cells.shape[dim] - width, cells.shape[dim], axis=dim)
        cells = jnp.concatenate(
            [
                lax.ppermute(tail, axis, [(i, (i + 1) % count) for i in range(count)]),
                cells,
                lax.ppermute(head, axis, [((i + 1) % count, i) for i in range(count)]),
            ],
            axis=dim,
        )
    return cells


def moves_of(slot):
    result = [()]
    for part in slot:
        options = (0,) if part == 0 else (0, part)
        result = [prior + (option,) for prior in result for option in options]
    return result


def partner_of(slot, move):
    return tuple((part - 2 * step for part, step in zip(slot, move)))


def shift_levels(array, step):
    if step == 0:
        return array
    zeros = jnp.zeros(array.shape[:-1] + (1,), array.dtype)
    if step > 0:
        return jnp.concatenate([array[..., 1:], zeros], axis=-1)
    return jnp.concatenate([zeros, array[..., :-1]], axis=-1)


def sum_slots(slots, fetch):
    totals = []
    for slot in slots:
        total = None
        for move in moves_of(slot):
            term = fetch(slots.index(partner_of(slot, move)), move)
            total = term if total is None else total + term
        totals.append(total)
    return totals


def faces_to_frame(values, turn):
    turn = turn[None, :, None, None]
    values = jnp.where(turn // 4 % 2 == 1, jnp.swapaxes(values, 2, 3), values)
    values = jnp.where(turn % 2 == 1, jnp.flip(values, 2), values)
    return jnp.where(turn // 2 % 2 == 1, jnp.flip(values, 3), values)


def faces_from_frame(values, turn):
    turn = turn[None, :, None, None]
    values = jnp.where(turn % 2 == 1, jnp.flip(values, 2), values)
    values = jnp.where(turn // 2 % 2 == 1, jnp.flip(values, 3), values)
    return jnp.where(turn // 4 % 2 == 1, jnp.swapaxes(values, 2, 3), values)


def flip_edges(values, turn):
    return jnp.where(turn[None, :, None] % 2 == 1, jnp.flip(values, 2), values)


def face_frame(slot):
    tangents = [axis for axis in range(3) if slot[axis] == 0]
    edge_list = []
    for axis in tangents:
        for sign in (-1, 1):
            corner = list(slot)
            corner[axis] = sign
            edge_list.append(EDGE_SLOTS.index(tuple(corner)))
    vertex_list = []
    for first in (-1, 1):
        for second in (-1, 1):
            corner = list(slot)
            corner[tangents[0]] = first
            corner[tangents[1]] = second
            vertex_list.append(VERTEX_SLOTS.index(tuple(corner)))
    return (edge_list, vertex_list)


def edge_ends(slot):
    axis = slot.index(0)
    start = list(slot)
    start[axis] = -1
    finish_point = list(slot)
    finish_point[axis] = 1
    return (VERTEX_SLOTS.index(tuple(start)), VERTEX_SLOTS.index(tuple(finish_point)))


def hartley(rows, columns, size):
    phase = rows[:, None] * columns[None, :] % size
    angle = 2.0 * math.pi / size * phase.astype(jnp.float32)
    return (jnp.cos(angle) + jnp.sin(angle)) / math.sqrt(size)


def circle_modes(indices, size):
    return 2.0 - 2.0 * jnp.cos(2.0 * math.pi / size * indices.astype(jnp.float32))


def level_solve(rhs, modes, element_heights):
    inverse = 1.0 / element_heights
    zero = jnp.zeros((1,), jnp.float32)
    stiff = jnp.concatenate([inverse, zero]) + jnp.concatenate([zero, inverse])
    mass = 0.5 * (
        jnp.concatenate([element_heights, zero]) + jnp.concatenate([zero, element_heights])
    )
    count = rhs.shape[0]
    primes = []
    values = []
    for level in range(count):
        diagonal = stiff[level] + modes * mass[level]
        if level == 0:
            pivot = diagonal
            value = rhs[0] / pivot
        else:
            pivot = diagonal + inverse[level - 1] * primes[-1]
            value = (rhs[level] + inverse[level - 1] * values[-1]) / pivot
        values.append(value)
        if level < count - 1:
            primes.append(-inverse[level] / pivot)
    solution = [values[-1]]
    for level in range(count - 2, -1, -1):
        solution.append(values[level] - primes[level] * solution[-1])
    return jnp.stack(solution[::-1], axis=0)


def spectral_solve(rhs, element_heights):
    span_x = rhs.shape[1]
    span_z = rhs.shape[2]
    index_x = jnp.arange(span_x, dtype=jnp.int32)
    index_z = jnp.arange(span_z, dtype=jnp.int32)
    spectrum = jnp.einsum(
        "kx,sxzl->skzl", hartley(index_x, index_x, span_x), rhs, precision=HIGHEST
    )
    spectrum = jnp.einsum(
        "mz,skzl->skml", hartley(index_z, index_z, span_z), spectrum, precision=HIGHEST
    )
    modes = (
        circle_modes(index_x, span_x)[:, None] + circle_modes(index_z, span_z)[None, :] + shift_mass
    )
    solved = level_solve(jnp.moveaxis(spectrum, 3, 0), modes, element_heights)
    return jnp.moveaxis(solved, 0, 3)


def finish(
    face_sums,
    face_cover,
    edge_sums,
    edge_cover,
    extended,
    face_turn,
    edge_turn,
    face_basis,
    face_eigs,
    extension,
    edge_diag,
):
    solves = face_sums.shape[0]
    nodes = face_basis.shape[0]
    size_x, size_z, layers = face_sums.shape[-3:]
    vertex_values = []
    for slot in VERTEX_SLOTS:
        low_x, low_z, low_y = [(part + 1) // 2 for part in slot]
        vertex_values.append(
            extended[:, low_x : low_x + size_x, low_z : low_z + size_z, low_y : low_y + layers]
        )
    vertex_values = jnp.stack(vertex_values, axis=1)
    fraction = (jnp.arange(nodes, dtype=jnp.float32) + 1.0) / (nodes + 1.0)
    fraction = fraction[:, None, None, None]
    edge_values = []
    for index, slot in enumerate(EDGE_SLOTS):
        start, stop = edge_ends(slot)
        local = edge_sums[:, index] / (edge_diag[:, None, None, None] * edge_cover[index])
        edge_values.append(
            local
            + (1.0 - fraction) * vertex_values[:, start][:, None]
            + fraction * vertex_values[:, stop][:, None]
        )
    edge_values = jnp.stack(edge_values, axis=1)
    modal = jnp.einsum("ai,sfabxzy->sfibxzy", face_basis, face_sums, precision=HIGHEST)
    modal = jnp.einsum("bj,sfibxzy->sfijxzy", face_basis, modal, precision=HIGHEST)
    spectrum = face_eigs[:, None] + face_eigs[None, :]
    modal = modal / (spectrum[None, None, :, :, None, None, None] * face_cover[None, :, None, None])
    direct = jnp.einsum("ai,sfijxzy->sfajxzy", face_basis, modal, precision=HIGHEST)
    direct = jnp.einsum("bj,sfajxzy->sfabxzy", face_basis, direct, precision=HIGHEST)
    lifted = []
    for slot in FACE_SLOTS:
        edge_list, vertex_list = face_frame(slot)
        boundary = jnp.concatenate(
            [edge_values[:, item] for item in edge_list]
            + [jnp.stack([vertex_values[:, item] for item in vertex_list], axis=1)],
            axis=1,
        )
        lifted.append(jnp.einsum("qk,skxzy->sqxzy", extension, boundary, precision=HIGHEST))
    lifted = jnp.stack(lifted, axis=1).reshape((solves, 6, nodes, nodes, size_x, size_z, layers))
    face_values = direct + lifted
    face_out = faces_from_frame(face_values, face_turn).reshape(
        (solves, 6, nodes * nodes, size_x, size_z * layers)
    )
    edge_out = flip_edges(edge_values, edge_turn).reshape(
        (solves, 12, nodes, size_x, size_z * layers)
    )
    vertex_out = vertex_values.reshape((solves, 8, size_x, size_z * layers))
    return (face_out, edge_out, vertex_out)


def per_device(
    face_residual,
    edge_residual,
    vertex_residual,
    face_orient,
    edge_orient,
    stiffness,
    face_basis,
    face_eigs,
    extension,
    edge_diag,
    element_heights,
):
    solves = face_residual.shape[0]
    nodes = face_basis.shape[0]
    size_x = face_residual.shape[3]
    layers = element_heights.shape[0]
    size_z = face_residual.shape[4] // layers
    grid = (size_x, size_z, layers)
    face_turn = face_orient.reshape((6,) + grid)
    edge_turn = edge_orient.reshape((12,) + grid)
    faces = faces_to_frame(face_residual.reshape((solves, 6, nodes, nodes) + grid), face_turn)
    edges = flip_edges(edge_residual.reshape((solves, 12, nodes) + grid), edge_turn)
    corners = vertex_residual.reshape((solves, 8) + grid)
    weight = stiffness.reshape(grid)
    edge_rows = solves * 12 * nodes
    vertex_rows = solves * 8
    cache = {}
    wire = jnp.concatenate(
        [edges.reshape((edge_rows,) + grid), corners.reshape((vertex_rows,) + grid), weight[None]],
        axis=0,
    )
    rim = extended_2(wire, (("gx", 1), ("gz", 2)), 1)

    def base_piece(key):
        block = rim[:, 1 + key[0] : 1 + key[0] + size_x, 1 + key[1] : 1 + key[1] + size_z]
        edge_block = block[:edge_rows].reshape((solves, 12, nodes) + grid)
        vertex_block = block[edge_rows : edge_rows + vertex_rows].reshape((solves, 8) + grid)
        edge_map = {item: edge_block[:, item] for item in range(12)}
        vertex_map = {item: vertex_block[:, item] for item in range(8)}
        return (edge_map, vertex_map, block[edge_rows + vertex_rows])

    bases = {}
    for step_x in (-1, 0, 1):
        for step_z in (-1, 0, 1):
            bases[step_x, step_z] = base_piece((step_x, step_z))

    def piece(move):
        if move not in cache:
            edge_map, vertex_map, moved_weight = bases[move[0], move[1]]
            cache[move] = (
                {item: shift_levels(value, move[2]) for item, value in edge_map.items()},
                {item: shift_levels(value, move[2]) for item, value in vertex_map.items()},
                shift_levels(moved_weight, move[2]),
            )
        return cache[move]

    def edge_fetch(index, move):
        return piece(move)[0][index]

    def vertex_fetch(index, move):
        return piece(move)[1][index]

    def weight_fetch(index, move):
        return piece(move)[2]

    edge_sums = jnp.stack(sum_slots(EDGE_SLOTS, edge_fetch), axis=1)
    vertex_sums = jnp.stack(sum_slots(VERTEX_SLOTS, vertex_fetch), axis=1)
    edge_cover = jnp.stack(sum_slots(EDGE_SLOTS, weight_fetch), axis=0)
    face_cover = jnp.stack(sum_slots(FACE_SLOTS, weight_fetch), axis=0)
    side_rows = solves * 4 * nodes * nodes
    bordered = extended_2(faces[:, :4].reshape((side_rows,) + grid), (("gx", 1), ("gz", 2)), 1)
    bordered = bordered.reshape((solves, 4, nodes, nodes, size_x + 2, size_z + 2, layers))

    def face_fetch(index, move):
        if index >= 4:
            return shift_levels(faces[:, index], move[2])
        return bordered[
            :, index, :, :, 1 + move[0] : 1 + move[0] + size_x, 1 + move[1] : 1 + move[1] + size_z
        ]

    face_sums = jnp.stack(sum_slots(FACE_SLOTS, face_fetch), axis=1)
    coarse_rhs = jnp.concatenate([vertex_sums[:, 0], vertex_sums[:, 1][..., -1:]], axis=-1)
    first_x = lax.axis_index("gx") * size_x
    first_z = lax.axis_index("gz") * size_z
    span_x = lax.axis_size("gx") * size_x
    span_z = lax.axis_size("gz") * size_z
    gathered = lax.all_gather(coarse_rhs, "gx", axis=1, tiled=True)
    gathered = lax.all_gather(gathered, "gz", axis=2, tiled=True)
    solved = spectral_solve(gathered, element_heights)
    index_x = jnp.arange(span_x, dtype=jnp.int32)
    index_z = jnp.arange(span_z, dtype=jnp.int32)
    rows_x = (first_x + jnp.arange(size_x + 1, dtype=jnp.int32)) % span_x
    rows_z = (first_z + jnp.arange(size_z + 1, dtype=jnp.int32)) % span_z
    back = jnp.einsum("xk,skml->sxml", hartley(rows_x, index_x, span_x), solved, precision=HIGHEST)
    extended = jnp.einsum(
        "zm,sxml->sxzl", hartley(rows_z, index_z, span_z), back, precision=HIGHEST
    )
    return finish(
        face_sums,
        face_cover,
        edge_sums,
        edge_cover,
        extended,
        face_turn,
        edge_turn,
        face_basis,
        face_eigs,
        extension,
        edge_diag,
    )


def solution(mesh):
    placed = (
        P(None, None, None, "gx", "gz"),
        P(None, None, None, "gx", "gz"),
        P(None, None, "gx", "gz"),
        P(None, "gx", "gz"),
        P(None, "gx", "gz"),
        P("gx", "gz"),
        P(),
        P(),
        P(),
        P(),
        P(),
    )
    return jax.shard_map(
        per_device,
        mesh=mesh,
        in_specs=placed,
        out_specs=(
            P(None, None, None, "gx", "gz"),
            P(None, None, None, "gx", "gz"),
            P(None, None, "gx", "gz"),
        ),
        check_vma=False,
    )
```

profile of v0, /device:TPU:0, one launch (start us, length us, event | category | flops | bytes accessed | tf_op | source)
XLA Modules:
  0.0 684.2 jit_solution(3743584585472277661)
XLA Ops:
  10.3 11.2 %bitcast_select_fusion = f32[2,6,11,11,1,8,32]{6,2,5,3,0,4,1:T(8,128)} fusion(f32[2,6,11,11,1,8,32]{6,5,3,2,1,0,4:T(8,128)} %reshape.2798, pred[6,8,32]{2,1,0:T(8,128)(4,1)S(1)} %get-tuple-element.229), kind=kLoop, calls=%fused_computation.7 | loop fusion | flops 371712 | bytes 2975232 | tf_op jit(solution)/shard_map/jit(_where)/select_n | solution.py:87
  21.4 16.6 %rev.21 = f32[2,6,11,11,1,8,32]{6,2,5,3,0,4,1:T(8,128)} reverse(f32[2,6,11,11,1,8,32]{6,2,5,3,0,4,1:T(8,128)} %bitcast_select_fusion), dimensions={2} | reverse | bytes 2973696 | tf_op jit(solution)/shard_map/jit(_flip)/rev | solution.py:88
  38.1 10.5 %broadcast_select_fusion.1 = f32[2,6,11,11,1,8,32]{6,2,5,3,0,4,1:T(8,128)S(1)} fusion(f32[2,6,11,11,1,8,32]{6,2,5,3,0,4,1:T(8,128)} %rev.21, pred[6,8,32]{2,1,0:T(8,128)(4,1)S(1)} %get-tuple-element.230, f32[2,6,11,11,1,8,32]{6,5,3,2,1,0,4:T(8,128)} %reshape.2798, pred[6,8,32]{2,1,0:T(8,128)(4,1)S(1)} %get-tuple-element.229), kind=kLoop, calls=%fused_computation.17 | loop fusion | flops 743424 | bytes 4463616 | tf_op jit(solution)/shard_map/jit(_where)/select_n | solution.py:88
  118.0 7.5 %multiply_add_fusion.49 = (f32[16,64]{1,0:T(8,128)}, f32[16,64]{1,0:T(8,128)}, f32[16,64]{1,0:T(8,128)}, f32[16,64]{1,0:T(8,128)}, f32[16,64]{1,0:T(8,128)}, /*i...) fusion(f32[]{:T(128)} %bitcast.52, f32[]{:T(128)} %bitcast.54, f32[]{:T(128)} %bitcast.53, ...), kind=kLoop, calls=%fused_computation.417 | loop fusion | flops 20480 | bytes 33148 | tf_op jit(solution)/shard_map/add | solution.py:156
  125.4 62.8 %multiply_add_fusion.18 = (f32[16,64]{1,0:T(8,128)S(1)}, f32[16,64]{1,0:T(8,128)}, f32[16,64]{1,0:T(8,128)}, f32[16,64]{1,0:T(8,128)}, f32[16,64]{1,0:T(8,128)},...) fusion(f32[]{:T(128)} %bitcast.145, ...), kind=kLoop, calls=%fused_computation.386 | loop fusion | flops 167936 | bytes 234312 | tf_op jit(solution)/shard_map/add | solution.py:156
  194.2 6.8 collective-permute-start.7
  247.2 17.7 %all_gather.6 = f32[2,16,8,33]{3,2,0,1:T(8,128)} all-gather(f32[2,1,8,33]{3,2,0,1:T(8,128)S(1)} %pad_maximum_fusion.19), channel_id=1, replica_groups=mesh['gx'=16,'gz'=8] {'gx'}, dimensions={1}, use_global_device_ids=true | all-gather | bytes 35904 | tf_op jit(solution)/shard_map/all_gather | solution.py:334
  266.7 50.7 %all_gather.7 = f32[2,16,64,33]{1,2,3,0:T(8,128)S(1)} all-gather(f32[2,16,8,33]{1,2,3,0:T(8,128)} %copy.614), channel_id=1, replica_groups=mesh['gx'=16,'gz'=8] {'gz'}, dimensions={2}, use_global_device_ids=true | all-gather | bytes 304128 | tf_op jit(solution)/shard_map/all_gather | solution.py:335
  324.3 21.0 %constant_dynamic-update-slice_fusion.38 = (f32[33,2,16,64]{3,2,1,0:T(8,128)S(1)}, f32[1,2,16,64]{3,2,1,0:T(8,128)S(1)}, f32[1,2,16,64]{3,2,1,0:T(8,128)S(1)}, f...) fusion(f32[16,64]{1,0:T(8,128)} %get-tuple-element.259, ...), kind=kLoop, calls=%fused_computation.168 | loop fusion | flops 329727 | bytes 1060992
  488.6 5.9 collective-permute-done.2
  500.8 9.2 %copy.573 = f32[968,3,10,32]{3,0,2,1:T(8,128)} copy(f32[968,3,10,32]{0,3,2,1:T(8,128)} %pad_maximum_fusion) | data formatting | bytes 7434240 | tf_op jit(solution)/shard_map/concatenate | solution.py:42
  510.1 18.6 %reshape.2800 = f32[2,4,11,11,3,10,32]{6,3,2,1,0,5,4:T(8,128)} reshape(f32[968,3,10,32]{3,0,2,1:T(8,128)} %copy.573) | data formatting | bytes 7434240 | tf_op jit(solution)/shard_map/reshape | solution.py:319
  528.7 6.8 fusion.218
  544.1 9.0 %fusion.13 = f32[2,6,11,11,8,32]{5,2,4,3,1,0:T(8,128)S(1)} fusion(f32[2,6,11,11,1,8,32]{6,2,5,3,1,0,4:T(8,128)S(1)} %bitcast_dynamic-update-slice_fusion.1, f32[11,11]{1,0:T(8,128)S(1)} %copy-done.82), kind=kOutput, calls=%fused_computation.20 | convolution fusion | flops 49065984 | bytes 2974180 | tf_op jit(solution)/shard_map/ai,sfabxzy->sfibxzy/dot_general | solution.py:220
  553.1 13.6 %fusion = f32[2,6,11,11,8,32]{5,3,4,2,1,0:T(8,128)S(1)} fusion(f32[6,11,11,8,32]{4,2,3,1,0:T(8,128)S(1)} %bitcast.527, f32[2,6,11,11,8,32]{5,2,4,3,1,0:T(8,128)S(1)} %fusion.13, f32[11,11]{1,0:T(8,128)S(1)} %copy-done.82), kind=kOutput, calls=%fused_computation.4 | convolution fusion | flops 49437696 | bytes 3717604 | tf_op jit(solution)/shard_map/bj,sfibxzy->sfijxzy/dot_general | solution.py:221
  566.8 13.0 %fusion.10 = f32[2,6,11,11,8,32]{5,2,4,3,1,0:T(8,128)S(1)} fusion(f32[2,6,11,11,8,32]{5,3,4,2,1,0:T(8,128)S(1)} %fusion, f32[11,11]{1,0:T(8,128)S(1)} %copy-done.82), kind=kOutput, calls=%fused_computation.19 | convolution fusion | flops 49065984 | bytes 2974180 | tf_op jit(solution)/shard_map/ai,sfijxzy->sfajxzy/dot_general | solution.py:224
  579.7 14.6 %fusion.3 = f32[2,6,11,8,32,11]{4,5,3,2,1,0:T(8,128)} fusion(f32[2,6,11,11,8,32]{5,2,4,3,1,0:T(8,128)S(1)} %fusion.10, f32[11,11]{1,0:T(8,128)S(1)} %copy-done.82), kind=kOutput, calls=%fused_computation.9 | convolution fusion | flops 49065984 | bytes 2974180 | tf_op jit(solution)/shard_map/bj,sfajxzy->sfabxzy/dot_general | solution.py:225
  594.3 14.5 %bitcast_add_fusion = f32[2,6,11,11,1,8,32]{6,2,5,3,0,4,1:T(8,128)} fusion(f32[2,6,11,11,1,8,32]{6,2,5,3,0,4,1:T(8,128)} %copy_dynamic-update-slice_fusion, f32[2,6,11,8,32,11]{4,5,3,2,1,0:T(8,128)} %fusion.3), kind=kLoop, calls=%fused_computation.2 | loop fusion | flops 371712 | bytes 4460544 | tf_op jit(solution)/shard_map/add | solution.py:236
  608.8 16.7 %rev.24 = f32[2,6,11,11,1,8,32]{6,2,5,3,0,4,1:T(8,128)} reverse(f32[2,6,11,11,1,8,32]{6,2,5,3,0,4,1:T(8,128)} %bitcast_add_fusion), dimensions={2} | reverse | bytes 2973696 | tf_op jit(solution)/shard_map/jit(_flip)/rev | solution.py:94
  625.5 12.7 %broadcast_select_fusion = f32[2,6,11,11,1,8,32]{6,2,5,3,0,4,1:T(8,128)} fusion(f32[2,6,11,11,1,8,32]{6,2,5,3,0,4,1:T(8,128)} %rev.24, f32[2,6,11,11,1,8,32]{6,2,5,3,0,4,1:T(8,128)} %bitcast_add_fusion, pred[6,8,32]{2,1,0:T(8,128)(4,1)S(1)} %copy-done.99), kind=kLoop, calls=%fused_computation.16 | loop fusion | flops 371712 | bytes 4462080 | tf_op jit(solution)/shard_map/jit(_where)/select_n | solution.py:94
  638.3 12.7 %fusion.9 = f32[2,6,11,11,1,8,32]{6,3,5,2,0,4,1:T(8,128)} fusion(f32[2,6,11,11,1,8,32]{6,2,5,3,0,4,1:T(8,128)} %broadcast_select_fusion, pred[6,8,32]{2,1,0:T(8,128)(4,1)S(1)} %copy-done.75), kind=kLoop, calls=%fused_computation.15 | loop fusion | flops 371712 | bytes 2975232 | tf_op jit(solution)/shard_map/transpose | solution.py:96
  651.0 19.3 %copy_select_fusion = f32[2,6,11,11,1,8,32]{6,2,5,3,0,4,1:T(8,128)} fusion(f32[2,6,11,11,1,8,32]{6,3,5,2,0,4,1:T(8,128)} %fusion.9, f32[2,6,11,11,1,8,32]{6,2,5,3,0,4,1:T(8,128)} %broadcast_select_fusion, pred[6,8,32]{2,1,0:T(8,128)(4,1)S(1)} %copy-done.75, pred[6,8,32]{2,1,0:T(8,128)(4,1)S(1)} %copy-done.77), kind=kLoop, calls=%fused_computation.8 | loop fusion | flops 743424 | bytes 4463616 | tf_op jit(solution)/shard_map/jit(_where)/select_n | solution.py:96
  670.4 7.8 %copy.681 = f32[2,6,11,11,1,8,32]{6,5,3,2,1,0,4:T(8,128)} copy(f32[2,6,11,11,1,8,32]{6,2,5,3,0,4,1:T(8,128)} %copy_select_fusion) | data formatting | bytes 2973696 | tf_op jit(solution)/shard_map/jit(_where)/select_n | solution.py:96
  678.2 5.8 reshape.2834
  (531 shorter events, 276.6 us)
Async XLA Ops:
  0.6 443.8 %copy-start = (f32[121,48]{0,1:T(8,128)S(1)}, f32[121,48]{0,1:T(8,128)}, u32[]{:S(2)}) copy-start(f32[121,48]{0,1:T(8,128)} %param.19) | copy-start | bytes 69700
  1.5 36.6 %copy-start.76 = (pred[6,8,32]{2,1,0:T(8,128)(4,1)}, pred[6,8,32]{2,1,0:T(8,128)(4,1)S(1)}, u32[]{:S(2)}) copy-start(pred[6,8,32]{2,1,0:T(8,128)(4,1)S(1)} %get-tuple-element.229) | copy-start | bytes 4612
  1.5 36.6 %copy-start.98 = (pred[6,8,32]{2,1,0:T(8,128)(4,1)}, pred[6,8,32]{2,1,0:T(8,128)(4,1)S(1)}, u32[]{:S(2)}) copy-start(pred[6,8,32]{2,1,0:T(8,128)(4,1)S(1)} %get-tuple-element.230) | copy-start | bytes 4612
  1.5 47.1 %copy-start.74 = (pred[6,8,32]{2,1,0:T(8,128)(4,1)}, pred[6,8,32]{2,1,0:T(8,128)(4,1)S(1)}, u32[]{:S(2)}) copy-start(pred[6,8,32]{2,1,0:T(8,128)(4,1)S(1)} %get-tuple-element.228) | copy-start | bytes 4612
  60.8 415.4 %collective-permute-start = (f32[968,1,8,32]{0,3,2,1:T(8,128)}, f32[968,1,8,32]{0,3,2,1:T(8,128)}, u32[]{:S(2)}, u32[]{:S(2)}) collective-permute-start(f32[968,1,8,32]{0,3,2,1:T(8,128)} %copy.570), channel_id=1, source_target_pairs={{0,8},{8,16},{16,24},{24,32},{32,40},{40,48},{48,56},{56,64},{64,7... | collective-permute-start | bytes 2973704 | tf_op jit(solution)/shard_map/ppermute | solution.py:44
  60.8 415.4 %collective-permute-start.1 = (f32[968,1,8,32]{0,3,2,1:T(8,128)}, f32[968,1,8,32]{0,3,2,1:T(8,128)}, u32[]{:S(2)}, u32[]{:S(2)}) collective-permute-start(f32[968,1,8,32]{0,3,2,1:T(8,128)} %copy.570), channel_id=1, source_target_pairs={{8,0},{16,8},{24,16},{32,24},{40,32},{48,40},{56,48},{64,56},{72,6... | collective-permute-start | bytes 2973704 | tf_op jit(solution)/shard_map/ppermute | solution.py:46
  82.9 13.4 %copy-start.132 = (f32[11]{0:T(128)S(1)}, f32[11]{0:T(128)}, u32[]{:S(2)}) copy-start(f32[11]{0:T(128)} %param.18) | copy-start | bytes 136
  82.9 109.7 %collective-permute-start.4 = (f32[281,1,8,32]{0,3,2,1:T(8,128)}, f32[281,1,8,32]{0,3,2,1:T(8,128)}, u32[]{:S(2)}, u32[]{:S(2)}) collective-permute-start(f32[281,1,8,32]{0,3,2,1:T(8,128)} %pad_maximum_fusion.5), channel_id=1, source_target_pairs={{0,8},{8,16},{16,24},{24,32},{32,40},{40,48},{48,56},{56,64},{64,7... | collective-permute-start | bytes 863240 | tf_op jit(solution)/shard_map/ppermute | solution.py:44
  82.9 109.7 %collective-permute-start.5 = (f32[281,1,8,32]{0,3,2,1:T(8,128)}, f32[281,1,8,32]{0,3,2,1:T(8,128)}, u32[]{:S(2)}, u32[]{:S(2)}) collective-permute-start(f32[281,1,8,32]{0,3,2,1:T(8,128)} %pad_maximum_fusion.5), channel_id=1, source_target_pairs={{8,0},{16,8},{24,16},{32,24},{40,32},{48,40},{56,48},{64,56},{72,6... | collective-permute-start | bytes 863240 | tf_op jit(solution)/shard_map/ppermute | solution.py:46
  94.9 30.5 %copy-start.133 = (f32[16]{0:T(128)}, f32[16]{0:T(128)S(1)}, u32[]{:S(2)}) copy-start(f32[16]{0:T(128)S(1)} %multiply_subtract_fusion.32) | copy-start | bytes 196
  97.0 106.3 %copy-start.69 = (f32[2,8,1,8,32]{4,3,0,2,1:T(8,128)}, f32[2,8,1,8,32]{4,3,0,2,1:T(8,128)S(1)}, u32[]{:S(2)}) copy-start(f32[2,8,1,8,32]{4,3,0,2,1:T(8,128)S(1)} %reshape_reshape_reshape.3) | copy-start | bytes 49156
  118.0 74.6 %copy-start.4 = (f32[264,1,8,32]{0,3,2,1:T(8,128)S(1)}, f32[264,1,8,32]{0,3,2,1:T(8,128)}, u32[]{:S(2)}) copy-start(f32[264,1,8,32]{0,3,2,1:T(8,128)} %copy.588) | copy-start | bytes 811012
  194.2 31.6 %collective-permute-start.7 = (f32[281,3,1,32]{0,3,2,1:T(8,128)}, f32[281,3,1,32]{0,3,2,1:T(8,128)}, u32[]{:S(2)}, u32[]{:S(2)}) collective-permute-start(f32[281,3,1,32]{0,3,2,1:T(8,128)} %get-tuple-element.167), channel_id=1, source_target_pairs={{1,0},{2,1},{3,2},{4,3},{5,4},{6,5},{7,6},{0,7},{9,8},{10,9},{11,1... | collective-permute-start | bytes 323720 | tf_op jit(solution)/shard_map/ppermute | solution.py:46
  201.0 28.0 %collective-permute-start.6 = (f32[281,3,1,32]{0,3,2,1:T(8,128)}, f32[281,3,1,32]{0,3,2,1:T(8,128)}, u32[]{:S(2)}, u32[]{:S(2)}) collective-permute-start(f32[281,3,1,32]{0,3,2,1:T(8,128)} %get-tuple-element.168), channel_id=1, source_target_pairs={{0,1},{1,2},{2,3},{3,4},{4,5},{5,6},{6,7},{7,0},{8,9},{9,10},{10,1... | collective-permute-start | bytes 323720 | tf_op jit(solution)/shard_map/ppermute | solution.py:44
  229.0 18.2 %copy-start.66 = (f32[1,1,8,32]{3,2,1,0:T(8,128)}, f32[1,1,8,32]{3,2,1,0:T(8,128)S(1)}, u32[]{:S(2)}) copy-start(f32[1,1,8,32]{3,2,1,0:T(8,128)S(1)} %copy.710) | copy-start | bytes 3076
  232.1 85.2 %copy-start.67 = (f32[1,1,8,32]{3,2,1,0:T(8,128)}, f32[1,1,8,32]{3,2,1,0:T(8,128)S(1)}, u32[]{:S(2)}) copy-start(f32[1,1,8,32]{3,2,1,0:T(8,128)S(1)} %copy.711) | copy-start | bytes 3076
  234.2 83.2 %copy-start.68 = (f32[1,1,8,32]{3,2,1,0:T(8,128)}, f32[1,1,8,32]{3,2,1,0:T(8,128)S(1)}, u32[]{:S(2)}) copy-start(f32[1,1,8,32]{3,2,1,0:T(8,128)S(1)} %copy.713) | copy-start | bytes 3076
  322.9 26.3 %copy-start.5 = (f32[264,1,8,32]{0,3,2,1:T(8,128)S(1)}, f32[264,1,8,32]{0,3,2,1:T(8,128)}, u32[]{:S(2)}) copy-start(f32[264,1,8,32]{0,3,2,1:T(8,128)} %copy.588) | copy-start | bytes 811012
  478.5 16.0 %collective-permute-start.2 = (f32[968,3,1,32]{0,3,2,1:T(8,128)}, f32[968,3,1,32]{0,3,2,1:T(8,128)}, u32[]{:S(2)}, u32[]{:S(2)}) collective-permute-start(f32[968,3,1,32]{0,3,2,1:T(8,128)} %get-tuple-element.148), channel_id=1, source_target_pairs={{0,1},{1,2},{2,3},{3,4},{4,5},{5,6},{6,7},{7,0},{8,9},{9,10},{10,1... | collective-permute-start | bytes 1115144 | tf_op jit(solution)/shard_map/ppermute | solution.py:44
  479.3 17.0 %collective-permute-start.3 = (f32[968,3,1,32]{0,3,2,1:T(8,128)}, f32[968,3,1,32]{0,3,2,1:T(8,128)}, u32[]{:S(2)}, u32[]{:S(2)}) collective-permute-start(f32[968,3,1,32]{0,3,2,1:T(8,128)} %get-tuple-element.149), channel_id=1, source_target_pairs={{1,0},{2,1},{3,2},{4,3},{5,4},{6,5},{7,6},{0,7},{9,8},{10,9},{11,1... | collective-permute-start | bytes 1115144 | tf_op jit(solution)/shard_map/ppermute | solution.py:46
  608.8 16.7 %copy-start.99 = (pred[6,8,32]{2,1,0:T(8,128)(4,1)S(1)}, pred[6,8,32]{2,1,0:T(8,128)(4,1)}, u32[]{:S(2)}) copy-start(pred[6,8,32]{2,1,0:T(8,128)(4,1)} %copy-done.98) | copy-start | bytes 4612
  625.5 12.8 %copy-start.75 = (pred[6,8,32]{2,1,0:T(8,128)(4,1)S(1)}, pred[6,8,32]{2,1,0:T(8,128)(4,1)}, u32[]{:S(2)}) copy-start(pred[6,8,32]{2,1,0:T(8,128)(4,1)} %copy-done.74) | copy-start | bytes 4612
  638.3 12.8 %copy-start.77 = (pred[6,8,32]{2,1,0:T(8,128)(4,1)S(1)}, pred[6,8,32]{2,1,0:T(8,128)(4,1)}, u32[]{:S(2)}) copy-start(pred[6,8,32]{2,1,0:T(8,128)(4,1)} %copy-done.76) | copy-start | bytes 4612
  670.4 13.6 %copy-start.1 = (f32[121,48]{0,1:T(8,128)S(1)}, f32[121,48]{0,1:T(8,128)}, u32[]{:S(2)}) copy-start(f32[121,48]{0,1:T(8,128)} %param.19) | copy-start | bytes 69700
  (122 other events, 710.7 us)
where the time goes:
time: 695 us; the launch traced here: 684 us
  local copies, waits for them, and re-layouts  258 us (37%)
  other arithmetic  246 us (35%)
  blocking collectives  68.4 us (10%)
  matrix products  61.5 us (9%)
  between operations  22.7 us (3%)
  starting transfers between devices  20.1 us (3%)
  waiting for transfers between devices  7.7 us (1%)
    unnamed x346, local copies, waits for them, and re-layouts  78.1 us
    add x2, other arithmetic, level_solve(): pivot = diagonal + inverse[level - 1] * primes[-1]  70.2 us
    unnamed x43, other arithmetic  52.9 us
    all_gather x1, blocking collectives, per_device(): gathered = lax.all_gather(gathered, 'gz', axis=2, tiled=True)  50.7 us
    select_n x1, other arithmetic, faces_from_frame(): return jnp.where(turn // 4 % 2 == 1, jnp.swapaxes(values, 2, 3), values)  19.3 us
    ppermute x4, starting transfers between devices, extended_2(): lax.ppermute(head, axis, [((i + 1) % count, i) for i in range(count)])  19.3 us
    reshape x1, local copies, waits for them, and re-layouts, per_device(): bordered.reshape((solves, 4, nodes, nodes, size_x + 2, size_z + 2, layers))  18.6 us
    all_gather x1, blocking collectives, per_device(): gathered = lax.all_gather(coarse_rhs, 'gx', axis=1, tiled=True)  17.7 us
  transfers between devices with their start and end apart: 8, of which 2 were waited for; matrix products, arithmetic and copies ran while one was open for 46% of the time, Pallas kernels for 0%

commit v1 on v0

v1 whole, which is shorter than its diff:
```python
import math

import jax
import jax.numpy as jnp
import numpy as np
from jax import lax
from jax.experimental import pallas as pl
from jax.experimental.pallas import tpu as pltpu
from jax.sharding import PartitionSpec as P

F32 = jnp.float32
BF16 = jnp.bfloat16
HIGHEST = lax.Precision.HIGHEST
SHIFT_MASS = 0.004
NX, NZ, LAYERS, LEVELS, NODES = 16, 64, 32, 33, 11
SPLIT_X, SPLIT_Z, OWN_Z = 16, 8, 8
FACE_NODES = 121
EDGE_ROWS = 16 * 12
SIDE_ROWS = 192
VMEM_LIMIT = 40 * 1024 * 1024

FACE_SLOTS = ((-1, 0, 0), (1, 0, 0), (0, -1, 0), (0, 1, 0), (0, 0, -1), (0, 0, 1))
EDGE_SLOTS = (
    (0, -1, -1), (0, -1, 1), (0, 1, -1), (0, 1, 1),
    (-1, 0, -1), (-1, 0, 1), (1, 0, -1), (1, 0, 1),
    (-1, -1, 0), (-1, 1, 0), (1, -1, 0), (1, 1, 0),
)
VERTEX_SLOTS = tuple((x, z, y) for x in (-1, 1) for z in (-1, 1) for y in (-1, 1))
SENT_XP, SENT_XM = (6, 7, 10, 11), (4, 5, 8, 9)
SENT_ZP, SENT_ZM = (2, 3, 9, 11), (0, 1, 8, 10)


def orbits():
    seen, result = set(), []
    last = NODES - 1
    for a in range(NODES):
        for b in range(NODES):
            if (a, b) in seen:
                continue
            group, queue = [], [(a, b)]
            while queue:
                node = queue.pop()
                if node in seen:
                    continue
                seen.add(node)
                group.append(node)
                p, q = node
                queue += [(q, p), (last - p, q), (p, last - q)]
            result.append(group)
    return result


ORBITS = orbits()


def face_frame(slot):
    tangents = [axis for axis in range(3) if slot[axis] == 0]
    edges, corners = [], []
    for axis in tangents:
        for sign in (-1, 1):
            corner = list(slot)
            corner[axis] = sign
            edges.append(EDGE_SLOTS.index(tuple(corner)))
    for first in (-1, 1):
        for second in (-1, 1):
            corner = list(slot)
            corner[tangents[0]] = first
            corner[tangents[1]] = second
            corners.append(VERTEX_SLOTS.index(tuple(corner)))
    return edges, corners


def edge_ends(slot):
    axis = slot.index(0)
    ends = []
    for sign in (-1, 1):
        point = list(slot)
        point[axis] = sign
        ends.append(VERTEX_SLOTS.index(tuple(point)))
    return ends


def hartley_table(size):
    phase = np.outer(np.arange(size), np.arange(size)) % size
    angle = 2.0 * np.pi / size * phase
    return (np.cos(angle) + np.sin(angle)) / math.sqrt(size)


HX, HZ = hartley_table(NX), hartley_table(NZ)


def build_tables():
    f32 = lambda a: np.ascontiguousarray(a, dtype=np.float32)
    tables = {}
    forward = np.zeros((NZ, 128))
    top_a, top_b = np.zeros((128, NZ)), np.zeros((128, NZ))
    for gz in range(SPLIT_Z):
        for kk in range(9):
            column = HZ[:, (8 * gz + kk) % NZ]
            forward[:, gz * 16 + kk] = column
            if kk < 7:
                top_a[gz * 16 + 9 + kk] = column
            else:
                top_b[gz * 16 + 2 + kk] = column
    tables["forward"] = f32(forward)
    tables["top_z"] = f32(np.concatenate([top_a, top_a, top_b, top_b], axis=1))
    lane = np.arange(128)
    lane_s, lane_bx, lane_j = lane // 64, lane // 32 % 2, lane % 32
    mix = np.zeros((NX * NX, 128))
    for k in range(NX):
        for x in range(NX):
            mix[k * NX + x] = HX[k, (x + lane_bx) % NX]
    tables["mix"] = f32(mix)
    top_x = np.zeros((2, 16, 128))
    modes = np.zeros((16, 128))
    waves_x = 2.0 - 2.0 * np.cos(2.0 * np.pi / NX * np.arange(NX))
    waves_z = 2.0 - 2.0 * np.cos(2.0 * np.pi / NZ * np.arange(NZ))
    for row in range(16):
        s, blk, par = row // 8, row // 2 % 4, row % 2
        for pair in range(2):
            k = blk * 4 + pair * 2 + par
            top_x[pair, row] = np.where(lane_s == s, HX[k, (lane_j % 16 + lane_bx) % NX], 0.0)
            modes[row, pair * 64 : pair * 64 + 64] = waves_x[k] + waves_z + SHIFT_MASS
    tables["top_x"] = f32(top_x.reshape(32, 128))
    tables["modes"] = f32(modes)
    back_z = np.zeros((SPLIT_Z, 2, 16, 2, NZ))
    for gz in range(SPLIT_Z):
        for kk in range(9):
            for pair in range(2):
                back_z[gz, pair, kk, pair] = HZ[(8 * gz + kk) % NZ]
    tables["back_z"] = f32(back_z.reshape(SPLIT_Z * 32, 128))
    back_x = np.zeros((SPLIT_X, 2, 4, 2, 2, 64))
    for gx in range(SPLIT_X):
        for bx in range(2):
            for k in range(NX):
                back_x[gx, bx, k // 4, k // 2 % 2, k % 2] = HX[(gx + bx) % NX, k]
    tables["back_x"] = f32(back_x.reshape(SPLIT_X * 16, 128))
    pick = np.zeros((32 + 192, 256))

    def fill(row, s, corner, half):
        bx, bz, by = corner // 4, corner // 2 % 2, corner % 2
        base = (((s * 2 + bx) * 2 + by) * 2 + bz) * 16
        for k in range(4):
            pick[row, base + half * 4 + k + bz] = 1.0

    for s in range(2):
        for half in range(2):
            for corner in range(8):
                fill((s * 8 + corner) * 2 + half, s, corner, half)
            for face, slot in enumerate(FACE_SLOTS):
                for place, corner in enumerate(face_frame(slot)[1]):
                    fill(32 + ((half * 2 + s) * 6 + face) * 8 + place, s, corner, half)
    tables["pick"] = f32(pick)
    expand = np.zeros((2, 128, NODES))
    for q in range(FACE_NODES):
        expand[0, q, q // NODES] = 1.0
        expand[1, q, q % NODES] = 1.0
    tables["rows_a"], tables["rows_b"] = f32(expand[0]), f32(expand[1])
    tables["cols_a"], tables["cols_b"] = f32(expand[0].T), f32(expand[1].T)
    return tables


TABLES = build_tables()


def lanes_of(shape):
    return lax.broadcasted_iota(jnp.int32, shape, 1)


def rows_of(shape):
    return lax.broadcasted_iota(jnp.int32, shape, 0)


def roll(value, shift):
    return pltpu.roll(value, shift % 128, 1)


def every(start, size, stride):
    return pl.ds(start, size, stride=stride)


def from_below(low, high=None):
    lane = lanes_of(low.shape)
    return jnp.where(lane % 32 > 0, roll(low, 1), 0.0)


def from_above(value):
    lane = lanes_of(value.shape)
    return jnp.where(lane % 32 < 31, roll(value, -1), 0.0)


def from_before(pair, halo):
    first, second = roll(pair[0], 32), roll(pair[1], 32)
    head = lanes_of(first.shape) < 32
    return jnp.where(head, halo, first), jnp.where(head, first, second)


def from_after(pair, halo):
    first, second = roll(pair[0], 96), roll(pair[1], 96)
    tail = lanes_of(first.shape) >= 96
    return jnp.where(tail, second, first), jnp.where(tail, halo, second)


def coarse_block(vert, station):
    small = (8, 128)
    lane8, row8 = lanes_of(small), rows_of(small)
    group8 = lane8 // 32
    big = (16, 128)
    lane, row = lanes_of(big), rows_of(big)
    group = lane // 32
    low = [vert[every(half, 8, 4), :] for half in range(2)]
    high = [vert[every(2 + half, 8, 4), :] for half in range(2)]

    def turned(halves):
        parts = []
        for half in range(2):
            for turn in range(4):
                moved = roll(halves[half], 32 * turn)
                for bz in range(2):
                    mask = (group8 == row8 // 2) & (row8 % 2 == bz)
                    total = jnp.sum(jnp.where(mask, moved, 0.0), axis=0, keepdims=True)
                    parts.append((half, turn, bz, jnp.broadcast_to(total, big)))
        return parts

    def spread(parts, point, valid):
        out = jnp.zeros(big, F32)
        for half, turn, bz, total in parts:
            k = point - bz
            mask = (k >= 4 * half) & (k < 4 * half + 4) & (((group - k + 8) % 4) == turn) & valid
            out = out + jnp.where(mask, total, 0.0)
        return out

    main = turned([low[half] + from_below(high[half]) for half in range(2)])
    top = turned(high)
    block = spread(main, row, row < 9)
    last = lane % 32 == 31
    top_a = jnp.where(last, spread(top, row - 9, row >= 9), 0.0)
    top_b = jnp.where(last, spread(top, row - 2, (row >= 9) & (row < 11)), 0.0)
    block = block + pltpu.roll(top_a, station + 97, 1)
    return block + pltpu.roll(top_b, station + 113, 1)


def first_kernel(pos, face, edge, vert, fturn, eturn, stiff, xf, ef, xp, xm, zp, zm, cb):
    block = coarse_block(vert, pos[0])
    for device in range(128):
        cb[device * 16 : device * 16 + 16, :] = block

    last = NODES - 1
    for half in range(2):
        turn = fturn[every(half, 6, 2), :]
        swap, flip_a, flip_b = (turn & 4) != 0, (turn & 1) != 0, (turn & 2) != 0
        for s in range(2):
            source = s * 6 * 242 + half
            target = (half * 2 + s) * 6 * 128
            for group in ORBITS:
                x = {n: face[every(source + 2 * (n[0] * 11 + n[1]), 6, 242), :] for n in group}
                x = {(a, b): jnp.where(swap, x[b, a], x[a, b]) for a, b in group}
                x = {(a, b): jnp.where(flip_a, x[last - a, b], x[a, b]) for a, b in group}
                x = {(a, b): jnp.where(flip_b, x[a, last - b], x[a, b]) for a, b in group}
                for a, b in group:
                    xf[every(target + a * 11 + b, 6, 128), :] = x[a, b]
            for pad in range(121, 128):
                xf[every(target + pad, 6, 128), :] = jnp.zeros((6, 128), F32)
        mirror = eturn[every(half, 12, 2), :] != 0
        for s in range(2):
            source = s * 12 * 22 + half
            target = (half * 2 + s) * EDGE_ROWS
            x = [edge[every(source + 2 * p, 12, 22), :] for p in range(NODES)]
            for p in range(NODES):
                ef[every(target + p, 12, 16), :] = jnp.where(mirror, x[last - p], x[p])
            for pad in range(NODES, 16):
                ef[every(target + pad, 12, 16), :] = jnp.zeros((12, 128), F32)

    for half in range(2):
        weight = stiff[half : half + 1, :]
        for s in range(2):
            tile = half * 2 + s
            base = tile * SIDE_ROWS
            for ref, slot, edges in ((xp, 1, SENT_XP), (xm, 0, SENT_XM)):
                ref[base : base + 128, :] = xf[(tile * 6 + slot) * 128 : (tile * 6 + slot + 1) * 128, :]
                ref[base + 127 : base + 128, :] = weight
                for place, e in enumerate(edges):
                    ref[base + 128 + place * 16 : base + 144 + place * 16, :] = ef[
                        (tile * 12 + e) * 16 : (tile * 12 + e + 1) * 16, :
                    ]
    for ref, half, slot, edges in ((zp, 1, 3, SENT_ZP), (zm, 0, 2, SENT_ZM)):
        own = 96 if half else 0
        group = lanes_of((128, 128)) // 32
        faces = [
            roll(xf[((half * 2 + s) * 6 + slot) * 128 : ((half * 2 + s) * 6 + slot + 1) * 128, :],
                 32 * s - own)
            for s in range(2)
        ]
        lines = jnp.concatenate(
            [ef[((half * 2 + s) * 12 + e) * 16 : ((half * 2 + s) * 12 + e + 1) * 16, :]
             for s in range(2) for e in edges],
            axis=0,
        )
        weight = jnp.broadcast_to(roll(stiff[half : half + 1, :], 96 - own), (128, 128))
        out = jnp.where(group == 0, faces[0], faces[1])
        out = jnp.where(group == 2, roll(lines, 64 - own), out)
        ref[...] = jnp.where(group == 3, weight, out)


def corner_kernel(zp, zm, rxm, rxp, out_p, out_m):
    lane, row = lanes_of((128, 128)), rows_of((128, 128))
    group = lane // 32
    for ref, out, half, place in ((zp, out_p, 1, 3), (zm, out_m, 0, 2)):
        own = 96 if half else 0
        out[...] = ref[...]
        for s in range(2):
            base = (half * 2 + s) * SIDE_ROWS + 128 + place * 16
            for third, side in ((2, rxm), (3, rxp)):
                at = s * 64 + third * 16
                moved = roll(side[base : base + 16, :], 64 - own)
                keep = lanes_of((16, 128)) // 32 == 2
                out[at : at + 16, :] += jnp.where(keep, moved, 0.0)
        for r, side in ((1, rxm), (2, rxp)):
            base = half * 2 * SIDE_ROWS + 127
            moved = roll(side[base : base + 1, :], 96 - own)
            out[r : r + 1, :] += jnp.where(lanes_of((1, 128)) >= 96, moved, 0.0)


def parameter_kernel(heights, diag, basis, eigs, ext, modes, rows_a, rows_b, cols_a, cols_b,
                     pivots, carry, back, lift, rdiag, work):
    def dot(x, y):
        return jnp.dot(x, y, precision=HIGHEST, preferred_element_type=F32)

    b = basis[...]
    kron = dot(dot(rows_a[...], b), cols_a[...]) * dot(dot(rows_b[...], b), cols_b[...])
    scale = dot(eigs[...], cols_a[...] + cols_b[...])
    scale = 1.0 / jnp.where(lanes_of((1, 128)) < FACE_NODES, scale, 1.0)
    work[...] = jnp.zeros((256, 128), F32)
    work[0:128, :] = lax.dot_general(
        kron * scale, kron, (((1,), (1,)), ((), ())), precision=HIGHEST,
        preferred_element_type=F32,
    )
    for place in range(4):
        work[128 + 16 * place : 139 + 16 * place, 0:FACE_NODES] = ext[11 * place : 11 * place + 11, :]
    work[192:196, 0:FACE_NODES] = ext[44:48, :]
    full = work[...].T
    high = full.astype(BF16)
    lift[0:128, :] = high
    lift[128:256, :] = (full - high.astype(F32)).astype(BF16)
    row = rows_of((16, 128))
    nodes = jnp.ones((16, 128), F32)
    for p in range(NODES):
        nodes = jnp.where(row == p, diag[0, p], nodes)
    rdiag[...] = 1.0 / nodes

    wave = modes[...]
    tall = [jnp.full((16, 128), heights[0, l], F32) for l in range(LAYERS)]
    inverse = [1.0 / h for h in tall]
    prime = None
    for l in range(LEVELS):
        if l == 0:
            stiff, mass = inverse[0], 0.5 * tall[0]
        elif l == LAYERS:
            stiff, mass = inverse[l - 1], 0.5 * tall[l - 1]
        else:
            stiff, mass = inverse[l - 1] + inverse[l], 0.5 * (tall[l - 1] + tall[l])
        pivot = stiff + wave * mass
        if l:
            pivot = pivot - inverse[l - 1] * prime
        rp = 1.0 / pivot
        pivots[l * 16 : l * 16 + 16, :] = rp
        if l:
            carry[l * 16 : l * 16 + 16, :] = inverse[l - 1] * rp
        else:
            carry[0:16, :] = jnp.zeros((16, 128), F32)
        if l < LAYERS:
            prime = inverse[l] * rp
            back[l * 16 : l * 16 + 16, :] = prime


def solve_kernel(pos, g, pivots, carry, back, forward, mix, top_z, top_x, back_z, back_x, pick,
                 v_out, vb_out, tz, px, zs, vs, ss, cs):
    def dot(x, y):
        return jnp.dot(x, y, precision=HIGHEST, preferred_element_type=F32)

    stations = [g[x * 128 : x * 128 + 128, :] for x in range(NX)]
    tz[...] = dot(forward[...], jnp.concatenate(stations, axis=1))
    total = g[0:128, :]
    for x in range(1, NX):
        total = total + g[x * 128 : x * 128 + 128, :]
    tops = dot(total.T, top_z[...])
    low = rows_of((128, 128)) % 32 < 16
    tops = jnp.where(low, tops[:, 0:128], tops[:, 128:256])
    tops = dot(top_x[...], tops)
    top = jnp.where(lanes_of((16, 128)) < 64, tops[0:16], tops[16:32])

    bx0 = lanes_of((16, 128)) // 32 % 2 == 0
    for m in range(4):
        t = [tz[m * 16 : m * 16 + 16, x * 128 : x * 128 + 128] for x in range(NX)]
        for kp in range(8):
            pair = []
            for par in range(2):
                k = kp * 2 + par
                acc = t[0] * mix[k * NX : k * NX + 1, :]
                for x in range(1, NX):
                    acc = acc + t[x] * mix[k * NX + x : k * NX + x + 1, :]
                pair.append(acc)
            even, odd = pair
            px[kp * 64 + m * 16 : kp * 64 + m * 16 + 16, :] = jnp.where(
                bx0, even + roll(even, 96), odd + roll(odd, 32)
            )
    for blk in range(4):
        turned = px[blk * 128 : blk * 128 + 128, :].T
        zs[blk * 64 : blk * 64 + 64, :] = turned[0:64]
        zs[256 + blk * 64 : 320 + blk * 64, :] = turned[64:128]

    value = None
    for l in range(LEVELS):
        rhs = zs[every(l, 16, 32), :] if l < LAYERS else top
        at = slice(l * 16, l * 16 + 16)
        value = rhs * pivots[at, :] if l == 0 else rhs * pivots[at, :] + carry[at, :] * value
        vs[at, :] = value
    ss[...] = jnp.zeros((1024, 128), F32)
    for l in range(LEVELS - 1, -1, -1):
        if l < LEVELS - 1:
            at = slice(l * 16, l * 16 + 16)
            value = vs[at, :] + back[at, :] * value
        ss[every(l, 16, 64), :] = value

    hz = back_z[pl.ds(pl.multiple_of(pos[1] * 32, 32), 32), :]
    q = lax.dot_general(hz, ss[...], (((1,), (1,)), ((), ())), precision=HIGHEST,
                        preferred_element_type=F32)
    hx = back_x[pl.ds(pl.multiple_of(pos[0] * 16, 16), 16), :]
    lane, row = lanes_of((16, 128)), rows_of((16, 128))
    group = lane // 32
    for s in range(2):
        for bx in range(2):
            acc = None
            for blk in range(4):
                for pair in range(2):
                    r = (bx * 4 + blk) * 2 + pair
                    term = q[pair * 16 : pair * 16 + 16, (s * 4 + blk) * 128 : (s * 4 + blk + 1) * 128]
                    term = term * hx[r : r + 1, :]
                    acc = term if acc is None else acc + term
            acc = acc + roll(acc, 64)
            for by in range(2):
                plain = roll(acc, 127) if by else acc
                moved = roll(plain, 32)
                mixed = jnp.where(group % 2 == 1, moved, plain)
                for bz in range(2):
                    base = (((s * 2 + bx) * 2 + by) * 2 + bz) * 16
                    keep = (row - bz + 4) % 4 == group
                    cs[base : base + 16, :] = jnp.where(keep, mixed, 0.0)
    picked = dot(pick[...], cs[...])
    v_out[...] = picked[0:32]
    vb_out[...] = picked[32:224]


def final_kernel(xf, ef, rxm, rxp, rzm, rzp, stiff, v, vb, lift, rdiag, fturn, eturn,
                 face_out, edge_out, oq, ev):
    last = NODES - 1
    w = [stiff[half : half + 1, :] for half in range(2)]

    def tile(half, s, f):
        at = ((half * 2 + s) * 6 + f) * 128
        return xf[at : at + 128, :]

    def line(half, s, e):
        at = ((half * 2 + s) * 12 + e) * 16
        return ef[at : at + 16, :]

    def side_face(ref, half, s):
        at = (half * 2 + s) * SIDE_ROWS
        return ref[at : at + 128, :]

    def side_line(ref, half, s, place):
        at = (half * 2 + s) * SIDE_ROWS + 128 + place * 16
        return ref[at : at + 16, :]

    def side_weight(ref, half):
        at = half * 2 * SIDE_ROWS + 127
        return ref[at : at + 1, :]

    def halo_line(ref, s, place, to):
        at = s * 64 + place * 16
        return roll(ref[at : at + 16, :], to - 64)

    wxm = [w[half] + side_weight(rxm, half) for half in range(2)]
    wxp = [w[half] + side_weight(rxp, half) for half in range(2)]
    wzm_in = [roll(rzm[r : r + 1, :], 32) for r in range(3)]
    wzp_in = [rzp[r : r + 1, :] for r in range(3)]

    def add_before(pair, halo):
        moved = from_before(pair, halo)
        return [pair[0] + moved[0], pair[1] + moved[1]]

    def add_after(pair, halo):
        moved = from_after(pair, halo)
        return [pair[0] + moved[0], pair[1] + moved[1]]

    wzm, wzp = add_before(w, wzm_in[0]), add_after(w, wzp_in[0])
    corner = [add_before(wxm, wzm_in[1]), add_after(wxm, wzp_in[1]),
              add_before(wxp, wzm_in[2]), add_after(wxp, wzp_in[2])]
    below = lambda pair: [x + from_below(x) for x in pair]
    above = lambda pair: [x + from_above(x) for x in pair]
    covers = [below(wzm), above(wzm), below(wzp), above(wzp),
              below(wxm), above(wxm), below(wxp), above(wxp)] + corner
    face_covers = [wxm, wxp, wzm, wzp, below(w), above(w)]
    rec_face = [[1.0 / x for x in pair] for pair in face_covers]
    rec_edge = [[1.0 / x for x in pair] for pair in covers]

    row16 = rows_of((16, 128))
    high_t = (row16 + 1).astype(F32) / (NODES + 1.0)
    low_t = 1.0 - high_t
    diag = rdiag[...]

    for s in range(2):
        e = {}
        for half in range(2):
            for k in range(4):
                e[k, half] = line(half, s, k)
            for k, place in ((4, 0), (5, 1), (8, 2), (9, 3)):
                e[k, half] = line(half, s, k) + side_line(rxm, half, s, place)
            for k, place in ((6, 0), (7, 1), (10, 2), (11, 3)):
                e[k, half] = line(half, s, k) + side_line(rxp, half, s, place)
        both = lambda k: (e[k, 0], e[k, 1])
        sums = {}
        for k, other, place in ((0, 2, 0), (1, 3, 1), (8, 9, 2), (10, 11, 3)):
            moved = from_before(both(other), halo_line(rzm, s, place, 0))
            for half in range(2):
                sums[k, half] = e[k, half] + moved[half]
        for k, other, place in ((2, 0, 0), (3, 1, 1), (9, 8, 2), (11, 10, 3)):
            moved = from_after(both(other), halo_line(rzp, s, place, 96))
            for half in range(2):
                sums[k, half] = e[k, half] + moved[half]
        for k in range(4, 8):
            for half in range(2):
                sums[k, half] = e[k, half]
        for half in range(2):
            for k in range(0, 8, 2):
                a, b = sums[k, half], sums[k + 1, half]
                sums[k, half], sums[k + 1, half] = a + from_below(b), b + from_above(a)
            tilebase = (half * 2 + s) * EDGE_ROWS
            vertex = v[every(s * 16 + half, 8, 2), :]
            for k in range(12):
                start, stop = edge_ends(EDGE_SLOTS[k])
                local = sums[k, half] * (diag * rec_edge[k][half])
                ev[tilebase + k * 16 : tilebase + k * 16 + 16, :] = (
                    local + low_t * vertex[start : start + 1] + high_t * vertex[stop : stop + 1]
                )
        for half in range(2):
            columns = []
            for f in range(6):
                own = tile(half, s, f)
                if f == 0:
                    total = own + side_face(rxm, half, s)
                elif f == 1:
                    total = own + side_face(rxp, half, s)
                elif f == 2:
                    halo = roll(rzm[...], -32 * s)
                    total = own + from_before((tile(0, s, 3), tile(1, s, 3)), halo)[half]
                elif f == 3:
                    halo = roll(rzp[...], 96 - 32 * s)
                    total = own + from_after((tile(0, s, 2), tile(1, s, 2)), halo)[half]
                elif f == 4:
                    total = own + from_below(tile(half, s, 5))
                else:
                    total = own + from_above(tile(half, s, 4))
                edges = face_frame(FACE_SLOTS[f])[0]
                tilebase = (half * 2 + s) * EDGE_ROWS
                at = ((half * 2 + s) * 6 + f) * 8
                columns.append(jnp.concatenate(
                    [total * rec_face[f][half]]
                    + [ev[tilebase + k * 16 : tilebase + k * 16 + 16, :] for k in edges]
                    + [vb[at : at + 8, :], jnp.zeros((56, 128), F32)], axis=0))
            full = jnp.concatenate(columns, axis=1)
            high = full.astype(BF16)
            rest = (full - high.astype(F32)).astype(BF16)
            main = jnp.dot(lift[...], high, preferred_element_type=F32)
            more = jnp.dot(lift[0:128, :], rest, preferred_element_type=F32)
            done = main[0:128] + (main[128:256] + more)
            for f in range(6):
                at = ((half * 2 + s) * 6 + f) * 128
                oq[at : at + 128, :] = done[:, f * 128 : f * 128 + 128]

    for half in range(2):
        turn = fturn[every(half, 6, 2), :]
        swap, flip_a, flip_b = (turn & 4) != 0, (turn & 1) != 0, (turn & 2) != 0
        mirror = eturn[every(half, 12, 2), :] != 0
        for s in range(2):
            target = s * 6 * 242 + half
            source = (half * 2 + s) * 6 * 128
            for group in ORBITS:
                x = {n: oq[every(source + n[0] * 11 + n[1], 6, 128), :] for n in group}
                x = {(a, b): jnp.where(flip_a, x[last - a, b], x[a, b]) for a, b in group}
                x = {(a, b): jnp.where(flip_b, x[a, last - b], x[a, b]) for a, b in group}
                x = {(a, b): jnp.where(swap, x[b, a], x[a, b]) for a, b in group}
                for a, b in group:
                    face_out[every(target + 2 * (a * 11 + b), 6, 242), :] = x[a, b]
            target = s * 12 * 22 + half
            source = (half * 2 + s) * EDGE_ROWS
            x = [ev[every(source + p, 12, 16), :] for p in range(NODES)]
            for p in range(NODES):
                edge_out[every(target + 2 * p, 12, 22), :] = jnp.where(mirror, x[last - p], x[p])


VMEM = pl.BlockSpec(memory_space=pltpu.VMEM)
SMEM = pl.BlockSpec(memory_space=pltpu.SMEM)


def call(kernel, outs, args, scalars=0, scratch=(), flops=0, name=None):
    shapes = [jax.ShapeDtypeStruct(o, F32) if isinstance(o, tuple) else o for o in outs]
    size = sum(int(np.prod(a.shape)) * 4 for a in args)
    return pl.pallas_call(
        kernel,
        out_shape=shapes,
        in_specs=[SMEM] * scalars + [VMEM] * (len(args) - scalars),
        out_specs=[VMEM] * len(shapes),
        scratch_shapes=[pltpu.VMEM(o, F32) for o in scratch],
        compiler_params=pltpu.CompilerParams(vmem_limit_bytes=VMEM_LIMIT),
        cost_estimate=pl.CostEstimate(flops=flops, bytes_accessed=size, transcendentals=0),
        name=name,
    )(*args)


def per_device(face_residual, edge_residual, vertex_residual, face_orient, edge_orient, stiffness,
               face_basis, face_eigs, extension, edge_diag, element_heights):
    table = {key: jnp.asarray(value) for key, value in TABLES.items()}
    pos = jnp.stack([lax.axis_index("gx"), lax.axis_index("gz")]).astype(jnp.int32)
    face = face_residual.reshape(2 * 6 * 121 * 2, 128)
    edge = edge_residual.reshape(2 * 12 * 11 * 2, 128)
    vert = vertex_residual.reshape(32, 128)
    fturn = face_orient.reshape(12, 128)
    eturn = edge_orient.reshape(24, 128)
    stiff = stiffness.reshape(2, 128)
    tiles = 24 * 128
    xf, ef, xp, xm, zp, zm, cb = call(
        first_kernel,
        [(tiles, 128), (4 * EDGE_ROWS, 128), (4 * SIDE_ROWS, 128), (4 * SIDE_ROWS, 128),
         (128, 128), (128, 128), (2048, 128)],
        (pos, face, edge, vert, fturn, eturn, stiff), scalars=1, name="frame")
    up = lambda n: [(i, (i + 1) % n) for i in range(n)]
    down = lambda n: [((i + 1) % n, i) for i in range(n)]
    rxm = lax.ppermute(xp, "gx", up(SPLIT_X))
    rxp = lax.ppermute(xm, "gx", down(SPLIT_X))
    pivots, carry, back, lift, rdiag = call(
        parameter_kernel,
        [(LEVELS * 16, 128), (LEVELS * 16, 128), (LAYERS * 16, 128),
         jax.ShapeDtypeStruct((256, 256), BF16), (16, 128)],
        (element_heights.reshape(1, LAYERS), edge_diag.reshape(1, NODES), face_basis,
         face_eigs.reshape(1, NODES), extension.T, table["modes"], table["rows_a"],
         table["rows_b"], table["cols_a"], table["cols_b"]),
        scalars=2, scratch=((256, 128),), name="parameters")
    g = lax.all_to_all(cb.reshape(128, 16, 128), ("gx", "gz"), 0, 0).reshape(2048, 128)
    zp, zm = call(corner_kernel, [(128, 128), (128, 128)], (zp, zm, rxm, rxp), name="corners")
    rzm = lax.ppermute(zp, "gz", up(SPLIT_Z))
    rzp = lax.ppermute(zm, "gz", down(SPLIT_Z))
    v, vb = call(
        solve_kernel, [(32, 128), (192, 128)],
        (pos, g, pivots, carry, back) + tuple(table[k] for k in (
            "forward", "mix", "top_z", "top_x", "back_z", "back_x", "pick")),
        scalars=1,
        scratch=((64, 2048), (512, 128), (512, 128), (LEVELS * 16, 128), (1024, 128), (256, 128)),
        flops=200_000_000, name="coarse")
    face_out, edge_out = call(
        final_kernel, [(2904, 128), (528, 128)],
        (xf, ef, rxm, rxp, rzm, rzp, stiff, v, vb, lift, rdiag, fturn, eturn),
        scratch=((tiles, 128), (4 * EDGE_ROWS, 128)), name="finish")
    return (face_out.reshape(face_residual.shape), edge_out.reshape(edge_residual.shape),
            v.reshape(vertex_residual.shape))


def solution(mesh):
    columns = P(None, None, None, "gx", "gz")
    placed = (columns, columns, P(None, None, "gx", "gz"), P(None, "gx", "gz"),
              P(None, "gx", "gz"), P("gx", "gz"), P(), P(), P(), P(), P())
    return jax.shard_map(
        per_device, mesh=mesh, in_specs=placed,
        out_specs=(columns, columns, P(None, None, "gx", "gz")), check_vma=False)
```

time: 695 us -> 81.1 us (0.12); the launches traced: 684 us -> 79.9 us
  other arithmetic: 246 us -> 0.79 us
  local copies, waits for them, and re-layouts: 258 us -> 29.9 us
  blocking collectives: 68.4 us -> 0 us
  matrix products: 61.5 us -> 0 us
  between operations: 22.7 us -> 0.78 us
  Pallas kernels: 0 us -> 12.7 us
  waiting for transfers between devices: 7.7 us -> 14.9 us
    add x8 -> x0, other arithmetic: 87.8 us -> none  [the longest x2 70.2 us: level_solve(): pivot = diagonal + inverse[level - 1] * primes[-1]]
    all_gather x2 -> x0, blocking collectives: 68.4 us -> none  [the longest x1 50.7 us: per_device(): gathered = lax.all_gather(gathered, 'gz', axis=2, tiled=True)]
    select_n x9 -> x0, other arithmetic: 61.7 us -> none  [the longest x1 19.3 us: faces_from_frame(): return jnp.where(turn // 4 % 2 == 1, jnp.swapaxes(values, 2, 3), values)]
    dot_general x14 -> x0, matrix products: 61.5 us -> none  [the longest x1 14.6 us: finish(): jnp.einsum('bj,sfajxzy->sfabxzy', face_basis, direct, precision=HIGHEST)]
    unnamed x43 -> x1, other arithmetic: 52.9 us -> 0.71 us
    unnamed x346 -> x88, local copies, waits for them, and re-layouts: 78.1 us -> 29.9 us
    rev x4 -> x0, local copies, waits for them, and re-layouts: 42.1 us -> none  [the longest x1 16.7 us: faces_from_frame(): values = jnp.where(turn % 2 == 1, jnp.flip(values, 2), values)]
    slice x36 -> x0, local copies, waits for them, and re-layouts: 39.9 us -> none  [the longest x16 12.4 us: shift_levels(): return jnp.concatenate([array[..., 1:], zeros], axis=-1)]
  transfers between devices with their start and end apart: 8 -> 5, of which waited for: 2 -> 1; matrix products, arithmetic and copies ran while one was open for 46% -> 0% of each run, Pallas kernels for 0% -> 8%
where the time goes in v1:
time: 81.1 us; the launch traced here: 79.9 us
  local copies, waits for them, and re-layouts  29.9 us (37%)
  starting transfers between devices  20.8 us (26%)
  waiting for transfers between devices  14.9 us (18%)
  Pallas kernels  12.7 us (16%)
    unnamed x88, local copies, waits for them, and re-layouts  29.9 us
    ppermute x1, waiting for transfers between devices, per_device(): rxm = lax.ppermute(xp, 'gx', up(SPLIT_X))  14.9 us
    pallas_call x5, Pallas kernels, call(): pl.pallas_call(kernel, out_shape=shapes, in_specs=[SMEM] * scalars + [VME...  12.7 us
    all_to_all x1, starting transfers between devices, per_device(): lax.all_to_all(cb.reshape(128, 16, 128), ('gx', 'gz'), 0, 0)  11.1 us
    ppermute x1, starting transfers between devices, per_device(): rxp = lax.ppermute(xm, 'gx', down(SPLIT_X))  3.84 us
    ppermute x1, starting transfers between devices, per_device(): rzp = lax.ppermute(zm, 'gz', down(SPLIT_Z))  2.92 us
    ppermute x1, starting transfers between devices, per_device(): rzm = lax.ppermute(zp, 'gz', up(SPLIT_Z))  2.77 us
  transfers between devices with their start and end apart: 5, of which 1 were waited for; matrix products, arithmetic and copies ran while one was open for 0% of the time, Pallas kernels for 8%

profile of v1, /device:TPU:0, one launch (start us, length us, event | category | flops | bytes accessed | tf_op | source)
XLA Modules:
  0.0 79.9 jit_solution(8563973884557008085)
XLA Ops:
  1.4 1.4 %copy-done = f32[2,6,121,1,256]{4,3,2,1,0:T(1,128)S(1)} copy-done((f32[2,6,121,1,256]{4,3,2,1,0:T(1,128)S(1)}, f32[2,6,121,1,256]{4,3,2,1,0:T(1,128)}, u32[]{:S(2)}) %copy-start) | copy-done | bytes 1486872
  2.8 1.0 %copy-done.4 = f32[2,12,11,1,256]{4,3,2,1,0:T(1,128)S(1)} copy-done((f32[2,12,11,1,256]{4,3,2,1,0:T(1,128)S(1)}, f32[2,12,11,1,256]{4,3,2,1,0:T(1,128)}, u32[]{:S(2)}) %copy-start.4) | copy-done | bytes 270360
  5.9 1.9 %frame.1 = (f32[3072,128]{1,0:T(8,128)S(1)}, f32[768,128]{1,0:T(8,128)S(1)}, f32[768,128]{1,0:T(8,128)S(1)}, f32[768,128]{1,0:T(8,128)S(1)}, f32[128,128]{1,0:T(...) custom-call(s32[2]{0:T(128)S(1)} %pad_add_fusion.pos, f32[2904,128]{1,0:T(8,128)S(1)} %bitcast.17, ...), custom_call_target="tpu_custom_call" | custom-call | bytes 1793032 | tf_op jit(solution)/shard_map/frame/pallas_call | solution.py:609
  7.8 1.0 %copy-done.1 = f32[2048,128]{1,0:T(8,128)} copy-done((f32[2048,128]{1,0:T(8,128)}, f32[2048,128]{1,0:T(8,128)S(1)}, u32[]{:S(2)}) %copy-start.1) | copy-done | bytes 1048600
  10.8 0.8 copy-done.42
  12.3 11.1 %all-to-all-start = ((f32[128,16,128]{2,1,0:T(8,128)}), f32[128,16,128]{2,1,0:T(8,128)S(1)}, u32[]{:S(2)}, u32[]{:S(2)}) async-start(f32[128,16,128]{2,1,0:T(8,128)} %bitcast.18), calls=%async_computation | async-start | bytes 2097152 | tf_op jit(solution)/shard_map/all_to_all | solution.py:649
  23.5 3.8 %collective-permute-start.1 = (f32[768,128]{1,0:T(8,128)}, f32[768,128]{1,0:T(8,128)S(1)}, u32[]{:S(2)}, u32[]{:S(2)}) collective-permute-start(f32[768,128]{1,0:T(8,128)} %copy-done.42), channel_id=1, source_target_pairs={{8,0},{16,8},{24,16},{32,24},{40,32},{48,40},{56,48},{64,56},{72,6... | collective-permute-start | bytes 1179656 | tf_op jit(solution)/shard_map/ppermute | solution.py:640
  27.4 14.9 %collective-permute-done.rxm = f32[768,128]{1,0:T(8,128)S(1)} collective-permute-done((f32[768,128]{1,0:T(8,128)}, f32[768,128]{1,0:T(8,128)S(1)}, u32[]{:S(2)}, u32[]{:S(2)}) %collective-permute-start) | collective-permute-done | bytes 393248 | tf_op jit(solution)/shard_map/ppermute | solution.py:639
  42.3 0.8 %copy-done.19 = f32[128,128]{1,0:T(8,128)S(1)} copy-done((f32[128,128]{1,0:T(8,128)S(1)}, f32[128,128]{1,0:T(8,128)}, u32[]{:S(2)}) %copy-start.19) | copy-done | bytes 65560
  43.2 0.8 %copy-done.21 = f32[128,128]{1,0:T(8,128)S(1)} copy-done((f32[128,128]{1,0:T(8,128)S(1)}, f32[128,128]{1,0:T(8,128)}, u32[]{:S(2)}) %copy-start.21) | copy-done | bytes 65560
  44.7 2.8 %collective-permute-start.2 = (f32[128,128]{1,0:T(8,128)}, f32[128,128]{1,0:T(8,128)}, u32[]{:S(2)}, u32[]{:S(2)}) collective-permute-start(f32[128,128]{1,0:T(8,128)} %get-tuple-element.27), channel_id=1, source_target_pairs={{0,1},{1,2},{2,3},{3,4},{4,5},{5,6},{6,7},{7,0},{8,9},{9,10},{10,1... | collective-permute-start | bytes 196616 | tf_op jit(solution)/shard_map/ppermute | solution.py:651
  47.5 2.9 %collective-permute-start.3 = (f32[128,128]{1,0:T(8,128)}, f32[128,128]{1,0:T(8,128)}, u32[]{:S(2)}, u32[]{:S(2)}) collective-permute-start(f32[128,128]{1,0:T(8,128)} %get-tuple-element.28), channel_id=1, source_target_pairs={{1,0},{2,1},{3,2},{4,3},{5,4},{6,5},{7,6},{0,7},{9,8},{10,9},{11,1... | collective-permute-start | bytes 196616 | tf_op jit(solution)/shard_map/ppermute | solution.py:652
  50.4 0.8 %copy-done.22 = f32[128,11]{1,0:T(8,128)S(1)} copy-done((f32[128,11]{1,0:T(8,128)S(1)}, f32[128,11]{1,0:T(8,128)}, u32[]{:S(2)}) %copy-start.22) | copy-done | bytes 5656
  51.3 0.8 %copy-done.23 = f32[128,11]{1,0:T(8,128)S(1)} copy-done((f32[128,11]{1,0:T(8,128)S(1)}, f32[128,11]{1,0:T(8,128)}, u32[]{:S(2)}) %copy-start.23) | copy-done | bytes 5656
  57.6 1.6 %parameters.1 = (f32[528,128]{1,0:T(8,128)S(1)}, f32[528,128]{1,0:T(8,128)S(1)}, f32[512,128]{1,0:T(8,128)S(1)}, bf16[256,256]{1,0:T(8,128)(2,1)S(1)}, f32[16,128]{1,0:T(8,128)S(1)}) custom-call(f32[1,32]{1,0:T(1,128)S(1)} %bitcast.27, f32[1,11]{1,0:T(1,128)S(1)} %bitcast.28, f32[11,11]{1,0:T(8,128)S(1)} %copy-done.31, f32[1,11]{1,0:T(1,128)S(1)} %bitcast.29, ...), custom_call_target="tpu_custom_call" | custom-call | bytes 54652 | tf_op jit(solution)/shard_map/parameters/pallas_call | solution.py:609
  62.0 1.0 %copy-done.6 = f32[528,128]{1,0:T(8,128)S(1)} copy-done((f32[528,128]{1,0:T(8,128)S(1)}, f32[528,128]{1,0:T(8,128)}, u32[]{:S(2)}) %copy-start.6) | copy-done | bytes 270360
  63.0 1.0 %copy-done.8 = f32[528,128]{1,0:T(8,128)S(1)} copy-done((f32[528,128]{1,0:T(8,128)S(1)}, f32[528,128]{1,0:T(8,128)}, u32[]{:S(2)}) %copy-start.8) | copy-done | bytes 270360
  63.9 0.9 %copy-done.10 = f32[512,128]{1,0:T(8,128)S(1)} copy-done((f32[512,128]{1,0:T(8,128)S(1)}, f32[512,128]{1,0:T(8,128)}, u32[]{:S(2)}) %copy-start.10) | copy-done | bytes 262168
  64.9 0.9 %copy-done.11 = f32[224,256]{1,0:T(8,128)S(1)} copy-done((f32[224,256]{1,0:T(8,128)S(1)}, f32[224,256]{1,0:T(8,128)}, u32[]{:S(2)}) %copy-start.11) | copy-done | bytes 229400
  65.8 0.9 %copy-done.13 = f32[128,256]{1,0:T(8,128)S(1)} copy-done((f32[128,256]{1,0:T(8,128)S(1)}, f32[128,256]{1,0:T(8,128)}, u32[]{:S(2)}) %copy-start.13) | copy-done | bytes 131096
  66.7 0.9 %copy-done.14 = f32[256,128]{1,0:T(8,128)S(1)} copy-done((f32[256,128]{1,0:T(8,128)S(1)}, f32[256,128]{1,0:T(8,128)}, u32[]{:S(2)}) %copy-start.14) | copy-done | bytes 131096
  67.6 0.9 %copy-done.15 = f32[256,128]{1,0:T(8,128)S(1)} copy-done((f32[256,128]{1,0:T(8,128)S(1)}, f32[256,128]{1,0:T(8,128)}, u32[]{:S(2)}) %copy-start.15) | copy-done | bytes 131096
  70.7 4.2 %coarse.1 = (f32[32,128]{1,0:T(8,128)}, f32[192,128]{1,0:T(8,128)S(1)}) custom-call(s32[2]{0:T(128)S(1)} %copy-done.38, f32[2048,128]{1,0:T(8,128)S(1)} %bitcast.16, f32[528,128]{1,0:T(8,128)S(1)} %copy-done.6, f32[528,128]{1,0:T(8,128)S(1)} %copy-done.8, f32[512,128]{1,0:T(8,128)S(1)} %copy-done.10, f32[64,128]{1,0:T(8,128)S(1)} %copy-done.26, ...), custom_call_target="tpu_custom_call" | custom-call | flops 200000000 | bytes 2654216 | tf_op jit(solution)/shard_map/coarse/pallas_call | solution.py:609
  75.6 4.3 %finish.1 = (f32[2904,128]{1,0:T(8,128)}, f32[528,128]{1,0:T(8,128)}) custom-call(f32[3072,128]{1,0:T(8,128)S(1)} %get-tuple-element.21.xf, f32[768,128]{1,0:T(8,128)S(1)} %copy-done.3, f32[768,128]{1,0:T(8,128)S(1)} %collective-permute-done.rxm, f32[768,128]{1,0:T(8,128)S(1)} %collective-permute-done.1.rxp, f32[128,128]{1,0:T(8,128)} %collective-permute-done.2.rzm, ...), custom_call_target="tpu_custom_call" | custom-call | bytes 3288064 | tf_op jit(solution)/shard_map/finish/pallas_call | solution.py:609
  (82 shorter events, 17.6 us)
Async XLA Ops:
  1.4 10.1 %copy-start.37 = (s32[2]{0:T(128)}, s32[2]{0:T(128)S(1)}, u32[]{:S(2)}) copy-start(s32[2]{0:T(128)S(1)} %pad_add_fusion.pos) | copy-start | bytes 28
  1.4 1.4 %copy-start = (f32[2,6,121,1,256]{4,3,2,1,0:T(1,128)S(1)}, f32[2,6,121,1,256]{4,3,2,1,0:T(1,128)}, u32[]{:S(2)}) copy-start(f32[2,6,121,1,256]{4,3,2,1,0:T(1,128)} %param.23) | copy-start | bytes 4460548
  2.8 1.0 %copy-start.4 = (f32[2,12,11,1,256]{4,3,2,1,0:T(1,128)S(1)}, f32[2,12,11,1,256]{4,3,2,1,0:T(1,128)}, u32[]{:S(2)}) copy-start(f32[2,12,11,1,256]{4,3,2,1,0:T(1,128)} %param.24) | copy-start | bytes 811012
  7.8 1.0 %copy-start.1 = (f32[2048,128]{1,0:T(8,128)}, f32[2048,128]{1,0:T(8,128)S(1)}, u32[]{:S(2)}) copy-start(f32[2048,128]{1,0:T(8,128)S(1)} %get-tuple-element.29) | copy-start | bytes 3145732
  11.6 50.4 %copy-start.12 = (f32[256,128]{1,0:T(8,128)S(1)}, f32[256,128]{1,0:T(8,128)}, u32[]{:S(2)}) copy-start(f32[256,128]{1,0:T(8,128)} %constant.35.clone.mix) | copy-start | bytes 393220
  12.3 49.6 %all-to-all-start = ((f32[128,16,128]{2,1,0:T(8,128)}), f32[128,16,128]{2,1,0:T(8,128)S(1)}, u32[]{:S(2)}, u32[]{:S(2)}) async-start(f32[128,16,128]{2,1,0:T(8,128)} %bitcast.18), calls=%async_computation | async-start | bytes 2097152 | tf_op jit(solution)/shard_map/all_to_all | solution.py:649
  23.5 18.9 %collective-permute-start = (f32[768,128]{1,0:T(8,128)}, f32[768,128]{1,0:T(8,128)S(1)}, u32[]{:S(2)}, u32[]{:S(2)}) collective-permute-start(f32[768,128]{1,0:T(8,128)} %copy-done.43), channel_id=1, source_target_pairs={{0,8},{8,16},{16,24},{24,32},{32,40},{40,48},{48,56},{56,64},{64,7... | collective-permute-start | bytes 1179656 | tf_op jit(solution)/shard_map/ppermute | solution.py:639
  23.5 18.8 %collective-permute-start.1 = (f32[768,128]{1,0:T(8,128)}, f32[768,128]{1,0:T(8,128)S(1)}, u32[]{:S(2)}, u32[]{:S(2)}) collective-permute-start(f32[768,128]{1,0:T(8,128)} %copy-done.42), channel_id=1, source_target_pairs={{8,0},{16,8},{24,16},{32,24},{40,32},{48,40},{56,48},{64,56},{72,6... | collective-permute-start | bytes 1179656 | tf_op jit(solution)/shard_map/ppermute | solution.py:640
  42.3 0.8 %copy-start.19 = (f32[128,128]{1,0:T(8,128)S(1)}, f32[128,128]{1,0:T(8,128)}, u32[]{:S(2)}) copy-start(f32[128,128]{1,0:T(8,128)} %copy-done.18) | copy-start | bytes 196612
  43.2 0.8 %copy-start.21 = (f32[128,128]{1,0:T(8,128)S(1)}, f32[128,128]{1,0:T(8,128)}, u32[]{:S(2)}) copy-start(f32[128,128]{1,0:T(8,128)} %copy-done.20) | copy-start | bytes 196612
  44.7 30.1 %collective-permute-start.2 = (f32[128,128]{1,0:T(8,128)}, f32[128,128]{1,0:T(8,128)}, u32[]{:S(2)}, u32[]{:S(2)}) collective-permute-start(f32[128,128]{1,0:T(8,128)} %get-tuple-element.27), channel_id=1, source_target_pairs={{0,1},{1,2},{2,3},{3,4},{4,5},{5,6},{6,7},{7,0},{8,9},{9,10},{10,1... | collective-permute-start | bytes 196616 | tf_op jit(solution)/shard_map/ppermute | solution.py:651
  47.5 27.3 %collective-permute-start.3 = (f32[128,128]{1,0:T(8,128)}, f32[128,128]{1,0:T(8,128)}, u32[]{:S(2)}, u32[]{:S(2)}) collective-permute-start(f32[128,128]{1,0:T(8,128)} %get-tuple-element.28), channel_id=1, source_target_pairs={{1,0},{2,1},{3,2},{4,3},{5,4},{6,5},{7,6},{0,7},{9,8},{10,9},{11,1... | collective-permute-start | bytes 196616 | tf_op jit(solution)/shard_map/ppermute | solution.py:652
  50.4 0.8 %copy-start.22 = (f32[128,11]{1,0:T(8,128)S(1)}, f32[128,11]{1,0:T(8,128)}, u32[]{:S(2)}) copy-start(f32[128,11]{1,0:T(8,128)} %constant.41.clone.rows_a) | copy-start | bytes 16900
  62.0 12.9 %copy-start.3 = (f32[768,128]{1,0:T(8,128)S(1)}, f32[768,128]{1,0:T(8,128)}, u32[]{:S(2)}) copy-start(f32[768,128]{1,0:T(8,128)} %copy-done.2) | copy-start | bytes 1179652
  62.0 1.0 %copy-start.6 = (f32[528,128]{1,0:T(8,128)S(1)}, f32[528,128]{1,0:T(8,128)}, u32[]{:S(2)}) copy-start(f32[528,128]{1,0:T(8,128)} %copy-done.5) | copy-start | bytes 811012
  63.0 1.0 %copy-start.8 = (f32[528,128]{1,0:T(8,128)S(1)}, f32[528,128]{1,0:T(8,128)}, u32[]{:S(2)}) copy-start(f32[528,128]{1,0:T(8,128)} %copy-done.7) | copy-start | bytes 811012
  63.9 0.9 %copy-start.10 = (f32[512,128]{1,0:T(8,128)S(1)}, f32[512,128]{1,0:T(8,128)}, u32[]{:S(2)}) copy-start(f32[512,128]{1,0:T(8,128)} %copy-done.9) | copy-start | bytes 786436
  64.9 0.9 %copy-start.11 = (f32[224,256]{1,0:T(8,128)S(1)}, f32[224,256]{1,0:T(8,128)}, u32[]{:S(2)}) copy-start(f32[224,256]{1,0:T(8,128)} %constant.40.clone.pick) | copy-start | bytes 688132
  65.8 0.9 %copy-start.13 = (f32[128,256]{1,0:T(8,128)S(1)}, f32[128,256]{1,0:T(8,128)}, u32[]{:S(2)}) copy-start(f32[128,256]{1,0:T(8,128)} %constant.34.clone.top_z) | copy-start | bytes 393220
  66.7 0.9 %copy-start.14 = (f32[256,128]{1,0:T(8,128)S(1)}, f32[256,128]{1,0:T(8,128)}, u32[]{:S(2)}) copy-start(f32[256,128]{1,0:T(8,128)} %constant.38.clone.back_z) | copy-start | bytes 393220
  67.6 0.9 %copy-start.15 = (f32[256,128]{1,0:T(8,128)S(1)}, f32[256,128]{1,0:T(8,128)}, u32[]{:S(2)}) copy-start(f32[256,128]{1,0:T(8,128)} %constant.39.clone.back_x) | copy-start | bytes 393220
  70.7 4.2 %copy-start.17 = (bf16[256,256]{1,0:T(8,128)(2,1)S(1)}, bf16[256,256]{1,0:T(8,128)(2,1)}, u32[]{:S(2)}) copy-start(bf16[256,256]{1,0:T(8,128)(2,1)} %copy-done.16) | copy-start | bytes 393220
  70.7 4.2 %copy-start.25 = (s32[12,1,256]{2,1,0:T(1,128)S(1)}, s32[12,1,256]{2,1,0:T(1,128)}, u32[]{:S(2)}) copy-start(s32[12,1,256]{2,1,0:T(1,128)} %param.27) | copy-start | bytes 36868
  70.7 4.2 %copy-start.36 = (f32[1,256]{1,0:T(1,128)S(1)}, f32[1,256]{1,0:T(1,128)}, u32[]{:S(2)}) copy-start(f32[1,256]{1,0:T(1,128)} %param.28) | copy-start | bytes 3076
  (25 other events, 17.6 us)

commit v2 on v1

--- a/solution.py
+++ b/solution.py
@@ -17,7 +17,9 @@
 FACE_NODES = 121
 EDGE_ROWS = 16 * 12
 SIDE_ROWS = 192
-VMEM_LIMIT = 40 * 1024 * 1024
+VMEM_LIMIT = 24 * 1024 * 1024
+CORNER_FLOPS = 100_000_000_000
+VMEM_WHOLE = 60 * 1024 * 1024
 
 FACE_SLOTS = ((-1, 0, 0), (1, 0, 0), (0, -1, 0), (0, 1, 0), (0, 0, -1), (0, 0, 1))
 EDGE_SLOTS = (
@@ -155,12 +157,24 @@
     for q in range(FACE_NODES):
         expand[0, q, q // NODES] = 1.0
         expand[1, q, q % NODES] = 1.0
-    tables["rows_a"], tables["rows_b"] = f32(expand[0]), f32(expand[1])
     tables["cols_a"], tables["cols_b"] = f32(expand[0].T), f32(expand[1].T)
-    return tables
-
-
-TABLES = build_tables()
+    for name in ("top_z", "pick"):
+        wide = tables.pop(name)
+        tables[name + "_0"], tables[name + "_1"] = f32(wide[:, :128]), f32(wide[:, 128:])
+    rows, places, pieces = 0, {}, []
+    for name, value in tables.items():
+        count = -(-value.shape[0] // 16) * 16
+        places[name] = slice(rows, rows + value.shape[0])
+        pieces.append(np.pad(value, ((0, count - value.shape[0]), (0, 0))))
+        rows += count
+    return f32(np.concatenate(pieces, axis=0)), places
+
+
+TABLE, PLACE = build_tables()
+PIVOTS = TABLE.shape[0]
+CARRY = PIVOTS + LEVELS * 16
+BACK = CARRY + LEVELS * 16
+TABLE_ROWS = BACK + LAYERS * 16
 
 
 def lanes_of(shape):
@@ -240,14 +254,48 @@
     return block + pltpu.roll(top_b, station + 113, 1)
 
 
-def first_kernel(pos, face, edge, vert, fturn, eturn, stiff, xf, ef, xp, xm, zp, zm, cb):
-    block = coarse_block(vert, pos[0])
+def first_kernel(face_in, edge_in, vert_in, fturn_in, eturn_in, stiff_in,
+                 xf_out, ef_out, xp_out, xm_out, zp_out, zm_out, cb_out, turns_out, weights_out,
+                 xf, ef, xp, xm, zp, zm, cb, turns, weights,
+                 face, edge, vert, fturn, sems, out_sems):
+    copies = [
+        pltpu.make_async_copy(source, target, sems.at[at])
+        for at, (source, target) in enumerate((
+            (vert_in, vert),
+            (fturn_in, fturn),
+            (eturn_in, turns.at[16:40]),
+            (stiff_in, weights),
+            (face_in.at[0:1448], face.at[0:1448]),
+            (edge_in, edge),
+            (face_in.at[1448:2904], face.at[1448:2904]),
+        ))
+    ]
+    sent = []
+
+    def send(source, target):
+        copy = pltpu.make_async_copy(source, target, out_sems.at[len(sent)])
+        copy.start()
+        sent.append(copy)
+
+    for copy in copies:
+        copy.start()
+    copies[0].wait()
+    block = coarse_block(vert, lax.axis_index("gx"))
     for device in range(128):
         cb[device * 16 : device * 16 + 16, :] = block
+    send(cb, cb_out)
+    for copy in copies[1:]:
+        copy.wait()
+    for f in range(6):
+        turns[2 * f : 2 * f + 2, :] = fturn[f]
+    turns[12:16, :] = jnp.zeros((4, 128), jnp.int32)
+    send(turns, turns_out)
+    send(weights, weights_out)
+    stiff = weights
 
     last = NODES - 1
     for half in range(2):
-        turn = fturn[every(half, 6, 2), :]
+        turn = turns[every(half, 6, 2), :]
         swap, flip_a, flip_b = (turn & 4) != 0, (turn & 1) != 0, (turn & 2) != 0
         for s in range(2):
             source = s * 6 * 242 + half
@@ -261,7 +309,7 @@
                     xf[every(target + a * 11 + b, 6, 128), :] = x[a, b]
             for pad in range(121, 128):
                 xf[every(target + pad, 6, 128), :] = jnp.zeros((6, 128), F32)
-        mirror = eturn[every(half, 12, 2), :] != 0
+        mirror = turns[every(16 + half, 12, 2), :] != 0
         for s in range(2):
             source = s * 12 * 22 + half
             target = (half * 2 + s) * EDGE_ROWS
@@ -283,6 +331,10 @@
                     ref[base + 128 + place * 16 : base + 144 + place * 16, :] = ef[
                         (tile * 12 + e) * 16 : (tile * 12 + e + 1) * 16, :
                     ]
+    send(xp, xp_out)
+    send(xm, xm_out)
+    send(ef, ef_out)
+    send(xf, xf_out)
     for ref, half, slot, edges in ((zp, 1, 3, SENT_ZP), (zm, 0, 2, SENT_ZM)):
         own = 96 if half else 0
         group = lanes_of((128, 128)) // 32
@@ -300,6 +352,10 @@
         out = jnp.where(group == 0, faces[0], faces[1])
         out = jnp.where(group == 2, roll(lines, 64 - own), out)
         ref[...] = jnp.where(group == 3, weight, out)
+    send(zp, zp_out)
+    send(zm, zm_out)
+    for copy in sent:
+        copy.wait()
 
 
 def corner_kernel(zp, zm, rxm, rxp, out_p, out_m):
@@ -321,14 +377,32 @@
             out[r : r + 1, :] += jnp.where(lanes_of((1, 128)) >= 96, moved, 0.0)
 
 
-def parameter_kernel(heights, diag, basis, eigs, ext, modes, rows_a, rows_b, cols_a, cols_b,
-                     pivots, carry, back, lift, rdiag, work):
+def parameter_kernel(table_in, heights_in, diag_in, basis_in, eigs_in, ext_in,
+                     table, lift, rdiag, heights, diag, basis, eigs, ext, work, sems):
+    copies = [
+        pltpu.make_async_copy(source, target, sems.at[at])
+        for at, (source, target) in enumerate((
+            (heights_in, heights), (diag_in, diag), (basis_in, basis), (eigs_in, eigs),
+            (ext_in, ext), (table_in, table.at[0:PIVOTS]),
+        ))
+    ]
+    for copy in copies:
+        copy.start()
+    for copy in copies:
+        copy.wait()
+
     def dot(x, y):
         return jnp.dot(x, y, precision=HIGHEST, preferred_element_type=F32)
 
+    def dot_first(x, y):
+        return lax.dot_general(x, y, (((0,), (0,)), ((), ())), precision=HIGHEST,
+                               preferred_element_type=F32)
+
     b = basis[...]
-    kron = dot(dot(rows_a[...], b), cols_a[...]) * dot(dot(rows_b[...], b), cols_b[...])
-    scale = dot(eigs[...], cols_a[...] + cols_b[...])
+    cols_a, cols_b = table[PLACE["cols_a"], :], table[PLACE["cols_b"], :]
+    modes = table[PLACE["modes"], :]
+    kron = dot(dot_first(cols_a, b), cols_a) * dot(dot_first(cols_b, b), cols_b)
+    scale = dot(eigs[...], cols_a + cols_b)
     scale = 1.0 / jnp.where(lanes_of((1, 128)) < FACE_NODES, scale, 1.0)
     work[...] = jnp.zeros((256, 128), F32)
     work[0:128, :] = lax.dot_general(
@@ -345,11 +419,11 @@
     row = rows_of((16, 128))
     nodes = jnp.ones((16, 128), F32)
     for p in range(NODES):
-        nodes = jnp.where(row == p, diag[0, p], nodes)
+        nodes = jnp.where(row == p, diag[0:1, p : p + 1], nodes)
     rdiag[...] = 1.0 / nodes
 
-    wave = modes[...]
-    tall = [jnp.full((16, 128), heights[0, l], F32) for l in range(LAYERS)]
+    wave = modes
+    tall = [jnp.broadcast_to(heights[0:1, l : l + 1], (16, 128)) for l in range(LAYERS)]
     inverse = [1.0 / h for h in tall]
     prime = None
     for l in range(LEVELS):
@@ -363,30 +437,31 @@
         if l:
             pivot = pivot - inverse[l - 1] * prime
         rp = 1.0 / pivot
-        pivots[l * 16 : l * 16 + 16, :] = rp
+        table[PIVOTS + l * 16 : PIVOTS + l * 16 + 16, :] = rp
         if l:
-            carry[l * 16 : l * 16 + 16, :] = inverse[l - 1] * rp
+            table[CARRY + l * 16 : CARRY + l * 16 + 16, :] = inverse[l - 1] * rp
         else:
-            carry[0:16, :] = jnp.zeros((16, 128), F32)
+            table[CARRY : CARRY + 16, :] = jnp.zeros((16, 128), F32)
         if l < LAYERS:
             prime = inverse[l] * rp
-            back[l * 16 : l * 16 + 16, :] = prime
-
-
-def solve_kernel(pos, g, pivots, carry, back, forward, mix, top_z, top_x, back_z, back_x, pick,
-                 v_out, vb_out, tz, px, zs, vs, ss, cs):
+            table[BACK + l * 16 : BACK + l * 16 + 16, :] = prime
+
+
+def solve_kernel(g, table, v_out, v_hbm, vb_out, tz, px, zs, vs, ss, cs, sem):
     def dot(x, y):
         return jnp.dot(x, y, precision=HIGHEST, preferred_element_type=F32)
 
     stations = [g[x * 128 : x * 128 + 128, :] for x in range(NX)]
-    tz[...] = dot(forward[...], jnp.concatenate(stations, axis=1))
+    tz[...] = dot(table[PLACE["forward"], :], jnp.concatenate(stations, axis=1))
     total = g[0:128, :]
     for x in range(1, NX):
         total = total + g[x * 128 : x * 128 + 128, :]
-    tops = dot(total.T, top_z[...])
+    total = total.T
     low = rows_of((128, 128)) % 32 < 16
-    tops = jnp.where(low, tops[:, 0:128], tops[:, 128:256])
-    tops = dot(top_x[...], tops)
+    tops = jnp.where(low, dot(total, table[PLACE["top_z_0"], :]),
+                     dot(total, table[PLACE["top_z_1"], :]))
+    tops = dot(table[PLACE["top_x"], :], tops)
+    mix = PLACE["mix"].start
     top = jnp.where(lanes_of((16, 128)) < 64, tops[0:16], tops[16:32])
 
     bx0 = lanes_of((16, 128)) // 32 % 2 == 0
@@ -396,9 +471,9 @@
             pair = []
             for par in range(2):
                 k = kp * 2 + par
-                acc = t[0] * mix[k * NX : k * NX + 1, :]
+                acc = t[0] * table[mix + k * NX : mix + k * NX + 1, :]
                 for x in range(1, NX):
-                    acc = acc + t[x] * mix[k * NX + x : k * NX + x + 1, :]
+                    acc = acc + t[x] * table[mix + k * NX + x : mix + k * NX + x + 1, :]
                 pair.append(acc)
             even, odd = pair
             px[kp * 64 + m * 16 : kp * 64 + m * 16 + 16, :] = jnp.where(
@@ -412,20 +487,23 @@
     value = None
     for l in range(LEVELS):
         rhs = zs[every(l, 16, 32), :] if l < LAYERS else top
-        at = slice(l * 16, l * 16 + 16)
-        value = rhs * pivots[at, :] if l == 0 else rhs * pivots[at, :] + carry[at, :] * value
-        vs[at, :] = value
+        at = l * 16
+        step = rhs * table[PIVOTS + at : PIVOTS + at + 16, :]
+        value = step if l == 0 else step + table[CARRY + at : CARRY + at + 16, :] * value
+        vs[at : at + 16, :] = value
     ss[...] = jnp.zeros((1024, 128), F32)
     for l in range(LEVELS - 1, -1, -1):
         if l < LEVELS - 1:
-            at = slice(l * 16, l * 16 + 16)
-            value = vs[at, :] + back[at, :] * value
+            at = l * 16
+            value = vs[at : at + 16, :] + table[BACK + at : BACK + at + 16, :] * value
         ss[every(l, 16, 64), :] = value
 
-    hz = back_z[pl.ds(pl.multiple_of(pos[1] * 32, 32), 32), :]
+    at = PLACE["back_z"].start + lax.axis_index("gz") * 32
+    hz = table[pl.ds(pl.multiple_of(at, 16), 32), :]
     q = lax.dot_general(hz, ss[...], (((1,), (1,)), ((), ())), precision=HIGHEST,
                         preferred_element_type=F32)
-    hx = back_x[pl.ds(pl.multiple_of(pos[0] * 16, 16), 16), :]
+    at = PLACE["back_x"].start + lax.axis_index("gx") * 16
+    hx = table[pl.ds(pl.multiple_of(at, 16), 16), :]
     lane, row = lanes_of((16, 128)), rows_of((16, 128))
     group = lane // 32
     for s in range(2):
@@ -446,13 +524,16 @@
                     base = (((s * 2 + bx) * 2 + by) * 2 + bz) * 16
                     keep = (row - bz + 4) % 4 == group
                     cs[base : base + 16, :] = jnp.where(keep, mixed, 0.0)
-    picked = dot(pick[...], cs[...])
+    picked = dot(table[PLACE["pick_0"], :], cs[0:128, :]) + dot(table[PLACE["pick_1"], :], cs[128:256, :])
     v_out[...] = picked[0:32]
+    copy = pltpu.make_async_copy(v_out, v_hbm, sem)
+    copy.start()
     vb_out[...] = picked[32:224]
-
-
-def final_kernel(xf, ef, rxm, rxp, rzm, rzp, stiff, v, vb, lift, rdiag, fturn, eturn,
-                 face_out, edge_out, oq, ev):
+    copy.wait()
+
+
+def final_kernel(xf, ef, rxm, rxp, rzm, rzp, stiff, v, vb, lift, rdiag, turns,
+                 face_hbm, edge_hbm, oq, ev, face_out, edge_out, sems):
     last = NODES - 1
     w = [stiff[half : half + 1, :] for half in range(2)]
 
@@ -508,6 +589,7 @@
     high_t = (row16 + 1).astype(F32) / (NODES + 1.0)
     low_t = 1.0 - high_t
     diag = rdiag[...]
+    copies = []
 
     for s in range(2):
         e = {}
@@ -578,11 +660,9 @@
                 at = ((half * 2 + s) * 6 + f) * 128
                 oq[at : at + 128, :] = done[:, f * 128 : f * 128 + 128]
 
-    for half in range(2):
-        turn = fturn[every(half, 6, 2), :]
-        swap, flip_a, flip_b = (turn & 4) != 0, (turn & 1) != 0, (turn & 2) != 0
-        mirror = eturn[every(half, 12, 2), :] != 0
-        for s in range(2):
+        for half in range(2):
+            turn = turns[every(half, 6, 2), :]
+            swap, flip_a, flip_b = (turn & 4) != 0, (turn & 1) != 0, (turn & 2) != 0
             target = s * 6 * 242 + half
             source = (half * 2 + s) * 6 * 128
             for group in ORBITS:
@@ -592,27 +672,39 @@
                 x = {(a, b): jnp.where(swap, x[b, a], x[a, b]) for a, b in group}
                 for a, b in group:
                     face_out[every(target + 2 * (a * 11 + b), 6, 242), :] = x[a, b]
+            mirror = turns[every(16 + half, 12, 2), :] != 0
             target = s * 12 * 22 + half
             source = (half * 2 + s) * EDGE_ROWS
             x = [ev[every(source + p, 12, 16), :] for p in range(NODES)]
             for p in range(NODES):
                 edge_out[every(target + 2 * p, 12, 22), :] = jnp.where(mirror, x[last - p], x[p])
+        rows = (slice(0, 1448), slice(1448, 2904))[s]
+        copies.append(pltpu.make_async_copy(face_out.at[rows], face_hbm.at[rows], sems.at[2 * s]))
+        rows = slice(s * 264, s * 264 + 264)
+        copies.append(pltpu.make_async_copy(edge_out.at[rows], edge_hbm.at[rows], sems.at[2 * s + 1]))
+        for copy in copies[2 * s : 2 * s + 2]:
+            copy.start()
+    for copy in copies:
+        copy.wait()
 
 
 VMEM = pl.BlockSpec(memory_space=pltpu.VMEM)
-SMEM = pl.BlockSpec(memory_space=pltpu.SMEM)
-
-
-def call(kernel, outs, args, scalars=0, scratch=(), flops=0, name=None):
+HBM = pl.BlockSpec(memory_space=pltpu.HBM)
+
+
+def call(kernel, name, args, ins, outs, out_specs, scratch=(), sems=(), flops=0,
+         limit=VMEM_LIMIT):
     shapes = [jax.ShapeDtypeStruct(o, F32) if isinstance(o, tuple) else o for o in outs]
+    held = [pltpu.VMEM(o, F32) if isinstance(o, tuple) else o for o in scratch]
+    held += [pltpu.SemaphoreType.DMA(n) for n in sems]
     size = sum(int(np.prod(a.shape)) * 4 for a in args)
     return pl.pallas_call(
         kernel,
         out_shape=shapes,
-        in_specs=[SMEM] * scalars + [VMEM] * (len(args) - scalars),
-        out_specs=[VMEM] * len(shapes),
-        scratch_shapes=[pltpu.VMEM(o, F32) for o in scratch],
-        compiler_params=pltpu.CompilerParams(vmem_limit_bytes=VMEM_LIMIT),
+        in_specs=ins,
+        out_specs=out_specs,
+        scratch_shapes=held,
+        compiler_params=pltpu.CompilerParams(vmem_limit_bytes=limit),
         cost_estimate=pl.CostEstimate(flops=flops, bytes_accessed=size, transcendentals=0),
         name=name,
     )(*args)
@@ -620,49 +712,50 @@
 
 def per_device(face_residual, edge_residual, vertex_residual, face_orient, edge_orient, stiffness,
                face_basis, face_eigs, extension, edge_diag, element_heights):
-    table = {key: jnp.asarray(value) for key, value in TABLES.items()}
-    pos = jnp.stack([lax.axis_index("gx"), lax.axis_index("gz")]).astype(jnp.int32)
-    face = face_residual.reshape(2 * 6 * 121 * 2, 128)
-    edge = edge_residual.reshape(2 * 12 * 11 * 2, 128)
+    face = face_residual.reshape(2904, 128)
+    edge = edge_residual.reshape(528, 128)
     vert = vertex_residual.reshape(32, 128)
-    fturn = face_orient.reshape(12, 128)
+    fturn = face_orient.reshape(6, 2, 128)
     eturn = edge_orient.reshape(24, 128)
     stiff = stiffness.reshape(2, 128)
     tiles = 24 * 128
-    xf, ef, xp, xm, zp, zm, cb = call(
-        first_kernel,
-        [(tiles, 128), (4 * EDGE_ROWS, 128), (4 * SIDE_ROWS, 128), (4 * SIDE_ROWS, 128),
-         (128, 128), (128, 128), (2048, 128)],
-        (pos, face, edge, vert, fturn, eturn, stiff), scalars=1, name="frame")
+    kept = [(tiles, 128), (4 * EDGE_ROWS, 128), (4 * SIDE_ROWS, 128), (4 * SIDE_ROWS, 128),
+            (128, 128), (128, 128), (2048, 128), (40, 128), (2, 128)]
+    kinds = [F32] * 7 + [jnp.int32, F32]
+    xf, ef, xp, xm, zp, zm, cb, turns, weights = call(
+        first_kernel, "frame", (face, edge, vert, fturn, eturn, stiff), [HBM] * 6,
+        [jax.ShapeDtypeStruct(o, kind) for o, kind in zip(kept, kinds)], [HBM] * 9,
+        [pltpu.VMEM(o, kind) for o, kind in zip(kept, kinds)]
+        + [(2904, 128), (528, 128), (32, 128), pltpu.VMEM((6, 2, 128), jnp.int32)],
+        ((7,), (9,)), limit=VMEM_WHOLE)
     up = lambda n: [(i, (i + 1) % n) for i in range(n)]
     down = lambda n: [((i + 1) % n, i) for i in range(n)]
     rxm = lax.ppermute(xp, "gx", up(SPLIT_X))
     rxp = lax.ppermute(xm, "gx", down(SPLIT_X))
-    pivots, carry, back, lift, rdiag = call(
-        parameter_kernel,
-        [(LEVELS * 16, 128), (LEVELS * 16, 128), (LAYERS * 16, 128),
-         jax.ShapeDtypeStruct((256, 256), BF16), (16, 128)],
-        (element_heights.reshape(1, LAYERS), edge_diag.reshape(1, NODES), face_basis,
-         face_eigs.reshape(1, NODES), extension.T, table["modes"], table["rows_a"],
-         table["rows_b"], table["cols_a"], table["cols_b"]),
-        scalars=2, scratch=((256, 128),), name="parameters")
+    table, lift, rdiag = call(
+        parameter_kernel, "parameters",
+        (jnp.asarray(TABLE), element_heights.reshape(1, LAYERS), edge_diag.reshape(1, NODES),
+         face_basis, face_eigs.reshape(1, NODES), extension.T), [HBM] * 6,
+        [(TABLE_ROWS, 128), jax.ShapeDtypeStruct((256, 256), BF16), (16, 128)], [VMEM] * 3,
+        ((1, LAYERS), (1, NODES), (NODES, NODES), (1, NODES), (48, FACE_NODES), (256, 128)), ((6,),),
+        limit=VMEM_WHOLE)
     g = lax.all_to_all(cb.reshape(128, 16, 128), ("gx", "gz"), 0, 0).reshape(2048, 128)
-    zp, zm = call(corner_kernel, [(128, 128), (128, 128)], (zp, zm, rxm, rxp), name="corners")
+    zp, zm = call(corner_kernel, "corners", (zp, zm, rxm, rxp), [VMEM] * 4,
+                  [(128, 128), (128, 128)], [VMEM] * 2, flops=CORNER_FLOPS)
     rzm = lax.ppermute(zp, "gz", up(SPLIT_Z))
     rzp = lax.ppermute(zm, "gz", down(SPLIT_Z))
-    v, vb = call(
-        solve_kernel, [(32, 128), (192, 128)],
-        (pos, g, pivots, carry, back) + tuple(table[k] for k in (
-            "forward", "mix", "top_z", "top_x", "back_z", "back_x", "pick")),
-        scalars=1,
-        scratch=((64, 2048), (512, 128), (512, 128), (LEVELS * 16, 128), (1024, 128), (256, 128)),
-        flops=200_000_000, name="coarse")
+    v, v_out, vb = call(
+        solve_kernel, "coarse", (g, table), [VMEM] * 2, [(32, 128), (32, 128), (192, 128)],
+        [VMEM, HBM, VMEM],
+        ((64, 2048), (512, 128), (512, 128), (LEVELS * 16, 128), (1024, 128), (256, 128)), ((),),
+        flops=200_000_000)
     face_out, edge_out = call(
-        final_kernel, [(2904, 128), (528, 128)],
-        (xf, ef, rxm, rxp, rzm, rzp, stiff, v, vb, lift, rdiag, fturn, eturn),
-        scratch=((tiles, 128), (4 * EDGE_ROWS, 128)), name="finish")
+        final_kernel, "finish",
+        (xf, ef, rxm, rxp, rzm, rzp, weights, v, vb, lift, rdiag, turns), [VMEM] * 12,
+        [(2904, 128), (528, 128)], [HBM] * 2,
+        ((tiles, 128), (4 * EDGE_ROWS, 128), (2904, 128), (528, 128)), ((4,),))
     return (face_out.reshape(face_residual.shape), edge_out.reshape(edge_residual.shape),
-            v.reshape(vertex_residual.shape))
+            v_out.reshape(vertex_residual.shape))
 
 
 def solution(mesh):

time: 81.1 us -> 45 us (0.55)
  local copies, waits for them, and re-layouts: 29.9 us -> 1.46 us
  waiting for transfers between devices: 14.9 us -> 8.64 us
  Pallas kernels: 12.7 us -> 14.8 us
  starting transfers between devices: 20.8 us -> 18.7 us
    unnamed x88 -> x18, local copies, waits for them, and re-layouts: 29.9 us -> 1.46 us
    ppermute x1, waiting for transfers between devices: 14.9 us -> 0.01 us  [per_device(): rxm = lax.ppermute(xp, 'gx', up(SPLIT_X))]
    all_to_all x1, waiting for transfers between devices: 0.01 us -> 8.63 us  [per_device(): lax.all_to_all(cb.reshape(128, 16, 128), ('gx', 'gz'), 0, 0)]
    pallas_call x5, Pallas kernels: 12.7 us -> 14.8 us  [call(): pl.pallas_call(kernel, out_shape=shapes, in_specs=ins, out_specs=out_spec...]
    all_to_all x1, starting transfers between devices: 11.1 us -> 9.03 us  [per_device(): lax.all_to_all(cb.reshape(128, 16, 128), ('gx', 'gz'), 0, 0)]
  transfers between devices with their start and end apart: 5 -> 5, of which waited for: 1 -> 1; matrix products, arithmetic and copies ran while one was open for 0% -> 0% of each run, Pallas kernels for 8% -> 17%
where the time goes in v2:
time: 45 us; the launch traced here: 44.4 us
  starting transfers between devices  18.7 us (42%)
  Pallas kernels  14.8 us (33%)
  waiting for transfers between devices  8.64 us (19%)
  local copies, waits for them, and re-layouts  1.46 us (3%)
  between operations  0.79 us (2%)
    pallas_call x5, Pallas kernels, call(): pl.pallas_call(kernel, out_shape=shapes, in_specs=ins, out_specs=out_spec...  14.8 us
    all_to_all x1, starting transfers between devices, per_device(): lax.all_to_all(cb.reshape(128, 16, 128), ('gx', 'gz'), 0, 0)  9.03 us
    all_to_all x1, waiting for transfers between devices, per_device(): lax.all_to_all(cb.reshape(128, 16, 128), ('gx', 'gz'), 0, 0)  8.63 us
    ppermute x1, starting transfers between devices, per_device(): rxp = lax.ppermute(xm, 'gx', down(SPLIT_X))  3.84 us
    ppermute x1, starting transfers between devices, per_device(): rzp = lax.ppermute(zm, 'gz', down(SPLIT_Z))  3.17 us
    ppermute x1, starting transfers between devices, per_device(): rzm = lax.ppermute(zp, 'gz', up(SPLIT_Z))  2.54 us
    unnamed x18, local copies, waits for them, and re-layouts  1.46 us
  transfers between devices with their start and end apart: 5, of which 1 were waited for; matrix products, arithmetic and copies ran while one was open for 0% of the time, Pallas kernels for 17%

profile of v2, /device:TPU:0, one launch (start us, length us, event | category | flops | bytes accessed | tf_op | source)
XLA Modules:
  0.0 44.4 jit_solution(1614340723932456771)
XLA Ops:
  0.6 4.4 %frame.1 = (f32[3072,128]{1,0:T(8,128)}, f32[768,128]{1,0:T(8,128)}, f32[768,128]{1,0:T(8,128)}, f32[768,128]{1,0:T(8,128)}, f32[128,128]{1,0:T(8,128)}, /*index...) custom-call(f32[2904,128]{1,0:T(8,128)} %bitcast.16, f32[528,128]{1,0:T(8,128)} %bitcast.18, ...), custom_call_target="tpu_custom_call" | custom-call | bytes 1793024 | tf_op jit(solution)/shard_map/frame/pallas_call | solution.py:701
  5.1 0.0 copy-start.7
  5.1 0.0 copy-start.8
  5.1 0.1 collective-permute-start
  5.2 3.8 %collective-permute-start.1 = (f32[768,128]{1,0:T(8,128)}, f32[768,128]{1,0:T(8,128)S(1)}, u32[]{:S(2)}, u32[]{:S(2)}) collective-permute-start(f32[768,128]{1,0:T(8,128)} %get-tuple-element.25), channel_id=1, source_target_pairs={{8,0},{16,8},{24,16},{32,24},{40,32},{48,40},{56,48},{64,56},{72,6... | collective-permute-start | bytes 1179656 | tf_op jit(solution)/shard_map/ppermute | solution.py:734
  9.0 9.0 %all-to-all-start = ((f32[128,16,128]{2,1,0:T(8,128)}), f32[128,16,128]{2,1,0:T(8,128)S(1)}, u32[]{:S(2)}, u32[]{:S(2)}) async-start(f32[128,16,128]{2,1,0:T(8,128)} %bitcast.17), calls=%async_computation | async-start | bytes 2097152 | tf_op jit(solution)/shard_map/all_to_all | solution.py:742
  18.0 0.0 collective-permute-done.rxm
  18.0 0.0 collective-permute-done.1.rxp
  18.1 0.0 copy-done.7
  18.1 0.0 copy-done.8
  18.1 0.1 corners.1
  18.2 2.5 %collective-permute-start.2 = (f32[128,128]{1,0:T(8,128)S(1)}, f32[128,128]{1,0:T(8,128)S(1)}, u32[]{:S(2)}, u32[]{:S(2)}) collective-permute-start(f32[128,128]{1,0:T(8,128)S(1)} %get-tuple-element.28), channel_id=1, source_target_pairs={{0,1},{1,2},{2,3},{3,4},{4,5},{5,6},{6,7},{7,0},{8,9},{9,10},{10,1... | collective-permute-start | bytes 196616 | tf_op jit(solution)/shard_map/ppermute | solution.py:745
  20.7 3.2 %collective-permute-start.3 = (f32[128,128]{1,0:T(8,128)S(1)}, f32[128,128]{1,0:T(8,128)S(1)}, u32[]{:S(2)}, u32[]{:S(2)}) collective-permute-start(f32[128,128]{1,0:T(8,128)S(1)} %get-tuple-element.29), channel_id=1, source_target_pairs={{1,0},{2,1},{3,2},{4,3},{5,4},{6,5},{7,6},{0,7},{9,8},{10,9},{11,1... | collective-permute-start | bytes 196616 | tf_op jit(solution)/shard_map/ppermute | solution.py:746
  23.9 3.5 %parameters.1 = (f32[3184,128]{1,0:T(8,128)}, bf16[256,256]{1,0:T(8,128)(2,1)}, f32[16,128]{1,0:T(8,128)}) custom-call(f32[1616,128]{1,0:T(8,128)} %constant.2.clone.table_in, f32[1,32]{1,0:T(1,128)} %bitcast.24, f32[1,11]{1,0:T(1,128)} %bitcast.25, f32[11,11]{1,0:T(8,128)} %basis_in.1, f32[1,11]{1,0:T(1,128)} %bitcast.26, f32[48,121]{1,0:T(8,128)} %bitcast.19), custom_call_target="tpu_custom_call" | custom-call | bytes 851324 | tf_op jit(solution)/shard_map/parameters/pallas_call | solution.py:701
  27.4 8.6 %all-to-all-done = f32[128,16,128]{2,1,0:T(8,128)S(1)} async-done(((f32[128,16,128]{2,1,0:T(8,128)}), f32[128,16,128]{2,1,0:T(8,128)S(1)}, u32[]{:S(2)}, u32[]{:S(2)}) %all-to-all-start) | async-done | bytes 1048608 | tf_op jit(solution)/shard_map/all_to_all | solution.py:742
  36.1 1.4 %copy-done = f32[3184,128]{1,0:T(8,128)S(1)} copy-done((f32[3184,128]{1,0:T(8,128)S(1)}, f32[3184,128]{1,0:T(8,128)}, u32[]{:S(2)}) %copy-start) | copy-done | bytes 1630232
  37.5 3.7 %coarse.1 = (f32[32,128]{1,0:T(8,128)S(1)}, f32[32,128]{1,0:T(8,128)}, f32[192,128]{1,0:T(8,128)S(1)}) custom-call(f32[2048,128]{1,0:T(8,128)S(1)} %bitcast.15, f32[3184,128]{1,0:T(8,128)S(1)} %copy-done), custom_call_target="tpu_custom_call" | custom-call | flops 200000000 | bytes 2678784 | tf_op jit(solution)/shard_map/coarse/pallas_call | solution.py:701
  41.2 0.0 collective-permute-done.2.rzm
  41.2 0.0 collective-permute-done.3.rzp
  41.2 0.0 copy-done.2
  41.2 0.0 copy-done.4
  41.3 0.0 copy-done.6
  41.3 0.0 copy-done.1
  41.3 3.1 %finish.1 = (f32[2904,128]{1,0:T(8,128)}, f32[528,128]{1,0:T(8,128)}) custom-call(f32[3072,128]{1,0:T(8,128)S(1)} %copy-done.1, f32[768,128]{1,0:T(8,128)S(1)} %copy-done.2, f32[768,128]{1,0:T(8,128)S(1)} %collective-permute-done.rxm, f32[768,128]{1,0:T(8,128)S(1)} %collective-permute-done.1.rxp, f32[128,128]{1,0:T(8,128)S(1)} %collective-permute-done.2.rzm, ...), custom_call_target="tpu_custom_call" | custom-call | bytes 3290112 | tf_op jit(solution)/shard_map/finish/pallas_call | solution.py:701
  (9 shorter events, 0.0 us)
Async XLA Ops:
  5.1 13.0 %copy-start.7 = (f32[128,128]{1,0:T(8,128)S(1)}, f32[128,128]{1,0:T(8,128)}, u32[]{:S(2)}) copy-start(f32[128,128]{1,0:T(8,128)} %get-tuple-element.26.zp) | copy-start | bytes 196612
  5.1 13.0 %copy-start.8 = (f32[128,128]{1,0:T(8,128)S(1)}, f32[128,128]{1,0:T(8,128)}, u32[]{:S(2)}) copy-start(f32[128,128]{1,0:T(8,128)} %get-tuple-element.27.zm) | copy-start | bytes 196612
  5.1 13.0 %collective-permute-start = (f32[768,128]{1,0:T(8,128)}, f32[768,128]{1,0:T(8,128)S(1)}, u32[]{:S(2)}, u32[]{:S(2)}) collective-permute-start(f32[768,128]{1,0:T(8,128)} %get-tuple-element.24), channel_id=1, source_target_pairs={{0,8},{8,16},{16,24},{24,32},{32,40},{40,48},{48,56},{56,64},{64,7... | collective-permute-start | bytes 1179656 | tf_op jit(solution)/shard_map/ppermute | solution.py:733
  5.2 12.9 %collective-permute-start.1 = (f32[768,128]{1,0:T(8,128)}, f32[768,128]{1,0:T(8,128)S(1)}, u32[]{:S(2)}, u32[]{:S(2)}) collective-permute-start(f32[768,128]{1,0:T(8,128)} %get-tuple-element.25), channel_id=1, source_target_pairs={{8,0},{16,8},{24,16},{32,24},{40,32},{48,40},{56,48},{64,56},{72,6... | collective-permute-start | bytes 1179656 | tf_op jit(solution)/shard_map/ppermute | solution.py:734
  9.0 27.1 %all-to-all-start = ((f32[128,16,128]{2,1,0:T(8,128)}), f32[128,16,128]{2,1,0:T(8,128)S(1)}, u32[]{:S(2)}, u32[]{:S(2)}) async-start(f32[128,16,128]{2,1,0:T(8,128)} %bitcast.17), calls=%async_computation | async-start | bytes 2097152 | tf_op jit(solution)/shard_map/all_to_all | solution.py:742
  18.2 23.0 %collective-permute-start.2 = (f32[128,128]{1,0:T(8,128)S(1)}, f32[128,128]{1,0:T(8,128)S(1)}, u32[]{:S(2)}, u32[]{:S(2)}) collective-permute-start(f32[128,128]{1,0:T(8,128)S(1)} %get-tuple-element.28), channel_id=1, source_target_pairs={{0,1},{1,2},{2,3},{3,4},{4,5},{5,6},{6,7},{7,0},{8,9},{9,10},{10,1... | collective-permute-start | bytes 196616 | tf_op jit(solution)/shard_map/ppermute | solution.py:745
  20.7 20.5 %collective-permute-start.3 = (f32[128,128]{1,0:T(8,128)S(1)}, f32[128,128]{1,0:T(8,128)S(1)}, u32[]{:S(2)}, u32[]{:S(2)}) collective-permute-start(f32[128,128]{1,0:T(8,128)S(1)} %get-tuple-element.29), channel_id=1, source_target_pairs={{1,0},{2,1},{3,2},{4,3},{5,4},{6,5},{7,6},{0,7},{9,8},{10,9},{11,1... | collective-permute-start | bytes 196616 | tf_op jit(solution)/shard_map/ppermute | solution.py:746
  23.9 17.4 %copy-start.2 = (f32[768,128]{1,0:T(8,128)S(1)}, f32[768,128]{1,0:T(8,128)}, u32[]{:S(2)}) copy-start(f32[768,128]{1,0:T(8,128)} %get-tuple-element.23.ef) | copy-start | bytes 1179652
  23.9 17.4 %copy-start.4 = (s32[40,128]{1,0:T(8,128)S(1)}, s32[40,128]{1,0:T(8,128)}, u32[]{:S(2)}) copy-start(s32[40,128]{1,0:T(8,128)} %get-tuple-element.37.turns) | copy-start | bytes 61444
  23.9 17.4 %copy-start.6 = (f32[2,128]{1,0:T(2,128)S(1)}, f32[2,128]{1,0:T(2,128)}, u32[]{:S(2)}) copy-start(f32[2,128]{1,0:T(2,128)} %get-tuple-element.30.stiff) | copy-start | bytes 3076
  36.1 1.4 %copy-start = (f32[3184,128]{1,0:T(8,128)S(1)}, f32[3184,128]{1,0:T(8,128)}, u32[]{:S(2)}) copy-start(f32[3184,128]{1,0:T(8,128)} %get-tuple-element.32.table) | copy-start | bytes 4890628
  37.5 3.8 %copy-start.1 = (f32[3072,128]{1,0:T(8,128)S(1)}, f32[3072,128]{1,0:T(8,128)}, u32[]{:S(2)}) copy-start(f32[3072,128]{1,0:T(8,128)} %get-tuple-element.22.xf) | copy-start | bytes 4718596
  37.5 3.8 %copy-start.3 = (bf16[256,256]{1,0:T(8,128)(2,1)S(1)}, bf16[256,256]{1,0:T(8,128)(2,1)}, u32[]{:S(2)}) copy-start(bf16[256,256]{1,0:T(8,128)(2,1)} %get-tuple-element.35.lift) | copy-start | bytes 393220
  37.5 3.8 %copy-start.5 = (f32[16,128]{1,0:T(8,128)S(1)}, f32[16,128]{1,0:T(8,128)}, u32[]{:S(2)}) copy-start(f32[16,128]{1,0:T(8,128)} %get-tuple-element.36.rdiag) | copy-start | bytes 24580

commit v3 on v2

--- a/solution.py
+++ b/solution.py
@@ -17,6 +17,8 @@
 FACE_NODES = 121
 EDGE_ROWS = 16 * 12
 SIDE_ROWS = 192
+SENT = 12
+STATION = SENT * SPLIT_Z
 VMEM_LIMIT = 24 * 1024 * 1024
 CORNER_FLOPS = 100_000_000_000
 VMEM_WHOLE = 60 * 1024 * 1024
@@ -95,17 +97,14 @@
     f32 = lambda a: np.ascontiguousarray(a, dtype=np.float32)
     tables = {}
     forward = np.zeros((NZ, 128))
-    top_a, top_b = np.zeros((128, NZ)), np.zeros((128, NZ))
+    top_z = np.zeros((3, 128, 2 * NZ))
     for gz in range(SPLIT_Z):
         for kk in range(9):
             column = HZ[:, (8 * gz + kk) % NZ]
-            forward[:, gz * 16 + kk] = column
-            if kk < 7:
-                top_a[gz * 16 + 9 + kk] = column
-            else:
-                top_b[gz * 16 + 2 + kk] = column
+            forward[:, gz * SENT + kk] = column
+            top_z[kk // 3, gz * SENT + 9 + kk % 3] = np.tile(column, 2)
     tables["forward"] = f32(forward)
-    tables["top_z"] = f32(np.concatenate([top_a, top_a, top_b, top_b], axis=1))
+    tables["top_z"] = f32(top_z.reshape(3 * 128, 128))
     lane = np.arange(128)
     lane_s, lane_bx, lane_j = lane // 64, lane // 32 % 2, lane % 32
     mix = np.zeros((NX * NX, 128))
@@ -113,7 +112,7 @@
         for x in range(NX):
             mix[k * NX + x] = HX[k, (x + lane_bx) % NX]
     tables["mix"] = f32(mix)
-    top_x = np.zeros((2, 16, 128))
+    top_x = np.zeros((2, 2, 16, 128))
     modes = np.zeros((16, 128))
     waves_x = 2.0 - 2.0 * np.cos(2.0 * np.pi / NX * np.arange(NX))
     waves_z = 2.0 - 2.0 * np.cos(2.0 * np.pi / NZ * np.arange(NZ))
@@ -121,9 +120,11 @@
         s, blk, par = row // 8, row // 2 % 4, row % 2
         for pair in range(2):
             k = blk * 4 + pair * 2 + par
-            top_x[pair, row] = np.where(lane_s == s, HX[k, (lane_j % 16 + lane_bx) % NX], 0.0)
+            for odd in range(2):
+                x = 2 * (lane_j % 8) + odd
+                top_x[odd, pair, row] = np.where(lane_s == s, HX[k, (x + lane_bx) % NX], 0.0)
             modes[row, pair * 64 : pair * 64 + 64] = waves_x[k] + waves_z + SHIFT_MASS
-    tables["top_x"] = f32(top_x.reshape(32, 128))
+    tables["top_x"] = f32(top_x.reshape(64, 128))
     tables["modes"] = f32(modes)
     back_z = np.zeros((SPLIT_Z, 2, 16, 2, NZ))
     for gz in range(SPLIT_Z):
@@ -158,7 +159,7 @@
         expand[0, q, q // NODES] = 1.0
         expand[1, q, q % NODES] = 1.0
     tables["cols_a"], tables["cols_b"] = f32(expand[0].T), f32(expand[1].T)
-    for name in ("top_z", "pick"):
+    for name in ("pick",):
         wide = tables.pop(name)
         tables[name + "_0"], tables[name + "_1"] = f32(wide[:, :128]), f32(wide[:, 128:])
     rows, places, pieces = 0, {}, []
@@ -248,10 +249,11 @@
     top = turned(high)
     block = spread(main, row, row < 9)
     last = lane % 32 == 31
-    top_a = jnp.where(last, spread(top, row - 9, row >= 9), 0.0)
-    top_b = jnp.where(last, spread(top, row - 2, (row >= 9) & (row < 11)), 0.0)
-    block = block + pltpu.roll(top_a, station + 97, 1)
-    return block + pltpu.roll(top_b, station + 113, 1)
+    for third in range(3):
+        moved = spread(top, row - 9 + 3 * third, (row >= 9) & (row < SENT))
+        moved = jnp.where(last, moved, 0.0)
+        block = block + pltpu.roll(moved, station // 2 + 8 * third + 97, 1)
+    return block
 
 
 def first_kernel(face_in, edge_in, vert_in, fturn_in, eturn_in, stiff_in,
@@ -282,7 +284,7 @@
     copies[0].wait()
     block = coarse_block(vert, lax.axis_index("gx"))
     for device in range(128):
-        cb[device * 16 : device * 16 + 16, :] = block
+        cb[device * SENT : device * SENT + SENT, :] = block[0:SENT]
     send(cb, cb_out)
     for copy in copies[1:]:
         copy.wait()
@@ -451,16 +453,20 @@
     def dot(x, y):
         return jnp.dot(x, y, precision=HIGHEST, preferred_element_type=F32)
 
-    stations = [g[x * 128 : x * 128 + 128, :] for x in range(NX)]
-    tz[...] = dot(table[PLACE["forward"], :], jnp.concatenate(stations, axis=1))
-    total = g[0:128, :]
-    for x in range(1, NX):
-        total = total + g[x * 128 : x * 128 + 128, :]
-    total = total.T
-    low = rows_of((128, 128)) % 32 < 16
-    tops = jnp.where(low, dot(total, table[PLACE["top_z_0"], :]),
-                     dot(total, table[PLACE["top_z_1"], :]))
-    tops = dot(table[PLACE["top_x"], :], tops)
+    stations = [g[x * STATION : x * STATION + STATION, :] for x in range(NX)]
+    tz[...] = dot(table[PLACE["forward"], 0:STATION], jnp.concatenate(stations, axis=1))
+    third = rows_of((128, 128)) % 32 // 8
+    base_z, base_x = PLACE["top_z"].start, PLACE["top_x"].start
+    tops = None
+    for odd in range(2):
+        total = stations[odd]
+        for x in range(odd + 2, NX, 2):
+            total = total + stations[x]
+        total = jnp.concatenate([total, jnp.zeros((128 - STATION, 128), F32)], axis=0).T
+        parts = [dot(total, table[base_z + 128 * q : base_z + 128 * q + 128, :]) for q in range(3)]
+        part = jnp.where(third == 0, parts[0], jnp.where(third == 1, parts[1], parts[2]))
+        part = dot(table[base_x + 32 * odd : base_x + 32 * odd + 32, :], part)
+        tops = part if tops is None else tops + part
     mix = PLACE["mix"].start
     top = jnp.where(lanes_of((16, 128)) < 64, tops[0:16], tops[16:32])
 
@@ -720,7 +726,7 @@
     stiff = stiffness.reshape(2, 128)
     tiles = 24 * 128
     kept = [(tiles, 128), (4 * EDGE_ROWS, 128), (4 * SIDE_ROWS, 128), (4 * SIDE_ROWS, 128),
-            (128, 128), (128, 128), (2048, 128), (40, 128), (2, 128)]
+            (128, 128), (128, 128), (128 * SENT, 128), (40, 128), (2, 128)]
     kinds = [F32] * 7 + [jnp.int32, F32]
     xf, ef, xp, xm, zp, zm, cb, turns, weights = call(
         first_kernel, "frame", (face, edge, vert, fturn, eturn, stiff), [HBM] * 6,
@@ -737,9 +743,9 @@
         (jnp.asarray(TABLE), element_heights.reshape(1, LAYERS), edge_diag.reshape(1, NODES),
          face_basis, face_eigs.reshape(1, NODES), extension.T), [HBM] * 6,
         [(TABLE_ROWS, 128), jax.ShapeDtypeStruct((256, 256), BF16), (16, 128)], [VMEM] * 3,
-        ((1, LAYERS), (1, NODES), (NODES, NODES), (1, NODES), (48, FACE_NODES), (256, 128)), ((6,),),
-        limit=VMEM_WHOLE)
-    g = lax.all_to_all(cb.reshape(128, 16, 128), ("gx", "gz"), 0, 0).reshape(2048, 128)
+        ((1, LAYERS), (1, NODES), (NODES, NODES), (1, NODES), (48, FACE_NODES), (256, 128)), ((6,),))
+    g = lax.all_to_all(cb.reshape(128, 3, 4, 128), ("gx", "gz"), 0, 0)
+    g = g.reshape(128 * SENT, 128)
     zp, zm = call(corner_kernel, "corners", (zp, zm, rxm, rxp), [VMEM] * 4,
                   [(128, 128), (128, 128)], [VMEM] * 2, flops=CORNER_FLOPS)
     rzm = lax.ppermute(zp, "gz", up(SPLIT_Z))

time: 45 us -> 41 us (0.911)
  local copies, waits for them, and re-layouts: 1.46 us -> 0.07 us
  Pallas kernels: 14.8 us -> 13.5 us
  waiting for transfers between devices: 8.64 us -> 7.7 us
    unnamed x18 -> x28, local copies, waits for them, and re-layouts: 1.46 us -> 0.07 us
    pallas_call x5, Pallas kernels: 14.8 us -> 13.5 us  [call(): pl.pallas_call(kernel, out_shape=shapes, in_specs=ins, out_specs=out_spec...]
    all_to_all x1, waiting for transfers between devices: 8.63 us -> 7.69 us  [per_device(): g = lax.all_to_all(cb.reshape(128, 3, 4, 128), ('gx', 'gz'), 0, 0)]
  transfers between devices with their start and end apart: 5 -> 5, of which waited for: 1 -> 1; matrix products, arithmetic and copies ran while one was open for 0% -> 0% of each run, Pallas kernels for 17% -> 15%
where the time goes in v3:
time: 41 us; the launch traced here: 40.8 us
  starting transfers between devices  18.6 us (45%)
  Pallas kernels  13.5 us (33%)
  waiting for transfers between devices  7.7 us (19%)
  between operations  0.87 us (2%)
    pallas_call x5, Pallas kernels, call(): pl.pallas_call(kernel, out_shape=shapes, in_specs=ins, out_specs=out_spec...  13.5 us
    all_to_all x1, starting transfers between devices, per_device(): g = lax.all_to_all(cb.reshape(128, 3, 4, 128), ('gx', 'gz'), 0, 0)  9.03 us
    all_to_all x1, waiting for transfers between devices, per_device(): g = lax.all_to_all(cb.reshape(128, 3, 4, 128), ('gx', 'gz'), 0, 0)  7.69 us
    ppermute x1, starting transfers between devices, per_device(): rxp = lax.ppermute(xm, 'gx', down(SPLIT_X))  3.84 us
    ppermute x1, starting transfers between devices, per_device(): rzp = lax.ppermute(zm, 'gz', down(SPLIT_Z))  3.17 us
    ppermute x1, starting transfers between devices, per_device(): rzm = lax.ppermute(zp, 'gz', up(SPLIT_Z))  2.47 us
  transfers between devices with their start and end apart: 5, of which 1 were waited for; matrix products, arithmetic and copies ran while one was open for 0% of the time, Pallas kernels for 15%

profile of v3, /device:TPU:0, one launch (start us, length us, event | category | flops | bytes accessed | tf_op | source)
XLA Modules:
  0.0 40.8 jit_solution(12487538228259904288)
XLA Ops:
  0.6 4.4 %frame.1 = (f32[3072,128]{1,0:T(8,128)}, f32[768,128]{1,0:T(8,128)}, f32[768,128]{1,0:T(8,128)}, f32[768,128]{1,0:T(8,128)}, f32[128,128]{1,0:T(8,128)}, /*index...) custom-call(f32[2904,128]{1,0:T(8,128)} %bitcast.20, f32[528,128]{1,0:T(8,128)} %bitcast.22, ...), custom_call_target="tpu_custom_call" | custom-call | bytes 1793024 | tf_op jit(solution)/shard_map/frame/pallas_call | solution.py:707
  5.1 0.0 copy-start.12
  5.1 0.0 copy-start.13
  5.1 0.1 collective-permute-start
  5.2 3.8 %collective-permute-start.1 = (f32[768,128]{1,0:T(8,128)}, f32[768,128]{1,0:T(8,128)S(1)}, u32[]{:S(2)}, u32[]{:S(2)}) collective-permute-start(f32[768,128]{1,0:T(8,128)} %get-tuple-element.25), channel_id=1, source_target_pairs={{8,0},{16,8},{24,16},{32,24},{40,32},{48,40},{56,48},{64,56},{72,6... | collective-permute-start | bytes 1179656 | tf_op jit(solution)/shard_map/ppermute | solution.py:740
  9.0 9.0 %all-to-all-start = ((f32[128,3,4,128]{3,2,1,0:T(4,128)}), f32[128,3,4,128]{3,2,1,0:T(4,128)S(1)}, u32[]{:S(2)}, u32[]{:S(2)}) async-start(f32[128,3,4,128]{3,2,1,0:T(4,128)} %bitcast.21), calls=%async_computation | async-start | bytes 1572864 | tf_op jit(solution)/shard_map/all_to_all | solution.py:747
  18.0 0.0 collective-permute-done.rxm
  18.1 0.0 collective-permute-done.1.rxp
  18.1 0.0 copy-start.1
  18.1 0.0 copy-start.5
  18.1 0.0 copy-start.7
  18.1 0.0 copy-start.9
  18.1 0.0 copy-start.10
  18.2 0.0 copy-start.11
  18.2 0.7 %corners.1 = (f32[128,128]{1,0:T(8,128)}, f32[128,128]{1,0:T(8,128)}) custom-call(f32[128,128]{1,0:T(8,128)S(1)} %copy-done.12, f32[128,128]{1,0:T(8,128)S(1)} %copy-done.13, f32[768,128]{1,0:T(8,128)S(1)} %collective-permute-done.rxm, f32[768,128]{1,0:T(8,128)S(1)} %collective-permute-done.1.rxp), custom_call_target="tpu_custom_call" | custom-call | flops 99999997952 | bytes 917504 | tf_op jit(solution)/shard_map/corners/pallas_call | solution.py:707
  18.9 2.5 %collective-permute-start.2 = (f32[128,128]{1,0:T(8,128)}, f32[128,128]{1,0:T(8,128)S(1)}, u32[]{:S(2)}, u32[]{:S(2)}) collective-permute-start(f32[128,128]{1,0:T(8,128)} %get-tuple-element.28), channel_id=1, source_target_pairs={{0,1},{1,2},{2,3},{3,4},{4,5},{5,6},{6,7},{7,0},{8,9},{9,10},{10,1... | collective-permute-start | bytes 196616 | tf_op jit(solution)/shard_map/ppermute | solution.py:751
  21.4 3.2 %collective-permute-start.3 = (f32[128,128]{1,0:T(8,128)}, f32[128,128]{1,0:T(8,128)S(1)}, u32[]{:S(2)}, u32[]{:S(2)}) collective-permute-start(f32[128,128]{1,0:T(8,128)} %get-tuple-element.29), channel_id=1, source_target_pairs={{1,0},{2,1},{3,2},{4,3},{5,4},{6,5},{7,6},{0,7},{9,8},{10,9},{11,1... | collective-permute-start | bytes 196616 | tf_op jit(solution)/shard_map/ppermute | solution.py:752
  24.5 0.0 copy-done.5
  24.6 1.4 %parameters.1 = (f32[3344,128]{1,0:T(8,128)S(1)}, bf16[256,256]{1,0:T(8,128)(2,1)S(1)}, f32[16,128]{1,0:T(8,128)S(1)}) custom-call(f32[1776,128]{1,0:T(8,128)S(1)} %copy-done.1, f32[1,32]{1,0:T(1,128)S(1)} %bitcast.17, f32[1,11]{1,0:T(1,128)S(1)} %bitcast.18, f32[11,11]{1,0:T(8,128)S(1)} %copy-done.7, f32[1,11]{1,0:T(1,128)S(1)} %bitcast.19, ...), custom_call_target="tpu_custom_call" | custom-call | bytes 933244 | tf_op jit(solution)/shard_map/parameters/pallas_call | solution.py:707
  26.0 7.7 %all-to-all-done = f32[128,3,4,128]{3,2,1,0:T(4,128)S(1)} async-done(((f32[128,3,4,128]{3,2,1,0:T(4,128)}), f32[128,3,4,128]{3,2,1,0:T(4,128)S(1)}, u32[]{:S(2)}, u32[]{:S(2)}) %all-to-all-start) | async-done | bytes 786464 | tf_op jit(solution)/shard_map/all_to_all | solution.py:747
  33.7 3.9 %coarse.1 = (f32[32,128]{1,0:T(8,128)S(1)}, f32[32,128]{1,0:T(8,128)}, f32[192,128]{1,0:T(8,128)S(1)}) custom-call(f32[1536,128]{1,0:T(8,128)S(1)} %bitcast.15, f32[3344,128]{1,0:T(8,128)S(1)} %get-tuple-element.32.table), custom_call_target="tpu_custom_call" | custom-call | flops 200000000 | bytes 2498560 | tf_op jit(solution)/shard_map/coarse/pallas_call | solution.py:707
  37.6 0.0 collective-permute-done.2.rzm
  37.6 0.0 collective-permute-done.3.rzp
  37.7 3.1 %finish.1 = (f32[2904,128]{1,0:T(8,128)}, f32[528,128]{1,0:T(8,128)}) custom-call(f32[3072,128]{1,0:T(8,128)S(1)} %copy-done, f32[768,128]{1,0:T(8,128)S(1)} %copy-done.2, f32[768,128]{1,0:T(8,128)S(1)} %collective-permute-done.rxm, f32[768,128]{1,0:T(8,128)S(1)} %copy-done.4, f32[128,128]{1,0:T(8,128)S(1)} %collective-permute-done.2.rzm, ...), custom_call_target="tpu_custom_call" | custom-call | bytes 3290112 | tf_op jit(solution)/shard_map/finish/pallas_call | solution.py:707
  (19 shorter events, 0.0 us)
Async XLA Ops:
  5.1 13.0 %copy-start.12 = (f32[128,128]{1,0:T(8,128)S(1)}, f32[128,128]{1,0:T(8,128)}, u32[]{:S(2)}) copy-start(f32[128,128]{1,0:T(8,128)} %get-tuple-element.26.zp) | copy-start | bytes 196612
  5.1 13.0 %copy-start.13 = (f32[128,128]{1,0:T(8,128)S(1)}, f32[128,128]{1,0:T(8,128)}, u32[]{:S(2)}) copy-start(f32[128,128]{1,0:T(8,128)} %get-tuple-element.27.zm) | copy-start | bytes 196612
  5.1 13.0 %collective-permute-start = (f32[768,128]{1,0:T(8,128)}, f32[768,128]{1,0:T(8,128)S(1)}, u32[]{:S(2)}, u32[]{:S(2)}) collective-permute-start(f32[768,128]{1,0:T(8,128)} %get-tuple-element.24), channel_id=1, source_target_pairs={{0,8},{8,16},{16,24},{24,32},{32,40},{40,48},{48,56},{56,64},{64,7... | collective-permute-start | bytes 1179656 | tf_op jit(solution)/shard_map/ppermute | solution.py:739
  5.2 12.9 %collective-permute-start.1 = (f32[768,128]{1,0:T(8,128)}, f32[768,128]{1,0:T(8,128)S(1)}, u32[]{:S(2)}, u32[]{:S(2)}) collective-permute-start(f32[768,128]{1,0:T(8,128)} %get-tuple-element.25), channel_id=1, source_target_pairs={{8,0},{16,8},{24,16},{32,24},{40,32},{48,40},{56,48},{64,56},{72,6... | collective-permute-start | bytes 1179656 | tf_op jit(solution)/shard_map/ppermute | solution.py:740
  9.0 24.7 %all-to-all-start = ((f32[128,3,4,128]{3,2,1,0:T(4,128)}), f32[128,3,4,128]{3,2,1,0:T(4,128)S(1)}, u32[]{:S(2)}, u32[]{:S(2)}) async-start(f32[128,3,4,128]{3,2,1,0:T(4,128)} %bitcast.21), calls=%async_computation | async-start | bytes 1572864 | tf_op jit(solution)/shard_map/all_to_all | solution.py:747
  18.1 0.8 %copy-start.3 = (f32[768,128]{1,0:T(8,128)}, f32[768,128]{1,0:T(8,128)S(1)}, u32[]{:S(2)}) copy-start(f32[768,128]{1,0:T(8,128)S(1)} %collective-permute-done.1.rxp) | copy-start | bytes 1179652
  18.1 6.4 %copy-start.1 = (f32[1776,128]{1,0:T(8,128)S(1)}, f32[1776,128]{1,0:T(8,128)}, u32[]{:S(2)}) copy-start(f32[1776,128]{1,0:T(8,128)} %constant.2.clone.table_in) | copy-start | bytes 2727940
  18.1 6.4 %copy-start.5 = (f32[121,48]{0,1:T(8,128)S(1)}, f32[121,48]{0,1:T(8,128)}, u32[]{:S(2)}) copy-start(f32[121,48]{0,1:T(8,128)} %param.20) | copy-start | bytes 69700
  18.1 6.4 %copy-start.7 = (f32[11,11]{1,0:T(8,128)S(1)}, f32[11,11]{1,0:T(8,128)}, u32[]{:S(2)}) copy-start(f32[11,11]{1,0:T(8,128)} %basis_in.1) | copy-start | bytes 1456
  18.1 6.4 %copy-start.9 = (f32[32]{0:T(128)S(1)}, f32[32]{0:T(128)}, u32[]{:S(2)}) copy-start(f32[32]{0:T(128)} %param.22) | copy-start | bytes 388
  18.1 6.4 %copy-start.10 = (f32[11]{0:T(128)S(1)}, f32[11]{0:T(128)}, u32[]{:S(2)}) copy-start(f32[11]{0:T(128)} %param.21) | copy-start | bytes 136
  18.2 6.4 %copy-start.11 = (f32[11]{0:T(128)S(1)}, f32[11]{0:T(128)}, u32[]{:S(2)}) copy-start(f32[11]{0:T(128)} %param.19) | copy-start | bytes 136
  18.9 18.7 %collective-permute-start.2 = (f32[128,128]{1,0:T(8,128)}, f32[128,128]{1,0:T(8,128)S(1)}, u32[]{:S(2)}, u32[]{:S(2)}) collective-permute-start(f32[128,128]{1,0:T(8,128)} %get-tuple-element.28), channel_id=1, source_target_pairs={{0,1},{1,2},{2,3},{3,4},{4,5},{5,6},{6,7},{7,0},{8,9},{9,10},{10,1... | collective-permute-start | bytes 196616 | tf_op jit(solution)/shard_map/ppermute | solution.py:751
  21.4 16.2 %collective-permute-start.3 = (f32[128,128]{1,0:T(8,128)}, f32[128,128]{1,0:T(8,128)S(1)}, u32[]{:S(2)}, u32[]{:S(2)}) collective-permute-start(f32[128,128]{1,0:T(8,128)} %get-tuple-element.29), channel_id=1, source_target_pairs={{1,0},{2,1},{3,2},{4,3},{5,4},{6,5},{7,6},{0,7},{9,8},{10,9},{11,1... | collective-permute-start | bytes 196616 | tf_op jit(solution)/shard_map/ppermute | solution.py:752
  24.6 13.0 %copy-start.2 = (f32[768,128]{1,0:T(8,128)S(1)}, f32[768,128]{1,0:T(8,128)}, u32[]{:S(2)}) copy-start(f32[768,128]{1,0:T(8,128)} %get-tuple-element.23.ef) | copy-start | bytes 1179652
  33.7 3.9 %copy-start = (f32[3072,128]{1,0:T(8,128)S(1)}, f32[3072,128]{1,0:T(8,128)}, u32[]{:S(2)}) copy-start(f32[3072,128]{1,0:T(8,128)} %get-tuple-element.22.xf) | copy-start | bytes 4718596
  33.7 3.9 %copy-start.4 = (f32[768,128]{1,0:T(8,128)S(1)}, f32[768,128]{1,0:T(8,128)}, u32[]{:S(2)}) copy-start(f32[768,128]{1,0:T(8,128)} %copy-done.3) | copy-start | bytes 1179652
  33.7 3.9 %copy-start.6 = (s32[40,128]{1,0:T(8,128)S(1)}, s32[40,128]{1,0:T(8,128)}, u32[]{:S(2)}) copy-start(s32[40,128]{1,0:T(8,128)} %get-tuple-element.37.turns) | copy-start | bytes 61444
  33.7 3.9 %copy-start.8 = (f32[2,128]{1,0:T(2,128)S(1)}, f32[2,128]{1,0:T(2,128)}, u32[]{:S(2)}) copy-start(f32[2,128]{1,0:T(2,128)} %get-tuple-element.30.stiff) | copy-start | bytes 3076

commit v4 on v3

--- a/solution.py
+++ b/solution.py
@@ -96,47 +96,46 @@
 def build_tables():
     f32 = lambda a: np.ascontiguousarray(a, dtype=np.float32)
     tables = {}
-    forward = np.zeros((NZ, 128))
+    forward = np.zeros((128, 2 * NZ))
     top_z = np.zeros((3, 128, 2 * NZ))
     for gz in range(SPLIT_Z):
         for kk in range(9):
             column = HZ[:, (8 * gz + kk) % NZ]
-            forward[:, gz * SENT + kk] = column
+            forward[gz * SENT + kk] = np.tile(column, 2)
             top_z[kk // 3, gz * SENT + 9 + kk % 3] = np.tile(column, 2)
     tables["forward"] = f32(forward)
     tables["top_z"] = f32(top_z.reshape(3 * 128, 128))
     lane = np.arange(128)
     lane_s, lane_bx, lane_j = lane // 64, lane // 32 % 2, lane % 32
-    mix = np.zeros((NX * NX, 128))
+    mix = np.zeros((NX // 2, NX, 2, NZ))
     for k in range(NX):
         for x in range(NX):
-            mix[k * NX + x] = HX[k, (x + lane_bx) % NX]
-    tables["mix"] = f32(mix)
+            mix[k // 2, x, k % 2] = HX[k, x]
+    tables["mix"] = f32(mix.reshape(NX * NX // 2, 128))
     top_x = np.zeros((2, 2, 16, 128))
     modes = np.zeros((16, 128))
     waves_x = 2.0 - 2.0 * np.cos(2.0 * np.pi / NX * np.arange(NX))
     waves_z = 2.0 - 2.0 * np.cos(2.0 * np.pi / NZ * np.arange(NZ))
     for row in range(16):
-        s, blk, par = row // 8, row // 2 % 4, row % 2
+        s = row // 8
         for pair in range(2):
-            k = blk * 4 + pair * 2 + par
+            k = row % 8 * 2 + pair
             for odd in range(2):
                 x = 2 * (lane_j % 8) + odd
                 top_x[odd, pair, row] = np.where(lane_s == s, HX[k, (x + lane_bx) % NX], 0.0)
             modes[row, pair * 64 : pair * 64 + 64] = waves_x[k] + waves_z + SHIFT_MASS
     tables["top_x"] = f32(top_x.reshape(64, 128))
     tables["modes"] = f32(modes)
-    back_z = np.zeros((SPLIT_Z, 2, 16, 2, NZ))
+    back_z = np.zeros((SPLIT_Z, 16, 2 * NZ))
     for gz in range(SPLIT_Z):
         for kk in range(9):
-            for pair in range(2):
-                back_z[gz, pair, kk, pair] = HZ[(8 * gz + kk) % NZ]
-    tables["back_z"] = f32(back_z.reshape(SPLIT_Z * 32, 128))
-    back_x = np.zeros((SPLIT_X, 2, 4, 2, 2, 64))
+            back_z[gz, kk] = np.tile(HZ[(8 * gz + kk) % NZ], 2)
+    tables["back_z"] = f32(back_z.reshape(SPLIT_Z * 16, 128))
+    back_x = np.zeros((SPLIT_X, 2, 8, 2, NZ))
     for gx in range(SPLIT_X):
         for bx in range(2):
             for k in range(NX):
-                back_x[gx, bx, k // 4, k // 2 % 2, k % 2] = HX[(gx + bx) % NX, k]
+                back_x[gx, bx, k // 2, k % 2] = HX[(gx + bx) % NX, k]
     tables["back_x"] = f32(back_x.reshape(SPLIT_X * 16, 128))
     pick = np.zeros((32 + 192, 256))
 
@@ -257,8 +256,8 @@
 
 
 def first_kernel(face_in, edge_in, vert_in, fturn_in, eturn_in, stiff_in,
-                 xf_out, ef_out, xp_out, xm_out, zp_out, zm_out, cb_out, turns_out, weights_out,
-                 xf, ef, xp, xm, zp, zm, cb, turns, weights,
+                 xf_out, ef_out, near_out, far_out, zp_out, zm_out, cb_out, turns_out, weights_out,
+                 xf, ef, near, far, zp, zm, cb, turns, weights,
                  face, edge, vert, fturn, sems, out_sems):
     copies = [
         pltpu.make_async_copy(source, target, sems.at[at])
@@ -267,9 +266,9 @@
             (fturn_in, fturn),
             (eturn_in, turns.at[16:40]),
             (stiff_in, weights),
-            (face_in.at[0:1448], face.at[0:1448]),
+            (face_in.at[0:1456], face.at[0:1456]),
             (edge_in, edge),
-            (face_in.at[1448:2904], face.at[1448:2904]),
+            (face_in.at[1456:2904], face.at[1456:2904]),
         ))
     ]
     sent = []
@@ -286,8 +285,8 @@
     for device in range(128):
         cb[device * SENT : device * SENT + SENT, :] = block[0:SENT]
     send(cb, cb_out)
-    for copy in copies[1:]:
-        copy.wait()
+    for at in (1, 2, 3, 5):
+        copies[at].wait()
     for f in range(6):
         turns[2 * f : 2 * f + 2, :] = fturn[f]
     turns[12:16, :] = jnp.zeros((4, 128), jnp.int32)
@@ -296,12 +295,20 @@
     stiff = weights
 
     last = NODES - 1
+    first_core = lax.axis_index("gx") % 2 == 0
+    mirrors, masks = [], []
     for half in range(2):
         turn = turns[every(half, 6, 2), :]
-        swap, flip_a, flip_b = (turn & 4) != 0, (turn & 1) != 0, (turn & 2) != 0
+        masks.append(((turn & 4) != 0, (turn & 1) != 0, (turn & 2) != 0))
+        mirrors.append(turns[every(16 + half, 12, 2), :] != 0)
+    for half in range(2):
         for s in range(2):
+            if half == 0:
+                copies[4 + 2 * s].wait()
+            swap, flip_a, flip_b = masks[half]
             source = s * 6 * 242 + half
-            target = (half * 2 + s) * 6 * 128
+            tile = half * 2 + s
+            target = tile * 6 * 128
             for group in ORBITS:
                 x = {n: face[every(source + 2 * (n[0] * 11 + n[1]), 6, 242), :] for n in group}
                 x = {(a, b): jnp.where(swap, x[b, a], x[a, b]) for a, b in group}
@@ -311,32 +318,32 @@
                     xf[every(target + a * 11 + b, 6, 128), :] = x[a, b]
             for pad in range(121, 128):
                 xf[every(target + pad, 6, 128), :] = jnp.zeros((6, 128), F32)
-        mirror = turns[every(16 + half, 12, 2), :] != 0
-        for s in range(2):
+            send(xf.at[target : target + 768], xf_out.at[target : target + 768])
             source = s * 12 * 22 + half
-            target = (half * 2 + s) * EDGE_ROWS
+            target = tile * EDGE_ROWS
             x = [edge[every(source + 2 * p, 12, 22), :] for p in range(NODES)]
             for p in range(NODES):
-                ef[every(target + p, 12, 16), :] = jnp.where(mirror, x[last - p], x[p])
+                ef[every(target + p, 12, 16), :] = jnp.where(mirrors[half], x[last - p], x[p])
             for pad in range(NODES, 16):
                 ef[every(target + pad, 12, 16), :] = jnp.zeros((12, 128), F32)
-
-    for half in range(2):
-        weight = stiff[half : half + 1, :]
-        for s in range(2):
-            tile = half * 2 + s
+            send(ef.at[target : target + EDGE_ROWS], ef_out.at[target : target + EDGE_ROWS])
             base = tile * SIDE_ROWS
-            for ref, slot, edges in ((xp, 1, SENT_XP), (xm, 0, SENT_XM)):
-                ref[base : base + 128, :] = xf[(tile * 6 + slot) * 128 : (tile * 6 + slot + 1) * 128, :]
-                ref[base + 127 : base + 128, :] = weight
-                for place, e in enumerate(edges):
-                    ref[base + 128 + place * 16 : base + 144 + place * 16, :] = ef[
-                        (tile * 12 + e) * 16 : (tile * 12 + e + 1) * 16, :
-                    ]
-    send(xp, xp_out)
-    send(xm, xm_out)
-    send(ef, ef_out)
-    send(xf, xf_out)
+            up = xf[(tile * 6 + 1) * 128 : (tile * 6 + 2) * 128, :]
+            down = xf[tile * 6 * 128 : (tile * 6 + 1) * 128, :]
+            near[base : base + 128, :] = jnp.where(first_core, up, down)
+            far[base : base + 128, :] = jnp.where(first_core, down, up)
+            for ref in (near, far):
+                ref[base + 127 : base + 128, :] = stiff[half : half + 1, :]
+            for place in range(4):
+                up_at = (tile * 12 + SENT_XP[place]) * 16
+                down_at = (tile * 12 + SENT_XM[place]) * 16
+                up, down = ef[up_at : up_at + 16, :], ef[down_at : down_at + 16, :]
+                at = base + 128 + place * 16
+                near[at : at + 16, :] = jnp.where(first_core, up, down)
+                far[at : at + 16, :] = jnp.where(first_core, down, up)
+            for ref, out in ((near, near_out), (far, far_out)):
+                send(ref.at[base : base + SIDE_ROWS], out.at[base : base + SIDE_ROWS])
+
     for ref, half, slot, edges in ((zp, 1, 3, SENT_ZP), (zm, 0, 2, SENT_ZM)):
         own = 96 if half else 0
         group = lanes_of((128, 128)) // 32
@@ -360,7 +367,17 @@
         copy.wait()
 
 
-def corner_kernel(zp, zm, rxm, rxp, out_p, out_m):
+class Side:
+    def __init__(self, first, second):
+        self.first, self.second = first, second
+        self.core = lax.axis_index("gx") % 2 == 0
+
+    def __getitem__(self, at):
+        return jnp.where(self.core, self.first[at], self.second[at])
+
+
+def corner_kernel(zp, zm, near, far, out_p, out_m):
+    rxm, rxp = Side(far, near), Side(near, far)
     lane, row = lanes_of((128, 128)), rows_of((128, 128))
     group = lane // 32
     for ref, out, half, place in ((zp, out_p, 1, 3), (zm, out_m, 0, 2)):
@@ -424,7 +441,6 @@
         nodes = jnp.where(row == p, diag[0:1, p : p + 1], nodes)
     rdiag[...] = 1.0 / nodes
 
-    wave = modes
     tall = [jnp.broadcast_to(heights[0:1, l : l + 1], (16, 128)) for l in range(LAYERS)]
     inverse = [1.0 / h for h in tall]
     prime = None
@@ -435,7 +451,7 @@
             stiff, mass = inverse[l - 1], 0.5 * tall[l - 1]
         else:
             stiff, mass = inverse[l - 1] + inverse[l], 0.5 * (tall[l - 1] + tall[l])
-        pivot = stiff + wave * mass
+        pivot = stiff + modes * mass
         if l:
             pivot = pivot - inverse[l - 1] * prime
         rp = 1.0 / pivot
@@ -449,12 +465,30 @@
             table[BACK + l * 16 : BACK + l * 16 + 16, :] = prime
 
 
-def solve_kernel(g, table, v_out, v_hbm, vb_out, tz, px, zs, vs, ss, cs, sem):
+def thirds(value):
+    high = value.astype(BF16)
+    rest = value - high.astype(F32)
+    middle = rest.astype(BF16)
+    return high, middle, (rest - middle.astype(F32)).astype(BF16)
+
+
+def solve_kernel(g, table, v_out, v_hbm, vb_out, tz, zs, vs, ss, cs, sem):
     def dot(x, y):
         return jnp.dot(x, y, precision=HIGHEST, preferred_element_type=F32)
 
-    stations = [g[x * STATION : x * STATION + STATION, :] for x in range(NX)]
-    tz[...] = dot(table[PLACE["forward"], 0:STATION], jnp.concatenate(stations, axis=1))
+    pad = jnp.zeros((128 - STATION, 128), F32)
+    stations = []
+    for x in range(NX):
+        station = g[x * STATION : x * STATION + STATION, :]
+        stations.append(jnp.concatenate([station, pad], axis=0).T)
+    high, middle, low = thirds(jnp.concatenate(stations, axis=0))
+    wave = thirds(table[PLACE["forward"], :])
+    both = jnp.concatenate(wave[0:2], axis=1)
+    main = jnp.dot(jnp.concatenate([high, middle], axis=1), jnp.concatenate([both, both], axis=0),
+                   preferred_element_type=F32)
+    more = jnp.dot(jnp.concatenate([high, low], axis=1),
+                   jnp.concatenate([wave[2], wave[0]], axis=0), preferred_element_type=F32)
+    tz[...] = main[:, 0:128] + (main[:, 128:256] + more)
     third = rows_of((128, 128)) % 32 // 8
     base_z, base_x = PLACE["top_z"].start, PLACE["top_x"].start
     tops = None
@@ -462,7 +496,6 @@
         total = stations[odd]
         for x in range(odd + 2, NX, 2):
             total = total + stations[x]
-        total = jnp.concatenate([total, jnp.zeros((128 - STATION, 128), F32)], axis=0).T
         parts = [dot(total, table[base_z + 128 * q : base_z + 128 * q + 128, :]) for q in range(3)]
         part = jnp.where(third == 0, parts[0], jnp.where(third == 1, parts[1], parts[2]))
         part = dot(table[base_x + 32 * odd : base_x + 32 * odd + 32, :], part)
@@ -470,25 +503,20 @@
     mix = PLACE["mix"].start
     top = jnp.where(lanes_of((16, 128)) < 64, tops[0:16], tops[16:32])
 
-    bx0 = lanes_of((16, 128)) // 32 % 2 == 0
-    for m in range(4):
-        t = [tz[m * 16 : m * 16 + 16, x * 128 : x * 128 + 128] for x in range(NX)]
-        for kp in range(8):
-            pair = []
-            for par in range(2):
-                k = kp * 2 + par
-                acc = t[0] * table[mix + k * NX : mix + k * NX + 1, :]
+    for s in range(2):
+        for j in (0, 16):
+            at = s * 64 + j
+            parts = []
+            for x in range(NX):
+                near, far = x * 128 + at, (x + NX - 1) % NX * 128 + at + 32
+                parts.append(tz[near : near + 16, :] + tz[far : far + 16, :])
+            for pair in range(NX // 2):
+                row = mix + pair * NX
+                acc = parts[0] * table[row : row + 1, :]
                 for x in range(1, NX):
-                    acc = acc + t[x] * table[mix + k * NX + x : mix + k * NX + x + 1, :]
-                pair.append(acc)
-            even, odd = pair
-            px[kp * 64 + m * 16 : kp * 64 + m * 16 + 16, :] = jnp.where(
-                bx0, even + roll(even, 96), odd + roll(odd, 32)
-            )
-    for blk in range(4):
-        turned = px[blk * 128 : blk * 128 + 128, :].T
-        zs[blk * 64 : blk * 64 + 64, :] = turned[0:64]
-        zs[256 + blk * 64 : 320 + blk * 64, :] = turned[64:128]
+                    acc = acc + parts[x] * table[row + x : row + x + 1, :]
+                to = (s * 8 + pair) * 32 + j
+                zs[to : to + 16, :] = acc
 
     value = None
     for l in range(LEVELS):
@@ -497,31 +525,36 @@
         step = rhs * table[PIVOTS + at : PIVOTS + at + 16, :]
         value = step if l == 0 else step + table[CARRY + at : CARRY + at + 16, :] * value
         vs[at : at + 16, :] = value
-    ss[...] = jnp.zeros((1024, 128), F32)
     for l in range(LEVELS - 1, -1, -1):
         if l < LEVELS - 1:
             at = l * 16
             value = vs[at : at + 16, :] + table[BACK + at : BACK + at + 16, :] * value
         ss[every(l, 16, 64), :] = value
-
-    at = PLACE["back_z"].start + lax.axis_index("gz") * 32
-    hz = table[pl.ds(pl.multiple_of(at, 16), 32), :]
-    q = lax.dot_general(hz, ss[...], (((1,), (1,)), ((), ())), precision=HIGHEST,
-                        preferred_element_type=F32)
+    for l in range(LEVELS, 40):
+        ss[every(l, 16, 64), :] = jnp.zeros((16, 128), F32)
+
     at = PLACE["back_x"].start + lax.axis_index("gx") * 16
     hx = table[pl.ds(pl.multiple_of(at, 16), 16), :]
+    columns = []
+    for s in range(2):
+        for bx in range(2):
+            acc = None
+            for t in range(8):
+                r = bx * 8 + t
+                term = ss[(s * 8 + t) * 64 : (s * 8 + t) * 64 + 40, :] * hx[r : r + 1, :]
+                acc = term if acc is None else acc + term
+            columns += [acc, jnp.zeros((24, 128), F32)]
+    at = PLACE["back_z"].start + lax.axis_index("gz") * 16
+    hz = table[pl.ds(pl.multiple_of(at, 16), 16), :]
+    q = lax.dot_general(hz, jnp.concatenate(columns, axis=0), (((1,), (1,)), ((), ())),
+                        precision=HIGHEST, preferred_element_type=F32)
     lane, row = lanes_of((16, 128)), rows_of((16, 128))
     group = lane // 32
     for s in range(2):
+        near = q[:, s * 128 : s * 128 + 128]
+        far = roll(near, 64)
         for bx in range(2):
-            acc = None
-            for blk in range(4):
-                for pair in range(2):
-                    r = (bx * 4 + blk) * 2 + pair
-                    term = q[pair * 16 : pair * 16 + 16, (s * 4 + blk) * 128 : (s * 4 + blk + 1) * 128]
-                    term = term * hx[r : r + 1, :]
-                    acc = term if acc is None else acc + term
-            acc = acc + roll(acc, 64)
+            acc = jnp.where((lane < 64) == (bx == 0), near, far)
             for by in range(2):
                 plain = roll(acc, 127) if by else acc
                 moved = roll(plain, 32)
@@ -530,7 +563,14 @@
                     base = (((s * 2 + bx) * 2 + by) * 2 + bz) * 16
                     keep = (row - bz + 4) % 4 == group
                     cs[base : base + 16, :] = jnp.where(keep, mixed, 0.0)
-    picked = dot(table[PLACE["pick_0"], :], cs[0:128, :]) + dot(table[PLACE["pick_1"], :], cs[128:256, :])
+    pick = jnp.concatenate(
+        [table[PLACE["pick_0"], :].astype(BF16), table[PLACE["pick_1"], :].astype(BF16)], axis=1)
+    rest, picked = cs[...], None
+    for _ in range(3):
+        part = rest.astype(BF16)
+        rest = rest - part.astype(F32)
+        chosen = jnp.dot(pick, part, preferred_element_type=F32)
+        picked = chosen if picked is None else picked + chosen
     v_out[...] = picked[0:32]
     copy = pltpu.make_async_copy(v_out, v_hbm, sem)
     copy.start()
@@ -538,9 +578,10 @@
     copy.wait()
 
 
-def final_kernel(xf, ef, rxm, rxp, rzm, rzp, stiff, v, vb, lift, rdiag, turns,
+def final_kernel(xf, ef, near, far, rzm, rzp, stiff, v, vb, lift, rdiag, turns,
                  face_hbm, edge_hbm, oq, ev, face_out, edge_out, sems):
     last = NODES - 1
+    rxm, rxp = Side(far, near), Side(near, far)
     w = [stiff[half : half + 1, :] for half in range(2)]
 
     def tile(half, s, f):
@@ -728,16 +769,18 @@
     kept = [(tiles, 128), (4 * EDGE_ROWS, 128), (4 * SIDE_ROWS, 128), (4 * SIDE_ROWS, 128),
             (128, 128), (128, 128), (128 * SENT, 128), (40, 128), (2, 128)]
     kinds = [F32] * 7 + [jnp.int32, F32]
-    xf, ef, xp, xm, zp, zm, cb, turns, weights = call(
+    xf, ef, near, far, zp, zm, cb, turns, weights = call(
         first_kernel, "frame", (face, edge, vert, fturn, eturn, stiff), [HBM] * 6,
         [jax.ShapeDtypeStruct(o, kind) for o, kind in zip(kept, kinds)], [HBM] * 9,
         [pltpu.VMEM(o, kind) for o, kind in zip(kept, kinds)]
         + [(2904, 128), (528, 128), (32, 128), pltpu.VMEM((6, 2, 128), jnp.int32)],
-        ((7,), (9,)), limit=VMEM_WHOLE)
+        ((7,), (21,)), limit=VMEM_WHOLE)
     up = lambda n: [(i, (i + 1) % n) for i in range(n)]
     down = lambda n: [((i + 1) % n, i) for i in range(n)]
-    rxm = lax.ppermute(xp, "gx", up(SPLIT_X))
-    rxp = lax.ppermute(xm, "gx", down(SPLIT_X))
+    swapped = lambda first: [p for i in range(first, first + SPLIT_X, 2)
+                             for p in ((i, (i + 1) % SPLIT_X), ((i + 1) % SPLIT_X, i))]
+    near = lax.ppermute(near, "gx", swapped(0))
+    far = lax.ppermute(far, "gx", swapped(1))
     table, lift, rdiag = call(
         parameter_kernel, "parameters",
         (jnp.asarray(TABLE), element_heights.reshape(1, LAYERS), edge_diag.reshape(1, NODES),
@@ -746,18 +789,18 @@
         ((1, LAYERS), (1, NODES), (NODES, NODES), (1, NODES), (48, FACE_NODES), (256, 128)), ((6,),))
     g = lax.all_to_all(cb.reshape(128, 3, 4, 128), ("gx", "gz"), 0, 0)
     g = g.reshape(128 * SENT, 128)
-    zp, zm = call(corner_kernel, "corners", (zp, zm, rxm, rxp), [VMEM] * 4,
+    zp, zm = call(corner_kernel, "corners", (zp, zm, near, far), [VMEM] * 4,
                   [(128, 128), (128, 128)], [VMEM] * 2, flops=CORNER_FLOPS)
     rzm = lax.ppermute(zp, "gz", up(SPLIT_Z))
     rzp = lax.ppermute(zm, "gz", down(SPLIT_Z))
     v, v_out, vb = call(
         solve_kernel, "coarse", (g, table), [VMEM] * 2, [(32, 128), (32, 128), (192, 128)],
         [VMEM, HBM, VMEM],
-        ((64, 2048), (512, 128), (512, 128), (LEVELS * 16, 128), (1024, 128), (256, 128)), ((),),
+        ((2048, 128), (512, 128), (LEVELS * 16, 128), (1024, 128), (256, 128)), ((),),
         flops=200_000_000)
     face_out, edge_out = call(
         final_kernel, "finish",
-        (xf, ef, rxm, rxp, rzm, rzp, weights, v, vb, lift, rdiag, turns), [VMEM] * 12,
+        (xf, ef, near, far, rzm, rzp, weights, v, vb, lift, rdiag, turns), [VMEM] * 12,
         [(2904, 128), (528, 128)], [HBM] * 2,
         ((tiles, 128), (4 * EDGE_ROWS, 128), (2904, 128), (528, 128)), ((4,),))
     return (face_out.reshape(face_residual.shape), edge_out.reshape(edge_residual.shape),

time: 41 us -> 39.2 us (0.956)
  Pallas kernels: 13.5 us -> 12.3 us
  starting transfers between devices: 18.6 us -> 18 us
    pallas_call x5, Pallas kernels: 13.5 us -> 12.3 us  [call(): pl.pallas_call(kernel, out_shape=shapes, in_specs=ins, out_specs=out_spec...]
    all_to_all x1, starting transfers between devices: 9.03 us -> 8.31 us  [per_device(): g = lax.all_to_all(cb.reshape(128, 3, 4, 128), ('gx', 'gz'), 0, 0)]
  transfers between devices with their start and end apart: 5 -> 5, of which waited for: 1 -> 1; matrix products, arithmetic and copies ran while one was open for 0% -> 0% of each run, Pallas kernels for 15% -> 14%
where the time goes in v4:
time: 39.2 us; the launch traced here: 39 us
  starting transfers between devices  18 us (46%)
  Pallas kernels  12.3 us (31%)
  waiting for transfers between devices  7.81 us (20%)
  between operations  0.88 us (2%)
    pallas_call x5, Pallas kernels, call(): pl.pallas_call(kernel, out_shape=shapes, in_specs=ins, out_specs=out_spec...  12.3 us
    all_to_all x1, starting transfers between devices, per_device(): g = lax.all_to_all(cb.reshape(128, 3, 4, 128), ('gx', 'gz'), 0, 0)  8.31 us
    all_to_all x1, waiting for transfers between devices, per_device(): g = lax.all_to_all(cb.reshape(128, 3, 4, 128), ('gx', 'gz'), 0, 0)  7.8 us
    ppermute x1, starting transfers between devices, per_device(): far = lax.ppermute(far, 'gx', swapped(1))  3.96 us
    ppermute x1, starting transfers between devices, per_device(): rzp = lax.ppermute(zm, 'gz', down(SPLIT_Z))  3.17 us
    ppermute x1, starting transfers between devices, per_device(): rzm = lax.ppermute(zp, 'gz', up(SPLIT_Z))  2.47 us
  transfers between devices with their start and end apart: 5, of which 1 were waited for; matrix products, arithmetic and copies ran while one was open for 0% of the time, Pallas kernels for 14%

profile of v4, /device:TPU:0, one launch (start us, length us, event | category | flops | bytes accessed | tf_op | source)
XLA Modules:
  0.0 39.0 jit_solution(12963132964469126929)
XLA Ops:
  0.6 3.7 %frame.1 = (f32[3072,128]{1,0:T(8,128)}, f32[768,128]{1,0:T(8,128)}, f32[768,128]{1,0:T(8,128)}, f32[768,128]{1,0:T(8,128)}, f32[128,128]{1,0:T(8,128)}, /*index...) custom-call(f32[2904,128]{1,0:T(8,128)} %bitcast.20, f32[528,128]{1,0:T(8,128)} %bitcast.22, ...), custom_call_target="tpu_custom_call" | custom-call | bytes 1793024 | tf_op jit(solution)/shard_map/frame/pallas_call | solution.py:748
  4.3 0.0 copy-start.12
  4.3 0.0 copy-start.13
  4.3 0.1 collective-permute-start
  4.4 4.0 %collective-permute-start.1 = (f32[768,128]{1,0:T(8,128)}, f32[768,128]{1,0:T(8,128)S(1)}, u32[]{:S(2)}, u32[]{:S(2)}) collective-permute-start(f32[768,128]{1,0:T(8,128)} %get-tuple-element.25), channel_id=1, source_target_pairs={{8,16},{16,8},{24,32},{32,24},{40,48},{48,40},{56,64},{64,56},{72,... | collective-permute-start | bytes 1179656 | tf_op jit(solution)/shard_map/ppermute | solution.py:783
  8.4 8.3 %all-to-all-start = ((f32[128,3,4,128]{3,2,1,0:T(4,128)}), f32[128,3,4,128]{3,2,1,0:T(4,128)S(1)}, u32[]{:S(2)}, u32[]{:S(2)}) async-start(f32[128,3,4,128]{3,2,1,0:T(4,128)} %bitcast.21), calls=%async_computation | async-start | bytes 1572864 | tf_op jit(solution)/shard_map/all_to_all | solution.py:790
  16.7 0.0 collective-permute-done.near
  16.7 0.0 collective-permute-done.1.far
  16.8 0.0 copy-start.1
  16.8 0.0 copy-start.5
  16.8 0.0 copy-start.7
  16.8 0.0 copy-start.9
  16.8 0.0 copy-start.10
  16.8 0.0 copy-start.11
  16.8 0.7 %corners.1 = (f32[128,128]{1,0:T(8,128)}, f32[128,128]{1,0:T(8,128)S(1)}) custom-call(f32[128,128]{1,0:T(8,128)S(1)} %copy-done.12, f32[128,128]{1,0:T(8,128)S(1)} %copy-done.13, f32[768,128]{1,0:T(8,128)S(1)} %collective-permute-done.near, f32[768,128]{1,0:T(8,128)S(1)} %collective-permute-done.1.far), custom_call_target="tpu_custom_call" | custom-call | flops 99999997952 | bytes 917504 | tf_op jit(solution)/shard_map/corners/pallas_call | solution.py:748
  17.6 2.5 %collective-permute-start.2 = (f32[128,128]{1,0:T(8,128)}, f32[128,128]{1,0:T(8,128)S(1)}, u32[]{:S(2)}, u32[]{:S(2)}) collective-permute-start(f32[128,128]{1,0:T(8,128)} %get-tuple-element.28), channel_id=1, source_target_pairs={{0,1},{1,2},{2,3},{3,4},{4,5},{5,6},{6,7},{7,0},{8,9},{9,10},{10,1... | collective-permute-start | bytes 196616 | tf_op jit(solution)/shard_map/ppermute | solution.py:794
  20.0 3.2 %collective-permute-start.3 = (f32[128,128]{1,0:T(8,128)S(1)}, f32[128,128]{1,0:T(8,128)S(1)}, u32[]{:S(2)}, u32[]{:S(2)}) collective-permute-start(f32[128,128]{1,0:T(8,128)S(1)} %get-tuple-element.29), channel_id=1, source_target_pairs={{1,0},{2,1},{3,2},{4,3},{5,4},{6,5},{7,6},{0,7},{9,8},{10,9},{11,1... | collective-permute-start | bytes 196616 | tf_op jit(solution)/shard_map/ppermute | solution.py:795
  23.2 0.0 copy-done.5
  23.3 1.3 %parameters.1 = (f32[3152,128]{1,0:T(8,128)S(1)}, bf16[256,256]{1,0:T(8,128)(2,1)S(1)}, f32[16,128]{1,0:T(8,128)S(1)}) custom-call(f32[1584,128]{1,0:T(8,128)S(1)} %copy-done.1, f32[1,32]{1,0:T(1,128)S(1)} %bitcast.17, f32[1,11]{1,0:T(1,128)S(1)} %bitcast.18, f32[11,11]{1,0:T(8,128)S(1)} %copy-done.7, f32[1,11]{1,0:T(1,128)S(1)} %bitcast.19, ...), custom_call_target="tpu_custom_call" | custom-call | bytes 834940 | tf_op jit(solution)/shard_map/parameters/pallas_call | solution.py:748
  24.6 7.8 %all-to-all-done = f32[128,3,4,128]{3,2,1,0:T(4,128)S(1)} async-done(((f32[128,3,4,128]{3,2,1,0:T(4,128)}), f32[128,3,4,128]{3,2,1,0:T(4,128)S(1)}, u32[]{:S(2)}, u32[]{:S(2)}) %all-to-all-start) | async-done | bytes 786464 | tf_op jit(solution)/shard_map/all_to_all | solution.py:790
  32.4 3.5 %coarse.1 = (f32[32,128]{1,0:T(8,128)S(1)}, f32[32,128]{1,0:T(8,128)}, f32[192,128]{1,0:T(8,128)S(1)}) custom-call(f32[1536,128]{1,0:T(8,128)S(1)} %bitcast.15, f32[3152,128]{1,0:T(8,128)S(1)} %get-tuple-element.32.table), custom_call_target="tpu_custom_call" | custom-call | flops 200000000 | bytes 2400256 | tf_op jit(solution)/shard_map/coarse/pallas_call | solution.py:748
  35.8 0.0 collective-permute-done.2.rzm
  35.9 0.0 collective-permute-done.3.rzp
  35.9 3.1 %finish.1 = (f32[2904,128]{1,0:T(8,128)}, f32[528,128]{1,0:T(8,128)}) custom-call(f32[3072,128]{1,0:T(8,128)S(1)} %copy-done, f32[768,128]{1,0:T(8,128)S(1)} %copy-done.2, f32[768,128]{1,0:T(8,128)S(1)} %collective-permute-done.near, f32[768,128]{1,0:T(8,128)S(1)} %copy-done.4, f32[128,128]{1,0:T(8,128)S(1)} %collective-permute-done.2.rzm, ...), custom_call_target="tpu_custom_call" | custom-call | bytes 3290112 | tf_op jit(solution)/shard_map/finish/pallas_call | solution.py:748
  (19 shorter events, 0.0 us)
Async XLA Ops:
  4.3 12.4 %copy-start.12 = (f32[128,128]{1,0:T(8,128)S(1)}, f32[128,128]{1,0:T(8,128)}, u32[]{:S(2)}) copy-start(f32[128,128]{1,0:T(8,128)} %get-tuple-element.26.zp) | copy-start | bytes 196612
  4.3 12.4 %copy-start.13 = (f32[128,128]{1,0:T(8,128)S(1)}, f32[128,128]{1,0:T(8,128)}, u32[]{:S(2)}) copy-start(f32[128,128]{1,0:T(8,128)} %get-tuple-element.27.zm) | copy-start | bytes 196612
  4.3 12.4 %collective-permute-start = (f32[768,128]{1,0:T(8,128)}, f32[768,128]{1,0:T(8,128)S(1)}, u32[]{:S(2)}, u32[]{:S(2)}) collective-permute-start(f32[768,128]{1,0:T(8,128)} %get-tuple-element.24), channel_id=1, source_target_pairs={{0,8},{8,0},{16,24},{24,16},{32,40},{40,32},{48,56},{56,48},{64,72... | collective-permute-start | bytes 1179656 | tf_op jit(solution)/shard_map/ppermute | solution.py:782
  4.4 12.3 %collective-permute-start.1 = (f32[768,128]{1,0:T(8,128)}, f32[768,128]{1,0:T(8,128)S(1)}, u32[]{:S(2)}, u32[]{:S(2)}) collective-permute-start(f32[768,128]{1,0:T(8,128)} %get-tuple-element.25), channel_id=1, source_target_pairs={{8,16},{16,8},{24,32},{32,24},{40,48},{48,40},{56,64},{64,56},{72,... | collective-permute-start | bytes 1179656 | tf_op jit(solution)/shard_map/ppermute | solution.py:783
  8.4 24.0 %all-to-all-start = ((f32[128,3,4,128]{3,2,1,0:T(4,128)}), f32[128,3,4,128]{3,2,1,0:T(4,128)S(1)}, u32[]{:S(2)}, u32[]{:S(2)}) async-start(f32[128,3,4,128]{3,2,1,0:T(4,128)} %bitcast.21), calls=%async_computation | async-start | bytes 1572864 | tf_op jit(solution)/shard_map/all_to_all | solution.py:790
  16.7 0.8 %copy-start.3 = (f32[768,128]{1,0:T(8,128)}, f32[768,128]{1,0:T(8,128)S(1)}, u32[]{:S(2)}) copy-start(f32[768,128]{1,0:T(8,128)S(1)} %collective-permute-done.1.far) | copy-start | bytes 1179652
  16.8 6.4 %copy-start.1 = (f32[1584,128]{1,0:T(8,128)S(1)}, f32[1584,128]{1,0:T(8,128)}, u32[]{:S(2)}) copy-start(f32[1584,128]{1,0:T(8,128)} %constant.2.clone.table_in) | copy-start | bytes 2433028
  16.8 6.4 %copy-start.5 = (f32[121,48]{0,1:T(8,128)S(1)}, f32[121,48]{0,1:T(8,128)}, u32[]{:S(2)}) copy-start(f32[121,48]{0,1:T(8,128)} %param.20) | copy-start | bytes 69700
  16.8 6.4 %copy-start.7 = (f32[11,11]{1,0:T(8,128)S(1)}, f32[11,11]{1,0:T(8,128)}, u32[]{:S(2)}) copy-start(f32[11,11]{1,0:T(8,128)} %basis_in.1) | copy-start | bytes 1456
  16.8 6.4 %copy-start.9 = (f32[32]{0:T(128)S(1)}, f32[32]{0:T(128)}, u32[]{:S(2)}) copy-start(f32[32]{0:T(128)} %param.22) | copy-start | bytes 388
  16.8 6.4 %copy-start.10 = (f32[11]{0:T(128)S(1)}, f32[11]{0:T(128)}, u32[]{:S(2)}) copy-start(f32[11]{0:T(128)} %param.21) | copy-start | bytes 136
  16.8 6.4 %copy-start.11 = (f32[11]{0:T(128)S(1)}, f32[11]{0:T(128)}, u32[]{:S(2)}) copy-start(f32[11]{0:T(128)} %param.19) | copy-start | bytes 136
  17.6 18.3 %collective-permute-start.2 = (f32[128,128]{1,0:T(8,128)}, f32[128,128]{1,0:T(8,128)S(1)}, u32[]{:S(2)}, u32[]{:S(2)}) collective-permute-start(f32[128,128]{1,0:T(8,128)} %get-tuple-element.28), channel_id=1, source_target_pairs={{0,1},{1,2},{2,3},{3,4},{4,5},{5,6},{6,7},{7,0},{8,9},{9,10},{10,1... | collective-permute-start | bytes 196616 | tf_op jit(solution)/shard_map/ppermute | solution.py:794
  20.0 15.8 %collective-permute-start.3 = (f32[128,128]{1,0:T(8,128)S(1)}, f32[128,128]{1,0:T(8,128)S(1)}, u32[]{:S(2)}, u32[]{:S(2)}) collective-permute-start(f32[128,128]{1,0:T(8,128)S(1)} %get-tuple-element.29), channel_id=1, source_target_pairs={{1,0},{2,1},{3,2},{4,3},{5,4},{6,5},{7,6},{0,7},{9,8},{10,9},{11,1... | collective-permute-start | bytes 196616 | tf_op jit(solution)/shard_map/ppermute | solution.py:795
  23.2 12.6 %copy-start.2 = (f32[768,128]{1,0:T(8,128)S(1)}, f32[768,128]{1,0:T(8,128)}, u32[]{:S(2)}) copy-start(f32[768,128]{1,0:T(8,128)} %get-tuple-element.23.ef) | copy-start | bytes 1179652
  23.2 12.6 %copy-start.6 = (s32[40,128]{1,0:T(8,128)S(1)}, s32[40,128]{1,0:T(8,128)}, u32[]{:S(2)}) copy-start(s32[40,128]{1,0:T(8,128)} %get-tuple-element.37.turns) | copy-start | bytes 61444
  23.2 12.6 %copy-start.8 = (f32[2,128]{1,0:T(2,128)S(1)}, f32[2,128]{1,0:T(2,128)}, u32[]{:S(2)}) copy-start(f32[2,128]{1,0:T(2,128)} %get-tuple-element.30.stiff) | copy-start | bytes 3076
  32.4 3.5 %copy-start = (f32[3072,128]{1,0:T(8,128)S(1)}, f32[3072,128]{1,0:T(8,128)}, u32[]{:S(2)}) copy-start(f32[3072,128]{1,0:T(8,128)} %get-tuple-element.22.xf) | copy-start | bytes 4718596
  32.4 3.5 %copy-start.4 = (f32[768,128]{1,0:T(8,128)S(1)}, f32[768,128]{1,0:T(8,128)}, u32[]{:S(2)}) copy-start(f32[768,128]{1,0:T(8,128)} %copy-done.3) | copy-start | bytes 1179652

commit v5 on v4

--- a/solution.py
+++ b/solution.py
@@ -472,7 +472,7 @@
     return high, middle, (rest - middle.astype(F32)).astype(BF16)
 
 
-def solve_kernel(g, table, v_out, v_hbm, vb_out, tz, zs, vs, ss, cs, sem):
+def solve_kernel(g, table, v_out, vb_out, tz, zs, vs, ss, cs):
     def dot(x, y):
         return jnp.dot(x, y, precision=HIGHEST, preferred_element_type=F32)
 
@@ -572,15 +572,14 @@
         chosen = jnp.dot(pick, part, preferred_element_type=F32)
         picked = chosen if picked is None else picked + chosen
     v_out[...] = picked[0:32]
-    copy = pltpu.make_async_copy(v_out, v_hbm, sem)
-    copy.start()
     vb_out[...] = picked[32:224]
-    copy.wait()
 
 
 def final_kernel(xf, ef, near, far, rzm, rzp, stiff, v, vb, lift, rdiag, turns,
-                 face_hbm, edge_hbm, oq, ev, face_out, edge_out, sems):
+                 face_hbm, edge_hbm, v_hbm, oq, ev, face_out, edge_out, sems):
     last = NODES - 1
+    vertex_copy = pltpu.make_async_copy(v, v_hbm, sems.at[4])
+    vertex_copy.start()
     rxm, rxp = Side(far, near), Side(near, far)
     w = [stiff[half : half + 1, :] for half in range(2)]
 
@@ -733,6 +732,7 @@
             copy.start()
     for copy in copies:
         copy.wait()
+    vertex_copy.wait()
 
 
 VMEM = pl.BlockSpec(memory_space=pltpu.VMEM)
@@ -793,16 +793,16 @@
                   [(128, 128), (128, 128)], [VMEM] * 2, flops=CORNER_FLOPS)
     rzm = lax.ppermute(zp, "gz", up(SPLIT_Z))
     rzp = lax.ppermute(zm, "gz", down(SPLIT_Z))
-    v, v_out, vb = call(
-        solve_kernel, "coarse", (g, table), [VMEM] * 2, [(32, 128), (32, 128), (192, 128)],
-        [VMEM, HBM, VMEM],
-        ((2048, 128), (512, 128), (LEVELS * 16, 128), (1024, 128), (256, 128)), ((),),
+    v, vb = call(
+        solve_kernel, "coarse", (g, table), [VMEM] * 2, [(32, 128), (192, 128)],
+        [VMEM, VMEM],
+        ((2048, 128), (512, 128), (LEVELS * 16, 128), (1024, 128), (256, 128)),
         flops=200_000_000)
-    face_out, edge_out = call(
+    face_out, edge_out, v_out = call(
         final_kernel, "finish",
         (xf, ef, near, far, rzm, rzp, weights, v, vb, lift, rdiag, turns), [VMEM] * 12,
-        [(2904, 128), (528, 128)], [HBM] * 2,
-        ((tiles, 128), (4 * EDGE_ROWS, 128), (2904, 128), (528, 128)), ((4,),))
+        [(2904, 128), (528, 128), (32, 128)], [HBM] * 3,
+        ((tiles, 128), (4 * EDGE_ROWS, 128), (2904, 128), (528, 128)), ((5,),))
     return (face_out.reshape(face_residual.shape), edge_out.reshape(edge_residual.shape),
             v_out.reshape(vertex_residual.shape))
 

time: 39.2 us -> 38.7 us (0.987)
  Pallas kernels: 12.3 us -> 11.7 us
    pallas_call x5, Pallas kernels: 12.3 us -> 11.7 us  [call(): pl.pallas_call(kernel, out_shape=shapes, in_specs=ins, out_specs=out_spec...]
  transfers between devices with their start and end apart: 5 -> 5, of which waited for: 1 -> 1; matrix products, arithmetic and copies ran while one was open for 0% -> 0% of each run, Pallas kernels for 14% -> 13%
where the time goes in v5:
time: 38.7 us; the launch traced here: 38.4 us
  starting transfers between devices  18 us (47%)
  Pallas kernels  11.7 us (30%)
  waiting for transfers between devices  7.81 us (20%)
  between operations  0.88 us (2%)
    pallas_call x5, Pallas kernels, call(): pl.pallas_call(kernel, out_shape=shapes, in_specs=ins, out_specs=out_spec...  11.7 us
    all_to_all x1, starting transfers between devices, per_device(): g = lax.all_to_all(cb.reshape(128, 3, 4, 128), ('gx', 'gz'), 0, 0)  8.31 us
    all_to_all x1, waiting for transfers between devices, per_device(): g = lax.all_to_all(cb.reshape(128, 3, 4, 128), ('gx', 'gz'), 0, 0)  7.8 us
    ppermute x1, starting transfers between devices, per_device(): far = lax.ppermute(far, 'gx', swapped(1))  3.96 us
    ppermute x1, starting transfers between devices, per_device(): rzp = lax.ppermute(zm, 'gz', down(SPLIT_Z))  3.17 us
    ppermute x1, starting transfers between devices, per_device(): rzm = lax.ppermute(zp, 'gz', up(SPLIT_Z))  2.47 us
  transfers between devices with their start and end apart: 5, of which 1 were waited for; matrix products, arithmetic and copies ran while one was open for 0% of the time, Pallas kernels for 13%

profile of v5, /device:TPU:0, one launch (start us, length us, event | category | flops | bytes accessed | tf_op | source)
XLA Modules:
  0.0 38.4 jit_solution(2417398993189753969)
XLA Ops:
  0.6 3.7 %frame.1 = (f32[3072,128]{1,0:T(8,128)}, f32[768,128]{1,0:T(8,128)}, f32[768,128]{1,0:T(8,128)}, f32[768,128]{1,0:T(8,128)}, f32[128,128]{1,0:T(8,128)}, /*index...) custom-call(f32[2904,128]{1,0:T(8,128)} %bitcast.20, f32[528,128]{1,0:T(8,128)} %bitcast.22, ...), custom_call_target="tpu_custom_call" | custom-call | bytes 1793024 | tf_op jit(solution)/shard_map/frame/pallas_call | solution.py:748
  4.3 0.0 copy-start.12
  4.3 0.0 copy-start.13
  4.3 0.1 collective-permute-start
  4.4 4.0 %collective-permute-start.1 = (f32[768,128]{1,0:T(8,128)}, f32[768,128]{1,0:T(8,128)S(1)}, u32[]{:S(2)}, u32[]{:S(2)}) collective-permute-start(f32[768,128]{1,0:T(8,128)} %get-tuple-element.25), channel_id=1, source_target_pairs={{8,16},{16,8},{24,32},{32,24},{40,48},{48,40},{56,64},{64,56},{72,... | collective-permute-start | bytes 1179656 | tf_op jit(solution)/shard_map/ppermute | solution.py:783
  8.4 8.3 %all-to-all-start = ((f32[128,3,4,128]{3,2,1,0:T(4,128)}), f32[128,3,4,128]{3,2,1,0:T(4,128)S(1)}, u32[]{:S(2)}, u32[]{:S(2)}) async-start(f32[128,3,4,128]{3,2,1,0:T(4,128)} %bitcast.21), calls=%async_computation | async-start | bytes 1572864 | tf_op jit(solution)/shard_map/all_to_all | solution.py:790
  16.7 0.0 collective-permute-done.near
  16.7 0.0 collective-permute-done.1.far
  16.8 0.0 copy-start.1
  16.8 0.0 copy-start.5
  16.8 0.0 copy-start.7
  16.8 0.0 copy-start.9
  16.8 0.0 copy-start.10
  16.8 0.0 copy-start.11
  16.8 0.7 %corners.1 = (f32[128,128]{1,0:T(8,128)}, f32[128,128]{1,0:T(8,128)S(1)}) custom-call(f32[128,128]{1,0:T(8,128)S(1)} %copy-done.12, f32[128,128]{1,0:T(8,128)S(1)} %copy-done.13, f32[768,128]{1,0:T(8,128)S(1)} %collective-permute-done.near, f32[768,128]{1,0:T(8,128)S(1)} %collective-permute-done.1.far), custom_call_target="tpu_custom_call" | custom-call | flops 99999997952 | bytes 917504 | tf_op jit(solution)/shard_map/corners/pallas_call | solution.py:748
  17.6 2.5 %collective-permute-start.2 = (f32[128,128]{1,0:T(8,128)}, f32[128,128]{1,0:T(8,128)S(1)}, u32[]{:S(2)}, u32[]{:S(2)}) collective-permute-start(f32[128,128]{1,0:T(8,128)} %get-tuple-element.28), channel_id=1, source_target_pairs={{0,1},{1,2},{2,3},{3,4},{4,5},{5,6},{6,7},{7,0},{8,9},{9,10},{10,1... | collective-permute-start | bytes 196616 | tf_op jit(solution)/shard_map/ppermute | solution.py:794
  20.0 3.2 %collective-permute-start.3 = (f32[128,128]{1,0:T(8,128)S(1)}, f32[128,128]{1,0:T(8,128)S(1)}, u32[]{:S(2)}, u32[]{:S(2)}) collective-permute-start(f32[128,128]{1,0:T(8,128)S(1)} %get-tuple-element.29), channel_id=1, source_target_pairs={{1,0},{2,1},{3,2},{4,3},{5,4},{6,5},{7,6},{0,7},{9,8},{10,9},{11,1... | collective-permute-start | bytes 196616 | tf_op jit(solution)/shard_map/ppermute | solution.py:795
  23.2 0.0 copy-start.8
  23.3 1.3 %parameters.1 = (f32[3152,128]{1,0:T(8,128)S(1)}, bf16[256,256]{1,0:T(8,128)(2,1)S(1)}, f32[16,128]{1,0:T(8,128)S(1)}) custom-call(f32[1584,128]{1,0:T(8,128)S(1)} %copy-done.1, f32[1,32]{1,0:T(1,128)S(1)} %bitcast.17, f32[1,11]{1,0:T(1,128)S(1)} %bitcast.18, f32[11,11]{1,0:T(8,128)S(1)} %copy-done.7, f32[1,11]{1,0:T(1,128)S(1)} %bitcast.19, ...), custom_call_target="tpu_custom_call" | custom-call | bytes 834940 | tf_op jit(solution)/shard_map/parameters/pallas_call | solution.py:748
  24.6 7.8 %all-to-all-done = f32[128,3,4,128]{3,2,1,0:T(4,128)S(1)} async-done(((f32[128,3,4,128]{3,2,1,0:T(4,128)}), f32[128,3,4,128]{3,2,1,0:T(4,128)S(1)}, u32[]{:S(2)}, u32[]{:S(2)}) %all-to-all-start) | async-done | bytes 786464 | tf_op jit(solution)/shard_map/all_to_all | solution.py:790
  32.4 2.9 %coarse.1 = (f32[32,128]{1,0:T(8,128)S(1)}, f32[192,128]{1,0:T(8,128)S(1)}) custom-call(f32[1536,128]{1,0:T(8,128)S(1)} %bitcast.15, f32[3152,128]{1,0:T(8,128)S(1)} %get-tuple-element.32.table), custom_call_target="tpu_custom_call" | custom-call | flops 200000000 | bytes 2400256 | tf_op jit(solution)/shard_map/coarse/pallas_call | solution.py:748
  35.3 0.0 collective-permute-done.2.rzm
  35.3 0.0 collective-permute-done.3.rzp
  35.3 3.1 %finish.1 = (f32[2904,128]{1,0:T(8,128)}, f32[528,128]{1,0:T(8,128)}, f32[32,128]{1,0:T(8,128)}) custom-call(f32[3072,128]{1,0:T(8,128)S(1)} %copy-done, f32[768,128]{1,0:T(8,128)S(1)} %copy-done.2, f32[768,128]{1,0:T(8,128)S(1)} %collective-permute-done.near, f32[768,128]{1,0:T(8,128)S(1)} %copy-done.4, f32[128,128]{1,0:T(8,128)S(1)} %collective-permute-done.2.rzm, ...), custom_call_target="tpu_custom_call" | custom-call | bytes 3290112 | tf_op jit(solution)/shard_map/finish/pallas_call | solution.py:748
  (19 shorter events, 0.0 us)
Async XLA Ops:
  4.3 12.4 %copy-start.12 = (f32[128,128]{1,0:T(8,128)S(1)}, f32[128,128]{1,0:T(8,128)}, u32[]{:S(2)}) copy-start(f32[128,128]{1,0:T(8,128)} %get-tuple-element.26.zp) | copy-start | bytes 196612
  4.3 12.4 %copy-start.13 = (f32[128,128]{1,0:T(8,128)S(1)}, f32[128,128]{1,0:T(8,128)}, u32[]{:S(2)}) copy-start(f32[128,128]{1,0:T(8,128)} %get-tuple-element.27.zm) | copy-start | bytes 196612
  4.3 12.4 %collective-permute-start = (f32[768,128]{1,0:T(8,128)}, f32[768,128]{1,0:T(8,128)S(1)}, u32[]{:S(2)}, u32[]{:S(2)}) collective-permute-start(f32[768,128]{1,0:T(8,128)} %get-tuple-element.24), channel_id=1, source_target_pairs={{0,8},{8,0},{16,24},{24,16},{32,40},{40,32},{48,56},{56,48},{64,72... | collective-permute-start | bytes 1179656 | tf_op jit(solution)/shard_map/ppermute | solution.py:782
  4.4 12.3 %collective-permute-start.1 = (f32[768,128]{1,0:T(8,128)}, f32[768,128]{1,0:T(8,128)S(1)}, u32[]{:S(2)}, u32[]{:S(2)}) collective-permute-start(f32[768,128]{1,0:T(8,128)} %get-tuple-element.25), channel_id=1, source_target_pairs={{8,16},{16,8},{24,32},{32,24},{40,48},{48,40},{56,64},{64,56},{72,... | collective-permute-start | bytes 1179656 | tf_op jit(solution)/shard_map/ppermute | solution.py:783
  8.4 24.0 %all-to-all-start = ((f32[128,3,4,128]{3,2,1,0:T(4,128)}), f32[128,3,4,128]{3,2,1,0:T(4,128)S(1)}, u32[]{:S(2)}, u32[]{:S(2)}) async-start(f32[128,3,4,128]{3,2,1,0:T(4,128)} %bitcast.21), calls=%async_computation | async-start | bytes 1572864 | tf_op jit(solution)/shard_map/all_to_all | solution.py:790
  16.7 0.8 %copy-start.3 = (f32[768,128]{1,0:T(8,128)}, f32[768,128]{1,0:T(8,128)S(1)}, u32[]{:S(2)}) copy-start(f32[768,128]{1,0:T(8,128)S(1)} %collective-permute-done.1.far) | copy-start | bytes 1179652
  16.8 6.4 %copy-start.1 = (f32[1584,128]{1,0:T(8,128)S(1)}, f32[1584,128]{1,0:T(8,128)}, u32[]{:S(2)}) copy-start(f32[1584,128]{1,0:T(8,128)} %constant.2.clone.table_in) | copy-start | bytes 2433028
  16.8 6.4 %copy-start.5 = (f32[121,48]{0,1:T(8,128)S(1)}, f32[121,48]{0,1:T(8,128)}, u32[]{:S(2)}) copy-start(f32[121,48]{0,1:T(8,128)} %param.20) | copy-start | bytes 69700
  16.8 6.4 %copy-start.7 = (f32[11,11]{1,0:T(8,128)S(1)}, f32[11,11]{1,0:T(8,128)}, u32[]{:S(2)}) copy-start(f32[11,11]{1,0:T(8,128)} %basis_in.1) | copy-start | bytes 1456
  16.8 6.4 %copy-start.9 = (f32[32]{0:T(128)S(1)}, f32[32]{0:T(128)}, u32[]{:S(2)}) copy-start(f32[32]{0:T(128)} %param.22) | copy-start | bytes 388
  16.8 6.4 %copy-start.10 = (f32[11]{0:T(128)S(1)}, f32[11]{0:T(128)}, u32[]{:S(2)}) copy-start(f32[11]{0:T(128)} %param.21) | copy-start | bytes 136
  16.8 6.4 %copy-start.11 = (f32[11]{0:T(128)S(1)}, f32[11]{0:T(128)}, u32[]{:S(2)}) copy-start(f32[11]{0:T(128)} %param.19) | copy-start | bytes 136
  17.6 17.7 %collective-permute-start.2 = (f32[128,128]{1,0:T(8,128)}, f32[128,128]{1,0:T(8,128)S(1)}, u32[]{:S(2)}, u32[]{:S(2)}) collective-permute-start(f32[128,128]{1,0:T(8,128)} %get-tuple-element.28), channel_id=1, source_target_pairs={{0,1},{1,2},{2,3},{3,4},{4,5},{5,6},{6,7},{7,0},{8,9},{9,10},{10,1... | collective-permute-start | bytes 196616 | tf_op jit(solution)/shard_map/ppermute | solution.py:794
  20.0 15.3 %collective-permute-start.3 = (f32[128,128]{1,0:T(8,128)S(1)}, f32[128,128]{1,0:T(8,128)S(1)}, u32[]{:S(2)}, u32[]{:S(2)}) collective-permute-start(f32[128,128]{1,0:T(8,128)S(1)} %get-tuple-element.29), channel_id=1, source_target_pairs={{1,0},{2,1},{3,2},{4,3},{5,4},{6,5},{7,6},{0,7},{9,8},{10,9},{11,1... | collective-permute-start | bytes 196616 | tf_op jit(solution)/shard_map/ppermute | solution.py:795
  23.2 12.1 %copy-start.2 = (f32[768,128]{1,0:T(8,128)S(1)}, f32[768,128]{1,0:T(8,128)}, u32[]{:S(2)}) copy-start(f32[768,128]{1,0:T(8,128)} %get-tuple-element.23.ef) | copy-start | bytes 1179652
  23.2 12.1 %copy-start.6 = (s32[40,128]{1,0:T(8,128)S(1)}, s32[40,128]{1,0:T(8,128)}, u32[]{:S(2)}) copy-start(s32[40,128]{1,0:T(8,128)} %get-tuple-element.37.turns) | copy-start | bytes 61444
  23.2 12.1 %copy-start.8 = (f32[2,128]{1,0:T(2,128)S(1)}, f32[2,128]{1,0:T(2,128)}, u32[]{:S(2)}) copy-start(f32[2,128]{1,0:T(2,128)} %get-tuple-element.30.stiff) | copy-start | bytes 3076
  32.4 3.0 %copy-start = (f32[3072,128]{1,0:T(8,128)S(1)}, f32[3072,128]{1,0:T(8,128)}, u32[]{:S(2)}) copy-start(f32[3072,128]{1,0:T(8,128)} %get-tuple-element.22.xf) | copy-start | bytes 4718596
  32.4 3.0 %copy-start.4 = (f32[768,128]{1,0:T(8,128)S(1)}, f32[768,128]{1,0:T(8,128)}, u32[]{:S(2)}) copy-start(f32[768,128]{1,0:T(8,128)} %copy-done.3) | copy-start | bytes 1179652
